TPU v7x, 32 devices: a whole 2x2x4 slice. The times are simulated.
32 devices in a mesh: groups: 2 (over y), latent: 4 (over z), rows: 4 (over x, core).
Axes of the slice: x: 2, y: 2, z: 4, core: 2. Of those that a mesh axis runs over, the one named last changes fastest.
Arguments:
- activations_in: bfloat16 [2, 128, 2304], P('groups', None, 'latent'), parts along dimension 0, may hold values from -6 to 6
- gate_proj: bfloat16 [2304, 4608], P('rows', 'latent'), may hold values from -0.125 to 0.125
- up_proj: bfloat16 [2304, 4608], P('rows', 'latent'), may hold values from -0.125 to 0.125
- down_proj: bfloat16 [4608, 2304], P('latent', 'rows'), may hold values from -0.09375 to 0.09375
- enc_weight: bfloat16 [4608, 65536], P(('groups', 'rows'), 'latent'), parts along dimension 0, may hold values from -6 to 6
- enc_bias: float32 [131072], P(('groups', 'latent')), parts along dimension 0, may hold values from -0.5 to 0.5
- dec_weight: bfloat16 [131072, 2304], P(('groups', 'latent'), 'rows'), parts along dimension 0, may hold values from -6 to 6
- dec_bias: float32 [4608], P(('groups', 'rows')), parts along dimension 0, may hold values from -0.5 to 0.5
Outputs:
- enc_weight_new: bfloat16 [4608, 65536], P(('groups', 'rows'), 'latent'), parts along dimension 0
- enc_bias_new: float32 [131072], P(('groups', 'latent')), parts along dimension 0
- dec_weight_new: bfloat16 [131072, 2304], P(('groups', 'latent'), 'rows'), parts along dimension 0
- dec_bias_new: float32 [4608], P(('groups', 'rows')), parts along dimension 0
There are 2 independent parts, one for each index of `groups`. A program takes and returns all parts, laid end to end along the dimension named above; an argument that names none is the same for every part. Nothing has to cross between parts.
All inputs are finite; a program needn't handle non-finite values.
Results may differ from a plain program's by a relative error of at most 0.02.
Values may be sent and summed in bfloat16 or wider, within the bound.
No kernel may reach another device: no remote copies, remote signals or barrier semaphores. Data moves between devices by JAX's collectives and lax.ppermute only.
A program may use at most 128 MiB of HBM per device.

v0:
```python
import jax
import jax.numpy as jnp
from jax import lax
from jax.sharding import PartitionSpec as P

MODEL_WIDTH = 2304
LATENTS = 65536


sparsity_cost = 0.1
sharpness = 8.0
weight_rate = 2.0
enc_bias_rate = 0.01
dec_bias_rate = 0.002


def row_total(term):
    return lax.psum(term.astype(jnp.bfloat16), "rows").astype(jnp.float32)


def body(activations_in, gate_proj, up_proj, down_proj, enc_weight, enc_bias, dec_weight, dec_bias):
    gate_full, up_full = (
        lax.all_gather(gate_proj, "rows", axis=0, tiled=True),
        lax.all_gather(up_proj, "rows", axis=0, tiled=True),
    )
    batches = activations_in.shape[0]
    batch_tokens = activations_in.shape[1]
    all_tokens = batches * batch_tokens
    token_rows = activations_in.reshape(all_tokens, activations_in.shape[2])
    portion = lax.all_gather(token_rows, "latent", axis=1, tiled=True)
    gate_term = jnp.dot(portion, gate_full, preferred_element_type=jnp.float32)
    up_term = jnp.dot(portion, up_full, preferred_element_type=jnp.float32)
    hidden = (jax.nn.gelu(gate_term, approximate=True) * up_term).astype(jnp.bfloat16)
    partial_value = jnp.dot(hidden, down_proj, preferred_element_type=jnp.float32)
    features = lax.psum(partial_value, "latent").astype(jnp.bfloat16)
    features = features.reshape(batches, batch_tokens, features.shape[1])
    enc_scale = MODEL_WIDTH ** (-0.5)
    dec_scale = LATENTS ** (-0.5)
    inputs = features[0]
    local_pre = jnp.dot(inputs, enc_weight, preferred_element_type=jnp.float32)
    pre_latent = enc_scale * row_total(local_pre) + enc_bias
    latents = (jax.nn.softplus(sharpness * pre_latent) / sharpness).astype(jnp.bfloat16)
    local_rebuilt = jnp.dot(latents, dec_weight, preferred_element_type=jnp.float32)
    rebuilt_share = lax.psum_scatter(local_rebuilt, "latent", scatter_dimension=1, tiled=True)
    share_cols = rebuilt_share.shape[1]
    col_offset = lax.axis_index("latent") * share_cols
    inputs_here = lax.dynamic_slice_in_dim(inputs, col_offset, share_cols, 1)
    bias_here = lax.dynamic_slice_in_dim(dec_bias, col_offset, share_cols, 0)
    grad_share = (
        2.0 * (dec_scale * rebuilt_share + bias_here - inputs_here.astype(jnp.float32))
    ).astype(jnp.bfloat16)
    residual_grad = lax.all_gather(grad_share, "latent", axis=1, tiled=True)
    local_back = lax.dot_general(
        residual_grad, dec_weight, (((1,), (1,)), ((), ())), preferred_element_type=jnp.float32
    )
    back_sum = row_total(local_back)
    latent_grad = (
        jax.nn.sigmoid(sharpness * pre_latent) * (dec_scale * back_sum + sparsity_cost)
    ).astype(jnp.bfloat16)
    dec_grad = dec_scale * lax.dot_general(
        latents, residual_grad, (((0,), (0,)), ((), ())), preferred_element_type=jnp.float32
    )
    enc_grad = enc_scale * lax.dot_general(
        inputs, latent_grad, (((0,), (0,)), ((), ())), preferred_element_type=jnp.float32
    )
    enc_bias = enc_bias - enc_bias_rate * jnp.sum(latent_grad, axis=0, dtype=jnp.float32)
    dec_bias = dec_bias - dec_bias_rate * jnp.sum(residual_grad, axis=0, dtype=jnp.float32)
    enc_weight = (enc_weight.astype(jnp.float32) - weight_rate * enc_grad).astype(jnp.bfloat16)
    dec_weight = (dec_weight.astype(jnp.float32) - weight_rate * dec_grad).astype(jnp.bfloat16)
    return (enc_weight, enc_bias, dec_weight, dec_bias)


def solution(mesh):
    return jax.shard_map(
        body,
        mesh=mesh,
        in_specs=(
            P("groups", None, "latent"),
            P("rows", "latent"),
            P("rows", "latent"),
            P("latent", "rows"),
            P(("groups", "rows"), "latent"),
            P(("groups", "latent")),
            P(("groups", "latent"), "rows"),
            P(("groups", "rows")),
        ),
        out_specs=(
            P(("groups", "rows"), "latent"),
            P(("groups", "latent")),
            P(("groups", "latent"), "rows"),
            P(("groups", "rows")),
        ),
        check_vma=False,
    )
```

profile of v0, /device:TPU:0, one launch (start us, length us, event | category | flops | bytes accessed | tf_op | source)
XLA Modules:
  0.0 395.7 jit_solution(4908214912626969955)
XLA Ops:
  7.2 0.0 copy-start
  7.2 0.0 all-gather.4.cloned.1.call-start
  7.2 0.7 all-gather.4.cloned.1.call-update
  7.9 0.0 all-gather.6.cloned.1.call-start
  8.0 0.7 all-gather.6.cloned.1.call-update
  8.7 0.0 all-reduce.4.cloned.1.call-start
  8.7 18.4 %all-gather = bf16[1,128,2304]{1,2,0:T(8,128)(2,1)S(1)} all-gather(bf16[1,128,576]{1,2,0:T(8,128)(2,1)} %param.8), channel_id=2, replica_groups=mesh['groups'=2,'latent'=4,'rows'=4] {'latent'}, dimensions={2}, use_global_device_ids=true | all-gather | bytes 737280 | tf_op jit(solution)/shard_map/all_gather | solution.py:30
  27.1 26.0 %all-gather.4.cloned.1.call-done = bf16[2304,1152]{1,0:T(8,128)(2,1)} async-done(((bf16[576,1152]{1,0:T(8,128)(2,1)}), bf16[2304,1152]{1,0:T(8,128)(2,1)}) %all-gather.4.cloned.1.call-update) | async-done | bytes 5308432 | tf_op jit(solution)/shard_map/all_gather | solution.py:23
  53.1 3.5 fusion.14
  56.6 38.9 %all-gather.6.cloned.1.call-done = bf16[2304,1152]{1,0:T(8,128)(2,1)} async-done(((bf16[576,1152]{1,0:T(8,128)(2,1)}), bf16[2304,1152]{1,0:T(8,128)(2,1)}) %all-gather.6.cloned.1.call-update) | async-done | bytes 5308432 | tf_op jit(solution)/shard_map/all_gather | solution.py:24
  95.5 0.0 copy-done
  95.5 4.0 fusion.3
  99.5 25.4 %all-reduce.7 = bf16[128,576]{0,1:T(8,128)(2,1)S(1)} all-reduce(f32[128,576]{0,1:T(8,128)S(1)} %fusion.3), channel_id=1, replica_groups=mesh['groups'=2,'latent'=4,'rows'=4] {'latent'}, use_global_device_ids=true, to_apply=%region_0.0 | all-reduce | flops 73728 | bytes 442368 | tf_op jit(solution)/shard_map/psum | solution.py:35
  124.9 0.0 copy-start.2
  124.9 12.0 %convolution_convert_fusion.1 = bf16[128,16384]{1,0:T(8,128)(2,1)} fusion(bf16[128,576]{0,1:T(8,128)(2,1)S(1)} %all-reduce.7, bf16[576,16384]{1,0:T(8,128)(2,1)} %param.12), kind=kOutput, calls=%fused_computation.4 | convolution fusion | flops 2418016256 | bytes 23216128 | tf_op jit(solution)/shard_map/dot_general | solution.py:40
  136.9 0.0 all-reduce.4.cloned.1.call-update
  136.9 0.0 copy-start.3
  136.9 0.2 reduce-scatter.2.cloned.1.call-start
  137.1 82.7 %all-reduce.4.cloned.1.call-done = bf16[128,16384]{1,0:T(8,128)(2,1)} async-done(((bf16[128,16384]{1,0:T(8,128)(2,1)}), bf16[128,16384]{1,0:T(8,128)(2,1)}) %all-reduce.4.cloned.1.call-update) | async-done | bytes 4194320 | tf_op jit(solution)/shard_map/psum | solution.py:18
  219.8 0.0 copy-done.2
  219.8 15.9 %fusion.25 = f32[128,576]{0,1:T(8,128)} fusion(bf16[16384,576]{0,1:T(8,128)(2,1)} %param.14, bf16[128,16384]{1,0:T(8,128)(2,1)} %all-reduce.4.cloned.1.call-done, f32[16384]{0:T(1024)S(1)} %copy-done.2), kind=kOutput, calls=%fused_computation.36 | convolution fusion | flops 2441084928 | bytes 23429120 | tf_op jit(solution)/shard_map/dot_general | solution.py:43
  235.7 0.0 reduce-scatter.2.cloned.1.call-update
  235.8 0.0 all-reduce.6.cloned.1.call-start
  235.8 0.0 copy-done.3
  235.8 0.1 dynamic_slice.6
  235.9 20.1 %reduce-scatter.2.cloned.1.call-done = f32[128,144]{0,1:T(8,128)} async-done(((f32[128,576]{0,1:T(8,128)}), f32[128,144]{0,1:T(8,128)}) %reduce-scatter.2.cloned.1.call-update) | async-done | bytes 73744 | tf_op jit(solution)/shard_map/reduce_scatter | solution.py:44
  256.0 1.0 multiply_convert_fusion.1
  256.9 13.5 %all_gather.15 = bf16[128,576]{0,1:T(8,128)(2,1)S(1)} all-gather(bf16[128,144]{0,1:T(8,128)(2,1)S(1)} %multiply_convert_fusion.1), channel_id=1, replica_groups=mesh['groups'=2,'latent'=4,'rows'=4] {'latent'}, dimensions={1}, use_global_device_ids=true | all-gather | bytes 184320 | tf_op jit(solution)/shard_map/all_gather | solution.py:52
  270.4 12.0 %convolution_convert_fusion = bf16[128,16384]{1,0:T(8,128)(2,1)} fusion(bf16[128,576]{0,1:T(8,128)(2,1)S(1)} %all_gather.15, bf16[16384,576]{0,1:T(8,128)(2,1)} %param.14), kind=kOutput, calls=%fused_computation.3 | convolution fusion | flops 2418016256 | bytes 23216128 | tf_op jit(solution)/shard_map/dot_general | solution.py:53
  282.3 0.1 convert_reduce_fusion.1
  282.5 0.0 all-reduce.6.cloned.1.call-update
  282.5 0.6 multiply_subtract_fusion.1
  283.1 32.5 %subtract_convert_fusion = bf16[16384,576]{0,1:T(8,128)(2,1)} fusion(bf16[16384,576]{0,1:T(8,128)(2,1)} %param.14, bf16[128,576]{0,1:T(8,128)(2,1)S(1)} %all_gather.15, bf16[128,16384]{1,0:T(8,128)(2,1)} %all-reduce.4.cloned.1.call-done, f32[16384]{0:T(1024)S(1)} %copy-done.2), kind=kOutput, calls=%fused_computation | convolution fusion | flops 2478833664 | bytes 42156032 | tf_op jit(solution)/shard_map/dot_general | solution.py:60
  315.6 50.7 %all-reduce.6.cloned.1.call-done = bf16[128,16384]{1,0:T(8,128)(2,1)} async-done(((bf16[128,16384]{1,0:T(8,128)(2,1)}), bf16[128,16384]{1,0:T(8,128)(2,1)}) %all-reduce.6.cloned.1.call-update) | async-done | bytes 4194320 | tf_op jit(solution)/shard_map/psum | solution.py:18
  366.3 7.7 %convert_reduce_fusion = (f32[16384]{0:T(1024)S(1)}, bf16[128,16384]{1,0:T(8,128)(2,1)}) fusion(bf16[128,16384]{1,0:T(8,128)(2,1)} %all-reduce.6.cloned.1.call-done, f32[16384]{0:T(1024)S(1)} %copy-done.2, bf16[128,16384]{1,0:T(8,128)(2,1)} %all-reduce.4.cloned.1.call-done), kind=kLoop, calls=%fused_computation.7 | loop fusion | flops 29343744 | bytes 12713984 | tf_op jit(solution)/shard_map/reduce_sum | solution.py:66
  374.0 0.0 copy-start.1
  374.0 14.5 %subtract_convert_fusion.1 = bf16[576,16384]{1,0:T(8,128)(2,1)} fusion(bf16[576,16384]{1,0:T(8,128)(2,1)} %param.12, bf16[128,576]{0,1:T(8,128)(2,1)S(1)} %all-reduce.7, bf16[128,16384]{1,0:T(8,128)(2,1)} %get-tuple-element.5), kind=kOutput, calls=%fused_computation.1 | convolution fusion | flops 2453667840 | bytes 42090496 | tf_op jit(solution)/shard_map/dot_general | solution.py:63
  388.5 0.6 multiply_subtract_fusion
  389.1 0.0 copy-done.1
Async XLA Ops:
  7.2 88.3 %copy-start = (bf16[1152,576]{0,1:T(8,128)(2,1)S(1)}, bf16[1152,576]{0,1:T(8,128)(2,1)}, u32[]{:S(2)}) copy-start(bf16[1152,576]{0,1:T(8,128)(2,1)} %param.11) | copy-start | bytes 3981316
  7.2 45.9 %all-gather.4.cloned.1.call-start = ((), (), s32[]{:S(2)}) async-start(), calls=%async_computation.1 | async-start | bytes 6635520 | tf_op jit(solution)/shard_map/all_gather | solution.py:23
  7.9 87.6 %all-gather.6.cloned.1.call-start = ((), (), s32[]{:S(2)}) async-start(), calls=%async_computation.2 | async-start | bytes 6635520 | tf_op jit(solution)/shard_map/all_gather | solution.py:24
  8.7 211.1 %all-reduce.4.cloned.1.call-start = ((), (), s32[]{:S(2)}) async-start(), calls=%async_computation.3 | async-start | bytes 8388608 | tf_op jit(solution)/shard_map/psum | solution.py:18
  124.9 94.9 %copy-start.2 = (f32[16384]{0:T(1024)S(1)}, f32[16384]{0:T(1024)}, u32[]{:S(2)}) copy-start(f32[16384]{0:T(1024)} %param.13) | copy-start | bytes 196612
  136.9 98.9 %copy-start.3 = (f32[576]{0:T(1024)S(1)}, f32[576]{0:T(1024)}, u32[]{:S(2)}) copy-start(f32[576]{0:T(1024)} %param.15) | copy-start | bytes 6916
  136.9 119.1 %reduce-scatter.2.cloned.1.call-start = ((), (), s32[]{:S(2)}) async-start(), calls=%async_computation.4 | async-start | bytes 368640 | tf_op jit(solution)/shard_map/reduce_scatter | solution.py:44
  235.8 130.6 %all-reduce.6.cloned.1.call-start = ((), (), s32[]{:S(2)}) async-start(), calls=%async_computation.5 | async-start | bytes 8388608 | tf_op jit(solution)/shard_map/psum | solution.py:18
  374.0 15.1 %copy-start.1 = (bf16[1152,576]{0,1:T(8,128)(2,1)S(1)}, bf16[1152,576]{0,1:T(8,128)(2,1)}, u32[]{:S(2)}) copy-start(bf16[1152,576]{0,1:T(8,128)(2,1)} %param.11) | copy-start | bytes 3981316
Sparse Core Ops, SparseCore 0:
  9.6 43.4 all-gather.3
  54.7 40.7 all-gather.5
  137.0 82.7 all-reduce.3
  235.9 20.0 reduce-scatter.1
  282.6 83.6 all-reduce.5
where the time goes:
time: 396 us
  waiting for transfers between devices  220 us (56%)
  matrix products  94.3 us (24%)
  blocking collectives  57.2 us (14%)
  between operations  13.8 us (3%)
  other arithmetic  10 us (3%)
    psum x2, waiting for transfers between devices, row_total(): return lax.psum(term.astype(jnp.bfloat16), 'rows').astype(jnp.float32)  133 us
    all_gather x1, waiting for transfers between devices, body(): lax.all_gather(up_proj, 'rows', axis=0, tiled=True)  38.9 us
    dot_general x1, matrix products, body(): lax.dot_general(latents, residual_grad, (((0,), (0,)), ((), ())), preferr...  32.5 us
    all_gather x1, waiting for transfers between devices, body(): lax.all_gather(gate_proj, 'rows', axis=0, tiled=True)  26 us
    psum x1, blocking collectives, body(): features = lax.psum(partial_value, 'latent').astype(jnp.bfloat16)  25.4 us
    reduce_scatter x1, waiting for transfers between devices, body(): lax.psum_scatter(local_rebuilt, 'latent', scatter_dimension=1, tiled=True)  20.1 us
    all_gather x1, blocking collectives, body(): portion = lax.all_gather(token_rows, 'latent', axis=1, tiled=True)  18.4 us
    dot_general x1, matrix products, body(): jnp.dot(latents, dec_weight, preferred_element_type=jnp.float32)  15.9 us
  transfers between devices with their start and end apart: 5, of which 5 were waited for; matrix products, arithmetic and copies ran while one was open for 9% of the time, Pallas kernels for 0%

commit v1 on v0

v1 whole, which is shorter than its diff:
```python
import math

import jax
import jax.numpy as jnp
from jax import lax
from jax.experimental import pallas as pl
from jax.experimental.pallas import tpu as pltpu
from jax.sharding import PartitionSpec as P

sparsity_cost = 0.1
sharpness = 8.0
weight_rate = 2.0
enc_bias_rate = 0.01
dec_bias_rate = 0.002

BF16, F32 = jnp.bfloat16, jnp.float32
MIB = 2 ** 20
IN_VMEM = pl.BlockSpec(memory_space=pltpu.VMEM)
UNTOUCHED = pl.BlockSpec(memory_space=pl.ANY)


def dot(a, b, over):
    return lax.dot_general(a, b, (over, ((), ())), preferred_element_type=F32)


def flip(value, axis, size, bit):
    return lax.ppermute(value, axis, [(i, i ^ bit) for i in range(size)])


SENT_PARTS = 4


def stacked(refs):
    return jnp.concatenate([ref[...] for ref in refs], axis=0)


def spread(value, refs):
    rows = refs[0].shape[0]
    for i, ref in enumerate(refs):
        ref[...] = value[i * rows:(i + 1) * rows]


class Cut:
    def __init__(self, half, start, width):
        self.half, self.start, self.width = half, start, width
        self.step = math.gcd(math.gcd(half, start), math.gcd(width, 4096))
        while self.step > 2048:
            self.step //= 2
        self.steps = width // self.step
        self.grid = 2 * self.steps

    def first(self, rows):
        return pl.BlockSpec((rows, self.step), lambda j, side: (0, jnp.minimum(j, self.steps - 1)))

    def second(self, rows):
        return pl.BlockSpec((rows, self.step), lambda j, side: (0, jnp.maximum(j - self.steps, 0)))

    def place(self, j, side):
        late = jnp.where(j < self.steps, 0, 1)
        half = jnp.where(j < self.steps, 1 - side[0], side[0])
        return (half * self.half + self.start) // self.step + j - late * self.steps

    def whole(self, rows):
        return pl.BlockSpec((rows, self.step), lambda j, side: (0, self.place(j, side)))

    def columns(self, side):
        return pl.ds(pl.multiple_of(self.place(pl.program_id(0), side) * self.step, self.step), self.step)

    def pick(self, first_refs, second_ref):
        return jnp.where(pl.program_id(0) < self.steps, stacked(first_refs), second_ref[...])


def cuts_of(half, shares):
    unit = half // sum(shares)
    if unit * sum(shares) != half or unit % 128:
        return [Cut(half, 0, half)]
    cuts, start = [], 0
    for share in shares:
        cuts.append(Cut(half, start, share * unit))
        start += share * unit
    return cuts


def shape(*dims, dtype=BF16):
    return jax.ShapeDtypeStruct(dims, dtype)


class Order:
    def __init__(self, side):
        self.side = side
        self.thread = jnp.zeros((8, 128), F32)
        self.kept = {}

    def call(self, kernel, grid, operands, in_specs, out_specs, out_shape, use=(), aliases=None, vmem=6, scratch=(),
             bring=None):
        names, bring = list(self.kept), bring or {}
        n_in, n_out, n_kept, n_new = len(operands), len(out_shape), len(names), len(bring)
        pieces = 12

        def within(side_ref, *refs):
            ins, refs = refs[:n_in], refs[n_in:]
            weights, refs = dict(zip(names, refs[:n_kept])), refs[n_kept + 1:]
            sources, refs = refs[:n_new], refs[n_new:]
            outs, refs = refs[:n_out], refs[n_out + n_kept + 1:]
            targets, refs = refs[:n_new], refs[n_new:]
            copies = []
            for source, target in zip(sources, targets):
                count = math.gcd(source.shape[0] // 16, pieces)
                rows = source.shape[0] // count
                for i in range(count):
                    part = pl.ds(i * rows, rows)
                    copies.append(pltpu.make_async_copy(source.at[part], target.at[part], refs[-1].at[len(copies)]))
            step = pl.program_id(0)

            @pl.when(step == 0)
            def _():
                for copy in copies:
                    copy.start()

            kernel(side_ref, *ins, *[weights[name] for name in use], *outs, *(refs[:-1] if bring else refs))

            @pl.when(step == grid - 1)
            def _():
                for copy in copies:
                    copy.wait()

        kept = [pltpu.with_memory_space_constraint(self.kept[name], pltpu.VMEM) for name in names]
        new = [pltpu.with_memory_space_constraint(weight, pltpu.HBM) for weight in bring.values()]
        joined = dict(aliases or {})
        joined.update({1 + n_in + i: n_out + i for i in range(n_kept + 1)})
        results = pl.pallas_call(
            within,
            grid_spec=pltpu.PrefetchScalarGridSpec(
                num_scalar_prefetch=1,
                grid=(grid,),
                in_specs=in_specs + [IN_VMEM] * n_kept + [UNTOUCHED] + [pl.BlockSpec(memory_space=pltpu.HBM)] * n_new,
                out_specs=out_specs + [IN_VMEM] * n_kept + [UNTOUCHED] + [IN_VMEM] * n_new,
                scratch_shapes=list(scratch) + ([pltpu.SemaphoreType.DMA((pieces * n_new,))] if bring else []),
            ),
            out_shape=out_shape
            + [pltpu.VMEM(k.shape, k.dtype) for k in kept]
            + [shape(8, 128, dtype=F32)]
            + [pltpu.VMEM(w.shape, w.dtype) for w in new],
            input_output_aliases=joined,
            compiler_params=pltpu.CompilerParams(vmem_limit_bytes=vmem * MIB),
            cost_estimate=pl.CostEstimate(flops=1, bytes_accessed=1, transcendentals=0),
        )(self.side, *operands, *kept, self.thread, *new)
        self.kept = dict(zip(names, results[n_out:]))
        self.thread = results[n_out + n_kept]
        self.kept.update(zip(bring, results[n_out + n_kept + 1:]))
        return list(results[:n_out])

    def keep(self, **weights):
        self.call(lambda *refs: None, 1, (), [], [], [], vmem=1, bring=weights)

    def drop(self, *names):
        for name in names:
            del self.kept[name]


def project(run, cut, tokens, weight):
    count, width = tokens.shape

    def kernel(side_ref, tokens_ref, weight_ref, *refs):
        product = dot(tokens_ref[...], weight_ref[:, cut.columns(side_ref)], ((1,), (0,))).astype(BF16)
        late = pl.program_id(0) >= cut.steps

        @pl.when(jnp.logical_not(late))
        def _():
            spread(product, refs[:-1])

        @pl.when(late)
        def _():
            refs[-1][...] = product

    each = count // SENT_PARTS
    *for_other, mine = run.call(
        kernel, cut.grid, (tokens,), [IN_VMEM], [cut.first(each)] * SENT_PARTS + [cut.second(count)],
        [shape(each, cut.width)] * SENT_PARTS + [shape(count, cut.width)], use=[weight],
    )
    return for_other, mine


def added(run, mine, received, dtype=BF16):
    def kernel(side_ref, mine_ref, received_ref, out_ref):
        out_ref[...] = (mine_ref[...].astype(F32) + received_ref[...].astype(F32)).astype(dtype)

    return run.call(
        kernel, 1, (mine, received), [IN_VMEM] * 2, [IN_VMEM], [shape(*mine.shape, dtype=dtype)],
    )[0]


def added_parts(run, mine, received):
    def kernel(side_ref, mine_ref, *refs):
        refs[-1][...] = (mine_ref[...].astype(F32) + stacked(refs[:-1]).astype(F32)).astype(BF16)

    return run.call(
        kernel, 1, (mine, *received), [IN_VMEM] * (1 + len(received)), [IN_VMEM], [shape(*mine.shape)]
    )[0]


def token_parts(run, activations_t, parts, rows):
    width, count = activations_t.shape
    each = count // parts

    def kernel(side_ref, activations_ref, *refs):
        tokens = activations_ref[...].T
        for part, out_ref in enumerate(refs[len(rows):len(rows) + parts]):
            out_ref[...] = tokens[part * each:(part + 1) * each]

    results = run.call(
        kernel, 1, (activations_t,) + tuple(rows), [IN_VMEM] + [UNTOUCHED] * len(rows),
        [IN_VMEM] * parts + [UNTOUCHED] * len(rows),
        [shape(each, width)] * parts + [shape(*r.shape, dtype=r.dtype) for r in rows],
        aliases={2 + i: parts + i for i in range(len(rows))},
    )
    return results[:parts], results[parts:]


def turned(run, parts):
    count, width = parts[0].shape

    def kernel(side_ref, first_ref, second_ref, out_ref):
        out_ref[...] = jnp.concatenate([first_ref[...], second_ref[...]], axis=0).T

    return run.call(
        kernel, 1, tuple(parts), [IN_VMEM] * 2, [IN_VMEM], [shape(width, 2 * count)]
    )[0]


def residual_grad(run, mine, received, bias, features, dec_scale):
    def kernel(side_ref, mine_ref, received_ref, bias_ref, features_ref, out_ref):
        rebuilt = dec_scale * (mine_ref[...].astype(F32) + received_ref[...].astype(F32)) + bias_ref[...]
        out_ref[...] = (2.0 * (rebuilt - features_ref[...].astype(F32))).astype(BF16)

    return run.call(
        kernel, 1, (mine, received, bias, features), [IN_VMEM] * 4, [IN_VMEM], [shape(*features.shape)],
    )[0]


def update_bias(run, bias, parts):
    def kernel(side_ref, bias_ref, first_ref, second_ref, out_ref):
        both = jnp.concatenate([first_ref[...], second_ref[...]], axis=0).astype(F32)
        out_ref[...] = (bias_ref[...] - dec_bias_rate * jnp.sum(both, axis=0, keepdims=True)).reshape(out_ref.shape)

    return run.call(
        kernel, 1, (bias,) + tuple(parts), [IN_VMEM] * 3, [IN_VMEM], [shape(bias.shape[1], dtype=F32)],
    )[0]


def gate_or_up(run, own, tokens, hidden, received=None):
    count = tokens.shape[0]

    def kernel(side_ref, tokens_ref, *refs):
        gate_ref, up_ref, out_ref = refs[-3:]
        for value, weight_ref in enumerate((gate_ref, up_ref) if own else (up_ref, gate_ref)):
            @pl.when(side_ref[0] == value)
            def _():
                total = dot(tokens_ref[...], weight_ref[...], ((1,), (0,)))
                if received is not None:
                    total = total + refs[0][...].astype(F32)
                out_ref[...] = total.astype(BF16)

    more = () if received is None else (received,)
    return run.call(
        kernel, 1, (tokens,) + more, [IN_VMEM] * (1 + len(more)), [IN_VMEM], [shape(count, hidden)],
        use=["gate", "up"],
    )[0]


def layer_output(run, own_term, other_term, width):
    count, hidden = own_term.shape

    def kernel(side_ref, own_ref, other_ref, down_ref, out_ref):
        for value, (gate_ref, up_ref) in enumerate(((own_ref, other_ref), (other_ref, own_ref))):
            @pl.when(side_ref[0] == value)
            def _():
                hidden = (jax.nn.gelu(gate_ref[...], approximate=True) * up_ref[...]).astype(BF16)
                out_ref[...] = dot(hidden, down_ref[...], ((1,), (1,))).astype(BF16)

    return run.call(
        kernel, 1, (own_term, other_term), [IN_VMEM] * 2, [IN_VMEM], [shape(count, width)], use=["down"],
    )[0]


def pre_of(mine, other, bias, enc_scale):
    return enc_scale * (mine.astype(F32) + other.astype(F32)) + bias


def over_own(cut):
    def local(rows):
        return pl.BlockSpec((rows, cut.step), lambda j, side: (0, j))

    def whole(rows):
        return pl.BlockSpec((rows, cut.step), lambda j, side: (0, cut.place(j + cut.steps, side)))

    return local, whole


def latents_of(run, cut, mine, other, bias, enc_scale):
    count = mine.shape[0]
    local, whole = over_own(cut)

    def kernel(side_ref, mine_ref, other_ref, bias_ref, latents_ref, *sent_refs):
        scaled = sharpness * pre_of(mine_ref[...], other_ref[...], bias_ref[...], enc_scale)
        soft = jnp.maximum(scaled, 0.0) + jnp.log1p(jnp.exp(-jnp.abs(scaled)))
        latents = (soft * (1.0 / sharpness)).astype(BF16)
        latents_ref[...] = latents
        spread(latents, sent_refs)

    each = count // SENT_PARTS
    latents, *sent = run.call(
        kernel, cut.steps, (mine, other, bias), [local(count), local(count), whole(1)],
        [local(count)] + [local(each)] * SENT_PARTS,
        [shape(count, cut.width)] + [shape(each, cut.width)] * SENT_PARTS,
    )
    return latents, sent


def decode(run, cut, latents_other, latents_own, weight, width, partial, last):
    count = latents_own.shape[0]

    n_first = len(latents_other)

    def kernel(side_ref, *refs):
        first_refs, second_ref = refs[:n_first], refs[n_first]
        weight_ref, sum_ref, total = refs[-3:]

        @pl.when(pl.program_id(0) == 0)
        def _():
            total[...] = jnp.zeros_like(total) if partial is None else refs[n_first + 1][...]

        total[...] += dot(
            cut.pick(first_refs, second_ref), weight_ref[:, cut.columns(side_ref)], ((1,), (1,))
        )

        @pl.when(pl.program_id(0) == cut.grid - 1)
        def _():
            sum_ref[...] = total[...].astype(sum_ref.dtype)

    more = () if partial is None else (partial,)
    return run.call(
        kernel, cut.grid, (*latents_other, latents_own) + more,
        [cut.first(count // n_first)] * n_first + [cut.second(count)] + [IN_VMEM] * len(more),
        [pl.BlockSpec((count, width), lambda j, side: (0, 0))],
        [shape(count, width, dtype=BF16 if last else F32)],
        use=[weight], scratch=[pltpu.VMEM((count, width), F32)],
    )[0]


def latent_grad(run, cut, mine, other, bias, back, back_other, enc_scale, dec_scale):
    count = mine.shape[0]
    local, whole = over_own(cut)

    def kernel(side_ref, mine_ref, other_ref, bias_ref, back_ref, back_other_ref, grad_ref, *sent_refs):
        scaled = sharpness * pre_of(mine_ref[...], other_ref[...], bias_ref[...], enc_scale)
        total = back_ref[...].astype(F32) + back_other_ref[...].astype(F32)
        grad = (jax.nn.sigmoid(scaled) * (dec_scale * total + sparsity_cost)).astype(BF16)
        grad_ref[...] = grad
        spread(grad, sent_refs)

    each = count // SENT_PARTS
    grad, *sent = run.call(
        kernel, cut.steps, (mine, other, bias, back, back_other),
        [local(count), local(count), whole(1), local(count), local(count)],
        [local(count)] + [local(each)] * SENT_PARTS,
        [shape(count, cut.width)] + [shape(each, cut.width)] * SENT_PARTS,
    )
    return grad, sent


def update(run, cut, left, rights, weight, scale, target, latents, bias=None):
    width = left.shape[0]
    count, n_first = rights[0][1].shape[0], len(rights[0][0])
    each = n_first + 1
    given = () if bias is None else (bias,)
    more = () if target is None else tuple(target)
    n_out = 1 + len(given)

    def kernel(side_ref, left_ref, *refs):
        weight_ref, outs = refs[-1 - n_out], refs[-n_out:]
        both = jnp.concatenate(
            [cut.pick(refs[i * each:i * each + n_first], refs[i * each + n_first]) for i in range(len(rights))], axis=0
        )
        step = (weight_rate * scale) * dot(left_ref[...], both, ((1,), (0,)))
        outs[0][...] = (weight_ref[:, cut.columns(side_ref)].astype(F32) - step).astype(BF16)
        if bias is not None:
            summed = jnp.sum(both.astype(F32), axis=0, keepdims=True)
            outs[1][...] = refs[each * len(rights)][...] - enc_bias_rate * summed

    operands = [left]
    for first, second in rights:
        operands += [*first, second]
    return run.call(
        kernel, cut.grid, (*operands, *given, *more),
        [IN_VMEM] + ([cut.first(count // n_first)] * n_first + [cut.second(count)]) * len(rights)
        + [cut.whole(1)] * len(given) + [UNTOUCHED] * len(more),
        [cut.whole(width)] + [cut.whole(1)] * len(given),
        [shape(width, latents)] + [shape(1, latents, dtype=F32)] * len(given),
        aliases={1 + len(operands) + len(given) + i: i for i in range(len(more))},
        use=[weight], vmem=14,
    )


def solution(mesh):
    n_rows, n_latent = mesh.shape["rows"], mesh.shape["latent"]
    row_bits = [1 << b for b in range(1, n_rows.bit_length() - 1)]
    latent_bits = [1 << b for b in range(n_latent.bit_length() - 1)]

    def beside(value):
        return flip(value, "rows", n_rows, 1)

    def across(run, value):
        for bit in row_bits[:-1]:
            value = added(run, value, flip(value, "rows", n_rows, bit))
        return value, flip(value, "rows", n_rows, row_bits[-1])

    def latent_terms(run, values):
        for bit in latent_bits[:-1]:
            received = [flip(value, "latent", n_latent, bit) for value in values]
            values = [added(run, *pair) for pair in zip(values, received)]
        return [(value, flip(value, "latent", n_latent, latent_bits[-1])) for value in values]

    def body(activations_in, gate_proj, up_proj, down_proj, enc_weight, enc_bias, dec_weight, dec_bias):
        width, local_latents = enc_weight.shape
        count = activations_in.shape[0] * activations_in.shape[1]
        enc_scale = (width * n_rows) ** -0.5
        dec_scale = (local_latents * n_latent) ** -0.5
        row = lax.axis_index("rows")
        core = row % 2
        own = core.astype(jnp.int32).reshape(1)

        parts = 2
        run = Order(own)
        pieces, (bias, out_bias) = token_parts(
            run, activations_in.reshape(count, activations_in.shape[2]).T, parts,
            (enc_bias.reshape(1, local_latents), dec_bias.reshape(1, width)),
        )
        if n_rows == n_latent:
            turn = [(a * n_rows + b, b * n_rows + a) for a in range(n_latent) for b in range(n_rows)]
            pieces = [lax.ppermute(piece, ("latent", "rows"), turn) for piece in pieces]
        else:
            pieces = [lax.all_gather(piece, "latent", axis=1, tiled=True) for piece in pieces]
            pieces = [lax.dynamic_slice_in_dim(piece, row * width, width, 1) for piece in pieces]

        cuts = cuts_of(local_latents // 2, (1, 1, 2))
        n_cuts = len(cuts)
        hidden = gate_proj.shape[1]
        run.keep(gate=gate_proj, up=up_proj, down=down_proj.T)
        run.keep(enc=enc_weight)
        chips = []
        for piece in pieces:
            received = beside(gate_or_up(run, False, piece, hidden))
            chips.append(across(run, gate_or_up(run, True, piece, hidden, received)))
        run.drop("gate", "up")
        layer_parts = []
        for mine, theirs in chips:
            half_term = added(run, mine, theirs, F32)
            layer_parts.append(layer_output(run, half_term, beside(half_term), width))
        run.drop("down")
        layer_terms = latent_terms(run, layer_parts)

        sums = [[None] * n_cuts for _ in range(parts)]
        backs = [[None] * n_cuts for _ in range(parts)]

        def project_all(tokens, weight, which, totals):
            held = None
            for i in [*which, None]:
                if i is not None:
                    for_other, mine = project(run, cuts[i], tokens, weight)
                    now = (i, mine, [beside(part) for part in for_other])
                if held is not None:
                    totals[held[0]] = across(run, added_parts(run, *held[1:]))
                held = now

        latents_own = [[None] * n_cuts for _ in range(parts)]
        latents_other = [[None] * n_cuts for _ in range(parts)]
        partials = [None] * parts

        def open_latents(part, i):
            latents_own[part][i], sent = latents_of(run, cuts[i], *sums[part][i], bias, enc_scale)
            latents_other[part][i] = [beside(piece) for piece in sent]

        def add_decoded(part, i):
            partials[part] = decode(
                run, cuts[i], latents_other[part][i], latents_own[part][i], "dec", width, partials[part], i == n_cuts - 1
            )

        def residual_of(part):
            return residual_grad(run, *latent_terms(run, [partials[part]])[0], out_bias, features[part], dec_scale)

        grads_own = [[None] * n_cuts for _ in range(parts)]
        grads_other = [[None] * n_cuts for _ in range(parts)]

        def open_grad(part, i):
            grads_own[part][i], sent = latent_grad(
                run, cuts[i], *sums[part][i], bias, *backs[part][i], enc_scale, dec_scale
            )
            grads_other[part][i] = [beside(piece) for piece in sent]

        early, late = [*range(n_cuts - 1)], n_cuts - 1
        features = [added(run, *layer_terms[0])]
        project_all(features[0], "enc", [*early, late], sums[0])
        features.append(added(run, *layer_terms[1]))
        waiting = []
        for i in [*early, late]:
            for_other, mine = project(run, cuts[i], features[1], "enc")
            waiting.append((mine, [beside(piece) for piece in for_other]))
        run.drop("enc")

        def send_second(i):
            sums[1][i] = across(run, added_parts(run, *waiting[i]))

        run.keep(dec=dec_weight.T)
        for i in early:
            open_latents(0, i)
            if i:
                add_decoded(0, i - 1)
                send_second(i - 1)
        if early:
            add_decoded(0, early[-1])
            send_second(early[-1])
        open_latents(0, late)
        send_second(late)
        add_decoded(0, late)
        for i in early:
            open_latents(1, i)
            add_decoded(1, i)
        residuals = [residual_of(0)]
        project_all(residuals[0], "dec", [*early, late], backs[0])
        open_latents(1, late)
        add_decoded(1, late)
        residuals.append(residual_of(1))
        if early:
            open_grad(0, 0)
        last_order = [late, *early]
        project_all(residuals[1], "dec", last_order, backs[1])

        residual_t = turned(run, residuals)
        dec_new = None
        for i in [*early, late]:
            if i:
                open_grad(0, i)
            rights = [(latents_other[part][i], latents_own[part][i]) for part in range(parts)]
            dec_new = update(
                run, cuts[i], residual_t, rights, "dec", dec_scale, dec_new, local_latents
            )
        if not early:
            open_grad(0, late)
        out_bias_new = update_bias(run, out_bias, residuals)

        run.drop("dec")
        run.keep(enc=enc_weight)
        features_t = turned(run, features)
        enc_new = None
        for i in last_order:
            open_grad(1, i)
            rights = [(grads_other[part][i], grads_own[part][i]) for part in range(parts)]
            enc_new = update(run, cuts[i], features_t, rights, "enc", enc_scale, enc_new, local_latents, bias)
        enc_new, bias_new = enc_new
        return enc_new, bias_new.reshape(local_latents), dec_new[0].T, out_bias_new

    return jax.shard_map(
        body,
        mesh=mesh,
        in_specs=(
            P("groups", None, "latent"),
            P("rows", "latent"),
            P("rows", "latent"),
            P("latent", "rows"),
            P(("groups", "rows"), "latent"),
            P(("groups", "latent")),
            P(("groups", "latent"), "rows"),
            P(("groups", "rows")),
        ),
        out_specs=(
            P(("groups", "rows"), "latent"),
            P(("groups", "latent")),
            P(("groups", "latent"), "rows"),
            P(("groups", "rows")),
        ),
        check_vma=False,
    )
```

time: 396 us -> 228 us (0.58)
  waiting for transfers between devices: 220 us -> 68.3 us
  matrix products: 94.3 us -> 0 us
  Pallas kernels: 0 us -> 92.2 us
  starting transfers between devices: 0.38 us -> 61.8 us
  blocking collectives: 57.2 us -> 0 us
  between operations: 13.8 us -> 1.83 us
  other arithmetic: 10 us -> 0 us
    psum x2 -> x0, waiting for transfers between devices: 133 us -> none  [row_total(): return lax.psum(term.astype(jnp.bfloat16), 'rows').astype(jnp.float32)]
    dot_general x7 -> x0, matrix products: 94.3 us -> none  [the longest x1 32.5 us: body(): lax.dot_general(latents, residual_grad, (((0,), (0,)), ((), ())), preferr...]
    pallas_call x0 -> x72, Pallas kernels: none -> 92.2 us  [call(): pl.pallas_call(within, grid_spec=pltpu.PrefetchScalarGridSpec(num_scalar_...]
    ppermute x0 -> x124, waiting for transfers between devices: none -> 68.3 us  [the longest x122 68.3 us: flip(): return lax.ppermute(value, axis, [(i, i ^ bit) for i in range(size)])]
    all_gather x2 -> x0, waiting for transfers between devices: 64.9 us -> none  [the longest x1 38.9 us: body(): lax.all_gather(up_proj, 'rows', axis=0, tiled=True)]
    ppermute x0 -> x124, starting transfers between devices: none -> 61.8 us  [the longest x122 60.4 us: flip(): return lax.ppermute(value, axis, [(i, i ^ bit) for i in range(size)])]
    all_gather x2 -> x0, blocking collectives: 31.8 us -> none  [the longest x1 18.4 us: body(): portion = lax.all_gather(token_rows, 'latent', axis=1, tiled=True)]
    psum x1 -> x0, blocking collectives: 25.4 us -> none  [body(): features = lax.psum(partial_value, 'latent').astype(jnp.bfloat16)]
  transfers between devices with their start and end apart: 5 -> 124, of which waited for: 5 -> 37; matrix products, arithmetic and copies ran while one was open for 9% -> 0% of each run, Pallas kernels for 0% -> 36%
where the time goes in v1:
time: 228 us; the launch traced here: 227 us
  Pallas kernels  92.2 us (40%)
  waiting for transfers between devices  68.3 us (30%)
  starting transfers between devices  61.8 us (27%)
  local copies, waits for them, and re-layouts  3.36 us (1%)
    pallas_call x72, Pallas kernels, call(): pl.pallas_call(within, grid_spec=pltpu.PrefetchScalarGridSpec(num_scalar_...  92.2 us
    ppermute x122, waiting for transfers between devices, flip(): return lax.ppermute(value, axis, [(i, i ^ bit) for i in range(size)])  68.3 us
    ppermute x122, starting transfers between devices, flip(): return lax.ppermute(value, axis, [(i, i ^ bit) for i in range(size)])  60.4 us
  transfers between devices with their start and end apart: 124, of which 37 were waited for; matrix products, arithmetic and copies ran while one was open for 0% of the time, Pallas kernels for 36%

profile of v1, /device:TPU:0, one launch (start us, length us, event | category | flops | bytes accessed | tf_op | source)
XLA Modules:
  0.0 227.4 jit_solution(3688824629062474563)
XLA Ops:
  3.9 2.5 %shard_map.112 = (f32[8,128]{1,0:T(8,128)S(1)}, bf16[576,1152]{1,0:T(8,128)(2,1)S(1)}, bf16[576,1152]{1,0:T(8,128)(2,1)S(1)}, bf16[576,1152]{1,0:T(8,128)(2,1)S(1)}) custom-call(s32[1]{0:T(128)} %bitcast.side_ref, f32[8,128]{1,0:T(8,128)S(1)} %get-tuple-element.332.refs_0_, bf16[576,1152]{1,0:T(8,128)(2,1)} %refs_1_.2, ...), custom_call_target="tpu_custom_call", output_to_operand_aliasing={{0}: (1, {})} | custom-call | flops 1 | bytes 1 | tf_op jit(solution)/shard_map/pallas_call | solution.py:131
  6.4 6.5 %shard_map.113 = (bf16[576,1152]{1,0:T(8,128)(2,1)S(1)}, bf16[576,1152]{1,0:T(8,128)(2,1)S(1)}, bf16[576,1152]{1,0:T(8,128)(2,1)S(1)}, f32[8,128]{1,0:T(8,128)S(1)}, bf16[576,16384]{1,0:T(8,128)(2,1)S(1)}) custom-call(s32[1]{0:T(128)} %bitcast.side_ref, ...), custom_call_target="tpu_custom_call", output_to_operand_aliasing={{0}: (1, {}), {1}: (2, {}), {2}: (3, {}), {3}: (4, {})} | custom-call | flops 1 | bytes 1 | tf_op jit(solution)/shard_map/pallas_call | solution.py:131
  13.3 4.4 %collective-permute-start.1 = (bf16[64,1152]{1,0:T(8,128)(2,1)S(1)}, bf16[64,1152]{1,0:T(8,128)(2,1)S(1)}, u32[]{:S(2)}, u32[]{:S(2)}) collective-permute-start(bf16[64,1152]{1,0:T(8,128)(2,1)S(1)} %get-tuple-element.342), channel_id=1, source_target_pairs={{0,1},{1,0},{2,3},{3,2},{4,5},{5,4},{6,7},{7,6},{8,9},{9,8},{10,11... | collective-permute-start | bytes 442376 | tf_op jit(solution)/shard_map/ppermute | solution.py:27
  19.5 4.4 %collective-permute-start.4 = (bf16[64,1152]{1,0:T(8,128)(2,1)S(1)}, bf16[64,1152]{1,0:T(8,128)(2,1)S(1)}, u32[]{:S(2)}, u32[]{:S(2)}) collective-permute-start(bf16[64,1152]{1,0:T(8,128)(2,1)S(1)} %get-tuple-element.355), channel_id=1, source_target_pairs={{0,1},{1,0},{2,3},{3,2},{4,5},{5,4},{6,7},{7,6},{8,9},{9,8},{10,11... | collective-permute-start | bytes 442376 | tf_op jit(solution)/shard_map/ppermute | solution.py:27
  24.0 6.8 %collective-permute-start.2 = (bf16[64,1152]{1,0:T(8,128)(2,1)S(1)}, bf16[64,1152]{1,0:T(8,128)(2,1)S(1)}, u32[]{:S(2)}, u32[]{:S(2)}) collective-permute-start(bf16[64,1152]{1,0:T(8,128)(2,1)S(1)} %get-tuple-element.348.refs_0_), channel_id=1, source_target_pairs={{0,2},{1,3},{2,0},{3,1},{4,6},{5,7},{6,4},{7,5},{8,10},{9,11},{10,... | collective-permute-start | bytes 442376 | tf_op jit(solution)/shard_map/ppermute | solution.py:27
  31.2 4.1 %collective-permute-done.2.refs_1_ = bf16[64,1152]{1,0:T(8,128)(2,1)S(1)} collective-permute-done((bf16[64,1152]{1,0:T(8,128)(2,1)S(1)}, bf16[64,1152]{1,0:T(8,128)(2,1)S(1)}, u32[]{:S(2)}, u32[]{:S(2)}) %collective-permute-start.2) | collective-permute-done | bytes 147488 | tf_op jit(solution)/shard_map/ppermute | solution.py:27
  35.3 1.8 collective-permute-start.7
  37.7 3.9 %collective-permute-done.7.refs_1_ = bf16[64,1152]{1,0:T(8,128)(2,1)S(1)} collective-permute-done((bf16[64,1152]{1,0:T(8,128)(2,1)S(1)}, bf16[64,1152]{1,0:T(8,128)(2,1)S(1)}, u32[]{:S(2)}, u32[]{:S(2)}) %collective-permute-start.7) | collective-permute-done | bytes 147488 | tf_op jit(solution)/shard_map/ppermute | solution.py:27
  41.8 1.5 collective-permute-done.8.refs_1_
  44.6 2.0 collective-permute-done.6.refs_1_
  47.2 1.3 collective-permute-done.10.refs_1_
  48.5 4.7 %collective-permute-done.9.refs_1_ = bf16[64,576]{1,0:T(8,128)(2,1)S(1)} collective-permute-done((bf16[64,576]{1,0:T(8,128)(2,1)S(1)}, bf16[64,576]{1,0:T(8,128)(2,1)S(1)}, u32[]{:S(2)}, u32[]{:S(2)}) %collective-permute-start.9) | collective-permute-done | bytes 73760 | tf_op jit(solution)/shard_map/ppermute | solution.py:27
  53.2 1.2 shard_map.125
  57.6 2.6 %shard_map.128 = (bf16[16,4096]{1,0:T(8,128)(2,1)S(1)}, bf16[16,4096]{1,0:T(8,128)(2,1)S(1)}, bf16[16,4096]{1,0:T(8,128)(2,1)S(1)}, bf16[16,4096]{1,0:T(8,128)(2...) custom-call(s32[1]{0:T(128)} %bitcast.side_ref, ...), custom_call_target="tpu_custom_call", output_to_operand_aliasing={{5}: (2, {}), {6}: (3, {})} | custom-call | flops 1 | bytes 1 | tf_op jit(solution)/shard_map/pallas_call | solution.py:131
  62.7 1.8 collective-permute-start.30
  65.0 1.8 collective-permute-start.29
  66.8 3.8 %collective-permute-done.11.refs_1_ = bf16[64,576]{1,0:T(8,128)(2,1)S(1)} collective-permute-done((bf16[64,576]{1,0:T(8,128)(2,1)S(1)}, bf16[64,576]{1,0:T(8,128)(2,1)S(1)}, u32[]{:S(2)}, u32[]{:S(2)}) %collective-permute-start.11) | collective-permute-done | bytes 73760 | tf_op jit(solution)/shard_map/ppermute | solution.py:27
  70.6 1.2 shard_map.132
  75.5 2.6 %shard_map.134 = (bf16[16,4096]{1,0:T(8,128)(2,1)S(1)}, bf16[16,4096]{1,0:T(8,128)(2,1)S(1)}, bf16[16,4096]{1,0:T(8,128)(2,1)S(1)}, bf16[16,4096]{1,0:T(8,128)(2...) custom-call(s32[1]{0:T(128)} %bitcast.side_ref, ...), custom_call_target="tpu_custom_call", output_to_operand_aliasing={{5}: (2, {}), {6}: (3, {})} | custom-call | flops 1 | bytes 1 | tf_op jit(solution)/shard_map/pallas_call | solution.py:131
  78.2 6.5 %shard_map.135 = (f32[8,128]{1,0:T(8,128)S(1)}, bf16[576,16384]{1,0:T(8,128)(2,1)S(1)}) custom-call(s32[1]{0:T(128)} %bitcast.side_ref, f32[8,128]{1,0:T(8,128)S(1)} %get-tuple-element.433.refs_0_, bf16[576,16384]{1,0:T(8,128)(2,1)} %bitcast.12), custom_call_target="tpu_custom_call", output_to_operand_aliasing={{0}: (1, {})} | custom-call | flops 1 | bytes 1 | tf_op jit(solution)/shard_map/pallas_call | solution.py:131
  85.9 2.2 collective-permute-done.29.refs_1_
  91.6 1.7 shard_map.138
  93.5 1.8 shard_map.140
  97.2 1.7 collective-permute-start.53
  101.2 3.7 %shard_map.144 = (bf16[64,576]{1,0:T(8,128)(2,1)S(1)}, bf16[576,16384]{1,0:T(8,128)(2,1)S(1)}, f32[8,128]{1,0:T(8,128)S(1)}) custom-call(s32[1]{0:T(128)} %bitcast.side_ref, bf16[16,4096]{1,0:T(8,128)(2,1)S(1)} %collective-permute-done.43.refs_0_.refs_1_, ...), custom_call_target="tpu_custom_call", output_to_operand_aliasing={{1}: (7, {}), {2}: (8, {})} | custom-call | flops 1 | bytes 1 | tf_op jit(solution)/shard_map/pallas_call | solution.py:131
  104.8 1.5 collective-permute-done.53.refs_1_
  108.1 1.7 collective-permute-start.63
  109.9 2.0 shard_map.146
  114.9 1.7 shard_map.148
  117.9 6.1 %collective-permute-done.62.refs_1_ = bf16[64,576]{1,0:T(8,128)(2,1)S(1)} collective-permute-done((bf16[64,576]{1,0:T(8,128)(2,1)S(1)}, bf16[64,576]{1,0:T(8,128)(2,1)S(1)}, u32[]{:S(2)}, u32[]{:S(2)}) %collective-permute-start.62) | collective-permute-done | bytes 73760 | tf_op jit(solution)/shard_map/ppermute | solution.py:27
  124.1 1.2 shard_map.151
  128.8 2.7 %shard_map.154 = (bf16[16,4096]{1,0:T(8,128)(2,1)S(1)}, bf16[16,4096]{1,0:T(8,128)(2,1)S(1)}, bf16[16,4096]{1,0:T(8,128)(2,1)S(1)}, bf16[16,4096]{1,0:T(8,128)(2...) custom-call(s32[1]{0:T(128)} %bitcast.side_ref, ...), custom_call_target="tpu_custom_call", output_to_operand_aliasing={{5}: (2, {}), {6}: (3, {})} | custom-call | flops 1 | bytes 1 | tf_op jit(solution)/shard_map/pallas_call | solution.py:131
  135.8 1.8 collective-permute-start.82
  137.6 3.7 %shard_map.158 = (bf16[64,576]{1,0:T(8,128)(2,1)S(1)}, bf16[576,16384]{1,0:T(8,128)(2,1)S(1)}, f32[8,128]{1,0:T(8,128)S(1)}) custom-call(s32[1]{0:T(128)} %bitcast.side_ref, bf16[16,4096]{1,0:T(8,128)(2,1)S(1)} %collective-permute-done.76.refs_0_.refs_6_, ...), custom_call_target="tpu_custom_call", output_to_operand_aliasing={{1}: (7, {}), {2}: (8, {})} | custom-call | flops 1 | bytes 1 | tf_op jit(solution)/shard_map/pallas_call | solution.py:131
  141.4 4.4 %collective-permute-done.80.refs_1_ = bf16[64,576]{1,0:T(8,128)(2,1)S(1)} collective-permute-done((bf16[64,576]{1,0:T(8,128)(2,1)S(1)}, bf16[64,576]{1,0:T(8,128)(2,1)S(1)}, u32[]{:S(2)}, u32[]{:S(2)}) %collective-permute-start.80) | collective-permute-done | bytes 73760 | tf_op jit(solution)/shard_map/ppermute | solution.py:27
  145.9 5.9 %collective-permute-done.81.refs_1_ = bf16[64,576]{1,0:T(8,128)(2,1)S(1)} collective-permute-done((bf16[64,576]{1,0:T(8,128)(2,1)S(1)}, bf16[64,576]{1,0:T(8,128)(2,1)S(1)}, u32[]{:S(2)}, u32[]{:S(2)}) %collective-permute-start.81) | collective-permute-done | bytes 73760 | tf_op jit(solution)/shard_map/ppermute | solution.py:27
  152.2 2.7 %shard_map.162 = (bf16[16,4096]{1,0:T(8,128)(2,1)S(1)}, bf16[16,4096]{1,0:T(8,128)(2,1)S(1)}, bf16[16,4096]{1,0:T(8,128)(2,1)S(1)}, bf16[16,4096]{1,0:T(8,128)(2...) custom-call(s32[1]{0:T(128)} %bitcast.side_ref, ...), custom_call_target="tpu_custom_call", output_to_operand_aliasing={{5}: (2, {}), {6}: (3, {})} | custom-call | flops 1 | bytes 1 | tf_op jit(solution)/shard_map/pallas_call | solution.py:131
  155.9 1.6 collective-permute-start.96
  159.9 1.6 collective-permute-start.95
  167.7 3.1 %shard_map.169 = (bf16[576,16384]{1,0:T(8,128)(2,1)}, bf16[576,16384]{1,0:T(8,128)(2,1)S(1)}, f32[8,128]{1,0:T(8,128)S(1)}) custom-call(s32[1]{0:T(128)} %bitcast.side_ref, bf16[576,128]{1,0:T(8,128)(2,1)S(1)} %get-tuple-element.584.refs_0_, ...), custom_call_target="tpu_custom_call", output_to_operand_aliasing={{1}: (12, {}), {2}: (13, {})} | custom-call | flops 1 | bytes 1 | tf_op jit(solution)/shard_map/pallas_call | solution.py:131
  170.7 16.8 %collective-permute-done.95.refs_4_ = bf16[64,2048]{1,0:T(8,128)(2,1)S(1)} collective-permute-done((bf16[64,2048]{1,0:T(8,128)(2,1)S(1)}, bf16[64,2048]{1,0:T(8,128)(2,1)S(1)}, u32[]{:S(2)}, u32[]{:S(2)}) %collective-permute-start.95) | collective-permute-done | bytes 262176 | tf_op jit(solution)/shard_map/ppermute | solution.py:27
  187.9 3.1 %shard_map.171 = (bf16[576,16384]{1,0:T(8,128)(2,1)}, bf16[576,16384]{1,0:T(8,128)(2,1)S(1)}, f32[8,128]{1,0:T(8,128)S(1)}) custom-call(s32[1]{0:T(128)} %bitcast.side_ref, bf16[576,128]{1,0:T(8,128)(2,1)S(1)} %get-tuple-element.584.refs_0_, bf16[16,2048]{1,0:T(8,128)(2,1)S(1)} %copy-done.31, ...), custom_call_target="tpu_custom_call", output_to_operand_aliasing={{0}: (12, {}), {1}: (13, {}), {2}: (14, {})} | custom-call | flops 1 | bytes 1 | tf_op jit(solution)/shard_map/pallas_call | solution.py:131
  192.9 5.8 %shard_map.173 = (bf16[576,16384]{1,0:T(8,128)(2,1)}, bf16[576,16384]{1,0:T(8,128)(2,1)S(1)}, f32[8,128]{1,0:T(8,128)S(1)}) custom-call(s32[1]{0:T(128)} %bitcast.side_ref, bf16[576,128]{1,0:T(8,128)(2,1)S(1)} %get-tuple-element.584.refs_0_, bf16[16,4096]{1,0:T(8,128)(2,1)S(1)} %copy-done.21, ...), custom_call_target="tpu_custom_call", output_to_operand_aliasing={{0}: (12, {}), {1}: (13, {}), {2}: (14, {})} | custom-call | flops 1 | bytes 1 | tf_op jit(solution)/shard_map/pallas_call | solution.py:131
  199.3 6.5 %shard_map.175 = (f32[8,128]{1,0:T(8,128)S(1)}, bf16[576,16384]{1,0:T(8,128)(2,1)S(1)}) custom-call(s32[1]{0:T(128)} %bitcast.side_ref, f32[8,128]{1,0:T(8,128)S(1)} %get-tuple-element.601.refs_0_, bf16[576,16384]{1,0:T(8,128)(2,1)} %refs_1_.3), custom_call_target="tpu_custom_call", output_to_operand_aliasing={{0}: (1, {})} | custom-call | flops 1 | bytes 1 | tf_op jit(solution)/shard_map/pallas_call | solution.py:131
  207.9 1.6 collective-permute-start.101
  210.6 5.7 %shard_map.178 = (bf16[576,16384]{1,0:T(8,128)(2,1)}, f32[1,16384]{1,0:T(1,128)}, bf16[576,16384]{1,0:T(8,128)(2,1)S(1)}, f32[8,128]{1,0:T(8,128)S(1)}) custom-call(s32[1]{0:T(128)} %bitcast.side_ref, bf16[576,128]{1,0:T(8,128)(2,1)S(1)} %get-tuple-element.604.refs_0_, ...), custom_call_target="tpu_custom_call", output_to_operand_aliasing={{2}: (13, {}), {3}: (14, {})} | custom-call | flops 1 | bytes 1 | tf_op jit(solution)/shard_map/pallas_call | solution.py:131
  218.9 3.1 %shard_map.180 = (bf16[576,16384]{1,0:T(8,128)(2,1)}, f32[1,16384]{1,0:T(1,128)}, bf16[576,16384]{1,0:T(8,128)(2,1)S(1)}, f32[8,128]{1,0:T(8,128)S(1)}) custom-call(s32[1]{0:T(128)} %bitcast.side_ref, bf16[576,128]{1,0:T(8,128)(2,1)S(1)} %get-tuple-element.604.refs_0_, ...), custom_call_target="tpu_custom_call", output_to_operand_aliasing={{0}: (13, {}), {1}: (14, {}), {2}: (15, {}), {3}: (16, {})} | custom-call | flops 1 | bytes 1 | tf_op jit(solution)/shard_map/pallas_call | solution.py:131
  224.3 3.1 %shard_map.182 = (bf16[576,16384]{1,0:T(8,128)(2,1)}, f32[1,16384]{1,0:T(1,128)}, bf16[576,16384]{1,0:T(8,128)(2,1)S(1)}, f32[8,128]{1,0:T(8,128)S(1)}) custom-call(s32[1]{0:T(128)} %bitcast.side_ref, bf16[576,128]{1,0:T(8,128)(2,1)S(1)} %get-tuple-element.604.refs_0_, ...), custom_call_target="tpu_custom_call", output_to_operand_aliasing={{0}: (13, {}), {1}: (14, {}), {2}: (15, {}), {3}: (16, {})} | custom-call | flops 1 | bytes 1 | tf_op jit(solution)/shard_map/pallas_call | solution.py:131
  (361 shorter events, 61.3 us)
Async XLA Ops:
  3.2 9.7 %collective-permute-start = (bf16[64,576]{1,0:T(8,128)(2,1)S(1)}, bf16[64,576]{1,0:T(8,128)(2,1)S(1)}, u32[]{:S(2)}, u32[]{:S(2)}) collective-permute-start(bf16[64,576]{1,0:T(8,128)(2,1)S(1)} %get-tuple-element.331), channel_id=1, source_target_pairs={{0,0},{1,4},{2,8},{3,12},{4,1},{5,5},{6,9},{7,13},{8,2},{9,6},{10,... | collective-permute-start | bytes 221192 | tf_op jit(solution)/shard_map/ppermute | solution.py:441
  13.3 5.5 %collective-permute-start.1 = (bf16[64,1152]{1,0:T(8,128)(2,1)S(1)}, bf16[64,1152]{1,0:T(8,128)(2,1)S(1)}, u32[]{:S(2)}, u32[]{:S(2)}) collective-permute-start(bf16[64,1152]{1,0:T(8,128)(2,1)S(1)} %get-tuple-element.342), channel_id=1, source_target_pairs={{0,1},{1,0},{2,3},{3,2},{4,5},{5,4},{6,7},{7,6},{8,9},{9,8},{10,11... | collective-permute-start | bytes 442376 | tf_op jit(solution)/shard_map/ppermute | solution.py:27
  19.5 11.2 %collective-permute-start.4 = (bf16[64,1152]{1,0:T(8,128)(2,1)S(1)}, bf16[64,1152]{1,0:T(8,128)(2,1)S(1)}, u32[]{:S(2)}, u32[]{:S(2)}) collective-permute-start(bf16[64,1152]{1,0:T(8,128)(2,1)S(1)} %get-tuple-element.355), channel_id=1, source_target_pairs={{0,1},{1,0},{2,3},{3,2},{4,5},{5,4},{6,7},{7,6},{8,9},{9,8},{10,11... | collective-permute-start | bytes 442376 | tf_op jit(solution)/shard_map/ppermute | solution.py:27
  24.0 11.2 %collective-permute-start.2 = (bf16[64,1152]{1,0:T(8,128)(2,1)S(1)}, bf16[64,1152]{1,0:T(8,128)(2,1)S(1)}, u32[]{:S(2)}, u32[]{:S(2)}) collective-permute-start(bf16[64,1152]{1,0:T(8,128)(2,1)S(1)} %get-tuple-element.348.refs_0_), channel_id=1, source_target_pairs={{0,2},{1,3},{2,0},{3,1},{4,6},{5,7},{6,4},{7,5},{8,10},{9,11},{10,... | collective-permute-start | bytes 442376 | tf_op jit(solution)/shard_map/ppermute | solution.py:27
  35.3 6.3 %collective-permute-start.7 = (bf16[64,1152]{1,0:T(8,128)(2,1)S(1)}, bf16[64,1152]{1,0:T(8,128)(2,1)S(1)}, u32[]{:S(2)}, u32[]{:S(2)}) collective-permute-start(bf16[64,1152]{1,0:T(8,128)(2,1)S(1)} %get-tuple-element.369.refs_0_), channel_id=1, source_target_pairs={{0,2},{1,3},{2,0},{3,1},{4,6},{5,7},{6,4},{7,5},{8,10},{9,11},{10,... | collective-permute-start | bytes 442376 | tf_op jit(solution)/shard_map/ppermute | solution.py:27
  41.7 4.9 %collective-permute-start.6 = (bf16[64,576]{1,0:T(8,128)(2,1)S(1)}, bf16[64,576]{1,0:T(8,128)(2,1)S(1)}, u32[]{:S(2)}, u32[]{:S(2)}) collective-permute-start(bf16[64,576]{1,0:T(8,128)(2,1)S(1)} %get-tuple-element.368.refs_0_), channel_id=1, source_target_pairs={{0,4},{4,0},{8,12},{12,8},{1,5},{5,1},{9,13},{13,9},{2,6},{6,2},{1... | collective-permute-start | bytes 221192 | tf_op jit(solution)/shard_map/ppermute | solution.py:27
  44.0 4.5 %collective-permute-start.10 = (bf16[64,576]{1,0:T(8,128)(2,1)S(1)}, bf16[64,576]{1,0:T(8,128)(2,1)S(1)}, u32[]{:S(2)}, u32[]{:S(2)}) collective-permute-start(bf16[64,576]{1,0:T(8,128)(2,1)S(1)} %get-tuple-element.380.refs_0_), channel_id=1, source_target_pairs={{0,4},{4,0},{8,12},{12,8},{1,5},{5,1},{9,13},{13,9},{2,6},{6,2},{1... | collective-permute-start | bytes 221192 | tf_op jit(solution)/shard_map/ppermute | solution.py:27
  46.6 6.6 %collective-permute-start.9 = (bf16[64,576]{1,0:T(8,128)(2,1)S(1)}, bf16[64,576]{1,0:T(8,128)(2,1)S(1)}, u32[]{:S(2)}, u32[]{:S(2)}) collective-permute-start(bf16[64,576]{1,0:T(8,128)(2,1)S(1)} %get-tuple-element.379.refs_0_), channel_id=1, source_target_pairs={{0,8},{4,12},{8,0},{12,4},{1,9},{5,13},{9,1},{13,5},{2,10},{6,14},... | collective-permute-start | bytes 221192 | tf_op jit(solution)/shard_map/ppermute | solution.py:27
  56.8 4.0 %collective-permute-start.20 = (bf16[16,2048]{1,0:T(8,128)(2,1)S(1)}, bf16[16,2048]{1,0:T(8,128)(2,1)S(1)}, u32[]{:S(2)}, u32[]{:S(2)}) collective-permute-start(bf16[16,2048]{1,0:T(8,128)(2,1)S(1)} %get-tuple-element.406), channel_id=1, source_target_pairs={{0,1},{1,0},{2,3},{3,2},{4,5},{5,4},{6,7},{7,6},{8,9},{9,8},{10,11... | collective-permute-start | bytes 196616 | tf_op jit(solution)/shard_map/ppermute | solution.py:27
  56.9 4.3 %collective-permute-start.21 = (bf16[16,2048]{1,0:T(8,128)(2,1)S(1)}, bf16[16,2048]{1,0:T(8,128)(2,1)S(1)}, u32[]{:S(2)}, u32[]{:S(2)}) collective-permute-start(bf16[16,2048]{1,0:T(8,128)(2,1)S(1)} %get-tuple-element.407), channel_id=1, source_target_pairs={{0,1},{1,0},{2,3},{3,2},{4,5},{5,4},{6,7},{7,6},{8,9},{9,8},{10,11... | collective-permute-start | bytes 196616 | tf_op jit(solution)/shard_map/ppermute | solution.py:27
  60.2 4.3 %collective-permute-start.16 = (bf16[16,4096]{1,0:T(8,128)(2,1)S(1)}, bf16[16,4096]{1,0:T(8,128)(2,1)S(1)}, u32[]{:S(2)}, u32[]{:S(2)}) collective-permute-start(bf16[16,4096]{1,0:T(8,128)(2,1)S(1)} %get-tuple-element.401), channel_id=1, source_target_pairs={{0,1},{1,0},{2,3},{3,2},{4,5},{5,4},{6,7},{7,6},{8,9},{9,8},{10,11... | collective-permute-start | bytes 393224 | tf_op jit(solution)/shard_map/ppermute | solution.py:27
  62.7 12.5 %collective-permute-start.30 = (bf16[64,2048]{1,0:T(8,128)(2,1)S(1)}, bf16[64,2048]{1,0:T(8,128)(2,1)S(1)}, u32[]{:S(2)}, u32[]{:S(2)}) collective-permute-start(bf16[64,2048]{1,0:T(8,128)(2,1)S(1)} %get-tuple-element.430.refs_0_), channel_id=1, source_target_pairs={{0,2},{1,3},{2,0},{3,1},{4,6},{5,7},{6,4},{7,5},{8,10},{9,11},{10,... | collective-permute-start | bytes 786440 | tf_op jit(solution)/shard_map/ppermute | solution.py:27
  64.7 31.3 %collective-permute-start.24 = (bf16[64,4096]{1,0:T(8,128)(2,1)S(1)}, bf16[64,4096]{1,0:T(8,128)(2,1)S(1)}, u32[]{:S(2)}, u32[]{:S(2)}) collective-permute-start(bf16[64,4096]{1,0:T(8,128)(2,1)S(1)} %get-tuple-element.418.refs_0_), channel_id=1, source_target_pairs={{0,2},{1,3},{2,0},{3,1},{4,6},{5,7},{6,4},{7,5},{8,10},{9,11},{10,... | collective-permute-start | bytes 1572872 | tf_op jit(solution)/shard_map/ppermute | solution.py:27
  65.0 5.6 %collective-permute-start.11 = (bf16[64,576]{1,0:T(8,128)(2,1)S(1)}, bf16[64,576]{1,0:T(8,128)(2,1)S(1)}, u32[]{:S(2)}, u32[]{:S(2)}) collective-permute-start(bf16[64,576]{1,0:T(8,128)(2,1)S(1)} %get-tuple-element.386.refs_0_), channel_id=1, source_target_pairs={{0,8},{4,12},{8,0},{12,4},{1,9},{5,13},{9,1},{13,5},{2,10},{6,14},... | collective-permute-start | bytes 221192 | tf_op jit(solution)/shard_map/ppermute | solution.py:27
  65.0 23.0 %collective-permute-start.29 = (bf16[64,2048]{1,0:T(8,128)(2,1)S(1)}, bf16[64,2048]{1,0:T(8,128)(2,1)S(1)}, u32[]{:S(2)}, u32[]{:S(2)}) collective-permute-start(bf16[64,2048]{1,0:T(8,128)(2,1)S(1)} %get-tuple-element.429.refs_0_), channel_id=1, source_target_pairs={{0,2},{1,3},{2,0},{3,1},{4,6},{5,7},{6,4},{7,5},{8,10},{9,11},{10,... | collective-permute-start | bytes 786440 | tf_op jit(solution)/shard_map/ppermute | solution.py:27
  73.4 11.7 %collective-permute-start.42 = (bf16[16,2048]{1,0:T(8,128)(2,1)S(1)}, bf16[16,2048]{1,0:T(8,128)(2,1)S(1)}, u32[]{:S(2)}, u32[]{:S(2)}) collective-permute-start(bf16[16,2048]{1,0:T(8,128)(2,1)S(1)} %get-tuple-element.455), channel_id=1, source_target_pairs={{0,1},{1,0},{2,3},{3,2},{4,5},{5,4},{6,7},{7,6},{8,9},{9,8},{10,11... | collective-permute-start | bytes 196616 | tf_op jit(solution)/shard_map/ppermute | solution.py:27
  75.0 10.4 %collective-permute-start.25 = (bf16[16,2048]{1,0:T(8,128)(2,1)S(1)}, bf16[16,2048]{1,0:T(8,128)(2,1)S(1)}, u32[]{:S(2)}, u32[]{:S(2)}) collective-permute-start(bf16[16,2048]{1,0:T(8,128)(2,1)S(1)} %get-tuple-element.425), channel_id=1, source_target_pairs={{0,1},{1,0},{2,3},{3,2},{4,5},{5,4},{6,7},{7,6},{8,9},{9,8},{10,11... | collective-permute-start | bytes 196616 | tf_op jit(solution)/shard_map/ppermute | solution.py:27
  75.2 10.5 %collective-permute-start.26 = (bf16[16,2048]{1,0:T(8,128)(2,1)S(1)}, bf16[16,2048]{1,0:T(8,128)(2,1)S(1)}, u32[]{:S(2)}, u32[]{:S(2)}) collective-permute-start(bf16[16,2048]{1,0:T(8,128)(2,1)S(1)} %get-tuple-element.426), channel_id=1, source_target_pairs={{0,1},{1,0},{2,3},{3,2},{4,5},{5,4},{6,7},{7,6},{8,9},{9,8},{10,11... | collective-permute-start | bytes 196616 | tf_op jit(solution)/shard_map/ppermute | solution.py:27
  89.6 7.6 %collective-permute-start.47 = (bf16[16,4096]{1,0:T(8,128)(2,1)S(1)}, bf16[16,4096]{1,0:T(8,128)(2,1)S(1)}, u32[]{:S(2)}, u32[]{:S(2)}) collective-permute-start(bf16[16,4096]{1,0:T(8,128)(2,1)S(1)} %get-tuple-element.471), channel_id=1, source_target_pairs={{0,1},{1,0},{2,3},{3,2},{4,5},{5,4},{6,7},{7,6},{8,9},{9,8},{10,11... | collective-permute-start | bytes 393224 | tf_op jit(solution)/shard_map/ppermute | solution.py:27
  90.3 5.0 %collective-permute-start.27 = (bf16[16,2048]{1,0:T(8,128)(2,1)S(1)}, bf16[16,2048]{1,0:T(8,128)(2,1)S(1)}, u32[]{:S(2)}, u32[]{:S(2)}) collective-permute-start(bf16[16,2048]{1,0:T(8,128)(2,1)S(1)} %get-tuple-element.427), channel_id=1, source_target_pairs={{0,1},{1,0},{2,3},{3,2},{4,5},{5,4},{6,7},{7,6},{8,9},{9,8},{10,11... | collective-permute-start | bytes 196616 | tf_op jit(solution)/shard_map/ppermute | solution.py:27
  90.5 5.1 %collective-permute-start.28 = (bf16[16,2048]{1,0:T(8,128)(2,1)S(1)}, bf16[16,2048]{1,0:T(8,128)(2,1)S(1)}, u32[]{:S(2)}, u32[]{:S(2)}) collective-permute-start(bf16[16,2048]{1,0:T(8,128)(2,1)S(1)} %get-tuple-element.428), channel_id=1, source_target_pairs={{0,1},{1,0},{2,3},{3,2},{4,5},{5,4},{6,7},{7,6},{8,9},{9,8},{10,11... | collective-permute-start | bytes 196616 | tf_op jit(solution)/shard_map/ppermute | solution.py:27
  91.2 7.8 %collective-permute-start.48 = (bf16[16,4096]{1,0:T(8,128)(2,1)S(1)}, bf16[16,4096]{1,0:T(8,128)(2,1)S(1)}, u32[]{:S(2)}, u32[]{:S(2)}) collective-permute-start(bf16[16,4096]{1,0:T(8,128)(2,1)S(1)} %get-tuple-element.472), channel_id=1, source_target_pairs={{0,1},{1,0},{2,3},{3,2},{4,5},{5,4},{6,7},{7,6},{8,9},{9,8},{10,11... | collective-permute-start | bytes 393224 | tf_op jit(solution)/shard_map/ppermute | solution.py:27
  97.2 9.1 %collective-permute-start.53 = (bf16[64,2048]{1,0:T(8,128)(2,1)S(1)}, bf16[64,2048]{1,0:T(8,128)(2,1)S(1)}, u32[]{:S(2)}, u32[]{:S(2)}) collective-permute-start(bf16[64,2048]{1,0:T(8,128)(2,1)S(1)} %get-tuple-element.481.refs_0_), channel_id=1, source_target_pairs={{0,2},{1,3},{2,0},{3,1},{4,6},{5,7},{6,4},{7,5},{8,10},{9,11},{10,... | collective-permute-start | bytes 786440 | tf_op jit(solution)/shard_map/ppermute | solution.py:27
  99.0 12.9 %collective-permute-start.52 = (bf16[64,2048]{1,0:T(8,128)(2,1)S(1)}, bf16[64,2048]{1,0:T(8,128)(2,1)S(1)}, u32[]{:S(2)}, u32[]{:S(2)}) collective-permute-start(bf16[64,2048]{1,0:T(8,128)(2,1)S(1)} %get-tuple-element.480.refs_0_), channel_id=1, source_target_pairs={{0,2},{1,3},{2,0},{3,1},{4,6},{5,7},{6,4},{7,5},{8,10},{9,11},{10,... | collective-permute-start | bytes 786440 | tf_op jit(solution)/shard_map/ppermute | solution.py:27
  108.1 25.6 %collective-permute-start.63 = (bf16[64,4096]{1,0:T(8,128)(2,1)S(1)}, bf16[64,4096]{1,0:T(8,128)(2,1)S(1)}, u32[]{:S(2)}, u32[]{:S(2)}) collective-permute-start(bf16[64,4096]{1,0:T(8,128)(2,1)S(1)} %get-tuple-element.507.refs_0_), channel_id=1, source_target_pairs={{0,2},{1,3},{2,0},{3,1},{4,6},{5,7},{6,4},{7,5},{8,10},{9,11},{10,... | collective-permute-start | bytes 1572872 | tf_op jit(solution)/shard_map/ppermute | solution.py:27
  112.4 4.9 %collective-permute-start.51 = (bf16[64,576]{1,0:T(8,128)(2,1)S(1)}, bf16[64,576]{1,0:T(8,128)(2,1)S(1)}, u32[]{:S(2)}, u32[]{:S(2)}) collective-permute-start(bf16[64,576]{1,0:T(8,128)(2,1)S(1)} %get-tuple-element.479.refs_0_), channel_id=1, source_target_pairs={{0,4},{4,0},{8,12},{12,8},{1,5},{5,1},{9,13},{13,9},{2,6},{6,2},{1... | collective-permute-start | bytes 221192 | tf_op jit(solution)/shard_map/ppermute | solution.py:27
  117.3 6.7 %collective-permute-start.62 = (bf16[64,576]{1,0:T(8,128)(2,1)S(1)}, bf16[64,576]{1,0:T(8,128)(2,1)S(1)}, u32[]{:S(2)}, u32[]{:S(2)}) collective-permute-start(bf16[64,576]{1,0:T(8,128)(2,1)S(1)} %get-tuple-element.503.refs_0_), channel_id=1, source_target_pairs={{0,8},{4,12},{8,0},{12,4},{1,9},{5,13},{9,1},{13,5},{2,10},{6,14},... | collective-permute-start | bytes 221192 | tf_op jit(solution)/shard_map/ppermute | solution.py:27
  135.8 16.0 %collective-permute-start.82 = (bf16[64,2048]{1,0:T(8,128)(2,1)S(1)}, bf16[64,2048]{1,0:T(8,128)(2,1)S(1)}, u32[]{:S(2)}, u32[]{:S(2)}) collective-permute-start(bf16[64,2048]{1,0:T(8,128)(2,1)S(1)} %get-tuple-element.552.refs_3_), channel_id=1, source_target_pairs={{0,2},{1,3},{2,0},{3,1},{4,6},{5,7},{6,4},{7,5},{8,10},{9,11},{10,... | collective-permute-start | bytes 786440 | tf_op jit(solution)/shard_map/ppermute | solution.py:27
  141.3 4.5 %collective-permute-start.80 = (bf16[64,576]{1,0:T(8,128)(2,1)S(1)}, bf16[64,576]{1,0:T(8,128)(2,1)S(1)}, u32[]{:S(2)}, u32[]{:S(2)}) collective-permute-start(bf16[64,576]{1,0:T(8,128)(2,1)S(1)} %get-tuple-element.545.refs_0_), channel_id=1, source_target_pairs={{0,4},{4,0},{8,12},{12,8},{1,5},{5,1},{9,13},{13,9},{2,6},{6,2},{1... | collective-permute-start | bytes 221192 | tf_op jit(solution)/shard_map/ppermute | solution.py:27
  145.8 6.0 %collective-permute-start.81 = (bf16[64,576]{1,0:T(8,128)(2,1)S(1)}, bf16[64,576]{1,0:T(8,128)(2,1)S(1)}, u32[]{:S(2)}, u32[]{:S(2)}) collective-permute-start(bf16[64,576]{1,0:T(8,128)(2,1)S(1)} %get-tuple-element.548.refs_0_), channel_id=1, source_target_pairs={{0,8},{4,12},{8,0},{12,4},{1,9},{5,13},{9,1},{13,5},{2,10},{6,14},... | collective-permute-start | bytes 221192 | tf_op jit(solution)/shard_map/ppermute | solution.py:27
  154.8 4.0 %collective-permute-start.83 = (bf16[16,4096]{1,0:T(8,128)(2,1)S(1)}, bf16[16,4096]{1,0:T(8,128)(2,1)S(1)}, u32[]{:S(2)}, u32[]{:S(2)}) collective-permute-start(bf16[16,4096]{1,0:T(8,128)(2,1)S(1)} %get-tuple-element.558), channel_id=1, source_target_pairs={{0,1},{1,0},{2,3},{3,2},{4,5},{5,4},{6,7},{7,6},{8,9},{9,8},{10,11... | collective-permute-start | bytes 393224 | tf_op jit(solution)/shard_map/ppermute | solution.py:27
  155.9 35.0 %collective-permute-start.96 = (bf16[64,4096]{1,0:T(8,128)(2,1)S(1)}, bf16[64,4096]{1,0:T(8,128)(2,1)S(1)}, u32[]{:S(2)}, u32[]{:S(2)}) collective-permute-start(bf16[64,4096]{1,0:T(8,128)(2,1)S(1)} %get-tuple-element.594.refs_3_), channel_id=1, source_target_pairs={{0,2},{1,3},{2,0},{3,1},{4,6},{5,7},{6,4},{7,5},{8,10},{9,11},{10,... | collective-permute-start | bytes 1572872 | tf_op jit(solution)/shard_map/ppermute | solution.py:27
  159.0 33.5 %collective-permute-start.111 = (bf16[64,4096]{1,0:T(8,128)(2,1)S(1)}, bf16[64,4096]{1,0:T(8,128)(2,1)S(1)}, u32[]{:S(2)}, u32[]{:S(2)}) collective-permute-start(bf16[64,4096]{1,0:T(8,128)(2,1)S(1)} %get-tuple-element.622.refs_3_), channel_id=1, source_target_pairs={{0,2},{1,3},{2,0},{3,1},{4,6},{5,7},{6,4},{7,5},{8,10},{9,11},{10,... | collective-permute-start | bytes 1572872 | tf_op jit(solution)/shard_map/ppermute | solution.py:27
  159.9 27.6 %collective-permute-start.95 = (bf16[64,2048]{1,0:T(8,128)(2,1)S(1)}, bf16[64,2048]{1,0:T(8,128)(2,1)S(1)}, u32[]{:S(2)}, u32[]{:S(2)}) collective-permute-start(bf16[64,2048]{1,0:T(8,128)(2,1)S(1)} %get-tuple-element.588.refs_3_), channel_id=1, source_target_pairs={{0,2},{1,3},{2,0},{3,1},{4,6},{5,7},{6,4},{7,5},{8,10},{9,11},{10,... | collective-permute-start | bytes 786440 | tf_op jit(solution)/shard_map/ppermute | solution.py:27
  165.9 42.0 %collective-permute-start.106 = (bf16[64,2048]{1,0:T(8,128)(2,1)S(1)}, bf16[64,2048]{1,0:T(8,128)(2,1)S(1)}, u32[]{:S(2)}, u32[]{:S(2)}) collective-permute-start(bf16[64,2048]{1,0:T(8,128)(2,1)S(1)} %get-tuple-element.616.refs_3_), channel_id=1, source_target_pairs={{0,2},{1,3},{2,0},{3,1},{4,6},{5,7},{6,4},{7,5},{8,10},{9,11},{10,... | collective-permute-start | bytes 786440 | tf_op jit(solution)/shard_map/ppermute | solution.py:27
  191.8 15.0 %collective-permute-start.107 = (bf16[16,4096]{1,0:T(8,128)(2,1)S(1)}, bf16[16,4096]{1,0:T(8,128)(2,1)S(1)}, u32[]{:S(2)}, u32[]{:S(2)}) collective-permute-start(bf16[16,4096]{1,0:T(8,128)(2,1)S(1)} %get-tuple-element.617), channel_id=1, source_target_pairs={{0,1},{1,0},{2,3},{3,2},{4,5},{5,4},{6,7},{7,6},{8,9},{9,8},{10,11... | collective-permute-start | bytes 393224 | tf_op jit(solution)/shard_map/ppermute | solution.py:27
  191.9 15.1 %collective-permute-start.108 = (bf16[16,4096]{1,0:T(8,128)(2,1)S(1)}, bf16[16,4096]{1,0:T(8,128)(2,1)S(1)}, u32[]{:S(2)}, u32[]{:S(2)}) collective-permute-start(bf16[16,4096]{1,0:T(8,128)(2,1)S(1)} %get-tuple-element.618), channel_id=1, source_target_pairs={{0,1},{1,0},{2,3},{3,2},{4,5},{5,4},{6,7},{7,6},{8,9},{9,8},{10,11... | collective-permute-start | bytes 393224 | tf_op jit(solution)/shard_map/ppermute | solution.py:27
  192.4 15.0 %collective-permute-start.109 = (bf16[16,4096]{1,0:T(8,128)(2,1)S(1)}, bf16[16,4096]{1,0:T(8,128)(2,1)S(1)}, u32[]{:S(2)}, u32[]{:S(2)}) collective-permute-start(bf16[16,4096]{1,0:T(8,128)(2,1)S(1)} %get-tuple-element.619), channel_id=1, source_target_pairs={{0,1},{1,0},{2,3},{3,2},{4,5},{5,4},{6,7},{7,6},{8,9},{9,8},{10,11... | collective-permute-start | bytes 393224 | tf_op jit(solution)/shard_map/ppermute | solution.py:27
  192.4 15.0 %collective-permute-start.110 = (bf16[16,4096]{1,0:T(8,128)(2,1)S(1)}, bf16[16,4096]{1,0:T(8,128)(2,1)S(1)}, u32[]{:S(2)}, u32[]{:S(2)}) collective-permute-start(bf16[16,4096]{1,0:T(8,128)(2,1)S(1)} %get-tuple-element.620), channel_id=1, source_target_pairs={{0,1},{1,0},{2,3},{3,2},{4,5},{5,4},{6,7},{7,6},{8,9},{9,8},{10,11... | collective-permute-start | bytes 393224 | tf_op jit(solution)/shard_map/ppermute | solution.py:27
  207.9 14.1 %collective-permute-start.101 = (bf16[64,2048]{1,0:T(8,128)(2,1)S(1)}, bf16[64,2048]{1,0:T(8,128)(2,1)S(1)}, u32[]{:S(2)}, u32[]{:S(2)}) collective-permute-start(bf16[64,2048]{1,0:T(8,128)(2,1)S(1)} %get-tuple-element.610.refs_3_), channel_id=1, source_target_pairs={{0,2},{1,3},{2,0},{3,1},{4,6},{5,7},{6,4},{7,5},{8,10},{9,11},{10,... | collective-permute-start | bytes 786440 | tf_op jit(solution)/shard_map/ppermute | solution.py:27
  209.6 7.0 %collective-permute-start.102 = (bf16[16,2048]{1,0:T(8,128)(2,1)S(1)}, bf16[16,2048]{1,0:T(8,128)(2,1)S(1)}, u32[]{:S(2)}, u32[]{:S(2)}) collective-permute-start(bf16[16,2048]{1,0:T(8,128)(2,1)S(1)} %get-tuple-element.611), channel_id=1, source_target_pairs={{0,1},{1,0},{2,3},{3,2},{4,5},{5,4},{6,7},{7,6},{8,9},{9,8},{10,11... | collective-permute-start | bytes 196616 | tf_op jit(solution)/shard_map/ppermute | solution.py:27
  209.6 7.1 %collective-permute-start.103 = (bf16[16,2048]{1,0:T(8,128)(2,1)S(1)}, bf16[16,2048]{1,0:T(8,128)(2,1)S(1)}, u32[]{:S(2)}, u32[]{:S(2)}) collective-permute-start(bf16[16,2048]{1,0:T(8,128)(2,1)S(1)} %get-tuple-element.612), channel_id=1, source_target_pairs={{0,1},{1,0},{2,3},{3,2},{4,5},{5,4},{6,7},{7,6},{8,9},{9,8},{10,11... | collective-permute-start | bytes 196616 | tf_op jit(solution)/shard_map/ppermute | solution.py:27
  210.1 7.0 %collective-permute-start.104 = (bf16[16,2048]{1,0:T(8,128)(2,1)S(1)}, bf16[16,2048]{1,0:T(8,128)(2,1)S(1)}, u32[]{:S(2)}, u32[]{:S(2)}) collective-permute-start(bf16[16,2048]{1,0:T(8,128)(2,1)S(1)} %get-tuple-element.613), channel_id=1, source_target_pairs={{0,1},{1,0},{2,3},{3,2},{4,5},{5,4},{6,7},{7,6},{8,9},{9,8},{10,11... | collective-permute-start | bytes 196616 | tf_op jit(solution)/shard_map/ppermute | solution.py:27
  210.1 7.1 %collective-permute-start.105 = (bf16[16,2048]{1,0:T(8,128)(2,1)S(1)}, bf16[16,2048]{1,0:T(8,128)(2,1)S(1)}, u32[]{:S(2)}, u32[]{:S(2)}) collective-permute-start(bf16[16,2048]{1,0:T(8,128)(2,1)S(1)} %get-tuple-element.614), channel_id=1, source_target_pairs={{0,1},{1,0},{2,3},{3,2},{4,5},{5,4},{6,7},{7,6},{8,9},{9,8},{10,11... | collective-permute-start | bytes 196616 | tf_op jit(solution)/shard_map/ppermute | solution.py:27
  217.9 4.7 %collective-permute-start.100 = (bf16[16,2048]{1,0:T(8,128)(2,1)S(1)}, bf16[16,2048]{1,0:T(8,128)(2,1)S(1)}, u32[]{:S(2)}, u32[]{:S(2)}) collective-permute-start(bf16[16,2048]{1,0:T(8,128)(2,1)S(1)} %get-tuple-element.608), channel_id=1, source_target_pairs={{0,1},{1,0},{2,3},{3,2},{4,5},{5,4},{6,7},{7,6},{8,9},{9,8},{10,11... | collective-permute-start | bytes 196616 | tf_op jit(solution)/shard_map/ppermute | solution.py:27
  218.0 4.9 %collective-permute-start.97 = (bf16[16,2048]{1,0:T(8,128)(2,1)S(1)}, bf16[16,2048]{1,0:T(8,128)(2,1)S(1)}, u32[]{:S(2)}, u32[]{:S(2)}) collective-permute-start(bf16[16,2048]{1,0:T(8,128)(2,1)S(1)} %get-tuple-element.605), channel_id=1, source_target_pairs={{0,1},{1,0},{2,3},{3,2},{4,5},{5,4},{6,7},{7,6},{8,9},{9,8},{10,11... | collective-permute-start | bytes 196616 | tf_op jit(solution)/shard_map/ppermute | solution.py:27
  218.4 4.7 %collective-permute-start.98 = (bf16[16,2048]{1,0:T(8,128)(2,1)S(1)}, bf16[16,2048]{1,0:T(8,128)(2,1)S(1)}, u32[]{:S(2)}, u32[]{:S(2)}) collective-permute-start(bf16[16,2048]{1,0:T(8,128)(2,1)S(1)} %get-tuple-element.606), channel_id=1, source_target_pairs={{0,1},{1,0},{2,3},{3,2},{4,5},{5,4},{6,7},{7,6},{8,9},{9,8},{10,11... | collective-permute-start | bytes 196616 | tf_op jit(solution)/shard_map/ppermute | solution.py:27
  218.5 4.9 %collective-permute-start.99 = (bf16[16,2048]{1,0:T(8,128)(2,1)S(1)}, bf16[16,2048]{1,0:T(8,128)(2,1)S(1)}, u32[]{:S(2)}, u32[]{:S(2)}) collective-permute-start(bf16[16,2048]{1,0:T(8,128)(2,1)S(1)} %get-tuple-element.607), channel_id=1, source_target_pairs={{0,1},{1,0},{2,3},{3,2},{4,5},{5,4},{6,7},{7,6},{8,9},{9,8},{10,11... | collective-permute-start | bytes 196616 | tf_op jit(solution)/shard_map/ppermute | solution.py:27
  (119 other events, 494.5 us)

commit v2 on v1

v2 whole, which is shorter than its diff:
```python
import math

import jax
import jax.numpy as jnp
from jax import lax
from jax.experimental import pallas as pl
from jax.experimental.pallas import tpu as pltpu
from jax.sharding import PartitionSpec as P

sparsity_cost = 0.1
sharpness = 8.0
weight_rate = 2.0
enc_bias_rate = 0.01
dec_bias_rate = 0.002

BF16, F32 = jnp.bfloat16, jnp.float32
MIB = 2 ** 20
IN_VMEM = pl.BlockSpec(memory_space=pltpu.VMEM)
UNTOUCHED = pl.BlockSpec(memory_space=pl.ANY)


def dot(a, b, over):
    return lax.dot_general(a, b, (over, ((), ())), preferred_element_type=F32)


def flip(value, axis, size, bit):
    return lax.ppermute(value, axis, [(i, i ^ bit) for i in range(size)])


SENT_PARTS = 2


def stacked(refs):
    return jnp.concatenate([ref[...] for ref in refs], axis=0)


def spread(value, refs):
    rows = refs[0].shape[0]
    for i, ref in enumerate(refs):
        ref[...] = value[i * rows:(i + 1) * rows]


class Cut:
    def __init__(self, half, start, width):
        self.half, self.start, self.width = half, start, width
        self.step = math.gcd(math.gcd(half, start), math.gcd(width, 4096))
        while self.step > 2048:
            self.step //= 2
        self.steps = width // self.step
        self.grid = 2 * self.steps

    def first(self, rows):
        return pl.BlockSpec((rows, self.step), lambda j, side: (0, jnp.minimum(j, self.steps - 1)))

    def second(self, rows):
        return pl.BlockSpec((rows, self.step), lambda j, side: (0, jnp.maximum(j - self.steps, 0)))

    def place(self, j, side):
        late = jnp.where(j < self.steps, 0, 1)
        half = jnp.where(j < self.steps, 1 - side[0], side[0])
        return (half * self.half + self.start) // self.step + j - late * self.steps

    def whole(self, rows):
        return pl.BlockSpec((rows, self.step), lambda j, side: (0, self.place(j, side)))

    def columns(self):
        return pl.ds(pl.multiple_of(pl.program_id(0) * self.step, self.step), self.step)

    def pick(self, first_refs, second_ref):
        return jnp.where(pl.program_id(0) < self.steps, stacked(first_refs), second_ref[...])


def cuts_of(half, shares):
    unit = half // sum(shares)
    if unit * sum(shares) != half or unit % 128:
        return [Cut(half, 0, half)]
    cuts, start = [], 0
    for share in shares:
        cuts.append(Cut(half, start, share * unit))
        start += share * unit
    return cuts


def shape(*dims, dtype=BF16):
    return jax.ShapeDtypeStruct(dims, dtype)


class Order:
    def __init__(self, side):
        self.side = side
        self.thread = jnp.zeros((8, 128), F32)
        self.kept = {}

    def call(self, kernel, grid, operands, in_specs, out_specs, out_shape, use=(), aliases=None, vmem=6, scratch=(),
             bring=None):
        names, bring = list(self.kept), bring or {}
        n_in, n_out, n_kept, n_new = len(operands), len(out_shape), len(names), len(bring)
        cuts = [cut for _, cut in bring.values()]

        def within(side_ref, *refs):
            ins, refs = refs[:n_in], refs[n_in:]
            weights, refs = dict(zip(names, refs[:n_kept])), refs[n_kept + 1:]
            sources, refs = refs[:n_new], refs[n_new:]
            outs, refs = refs[:n_out], refs[n_out + n_kept + 1:]
            targets, refs = refs[:n_new], refs[n_new:]

            def copies():
                made = []
                for source, target, cut in zip(sources, targets, cuts):
                    count = math.gcd(source.shape[0] // 16, 4)
                    rows = source.shape[0] // count
                    for half in range(1 if cut is None else 2):
                        for i in range(count):
                            start, end = source.at[pl.ds(i * rows, rows)], target.at[pl.ds(i * rows, rows)]
                            if cut is not None:
                                first = pl.multiple_of(cut.place(half * cut.steps, side_ref) * cut.step, cut.step)
                                start = source.at[pl.ds(i * rows, rows), pl.ds(first, cut.width)]
                                end = target.at[pl.ds(i * rows, rows), pl.ds(half * cut.width, cut.width)]
                            made.append(pltpu.make_async_copy(start, end, refs[-1].at[len(made)]))
                return made

            step = pl.program_id(0)

            @pl.when(step == 0)
            def _():
                for copy in copies():
                    copy.start()

            kernel(side_ref, *ins, *[weights[name] for name in use], *outs, *(refs[:-1] if bring else refs))

            @pl.when(step == grid - 1)
            def _():
                for copy in copies():
                    copy.wait()

        kept = [pltpu.with_memory_space_constraint(self.kept[name], pltpu.VMEM) for name in names]
        new = [pltpu.with_memory_space_constraint(weight, pltpu.HBM) for weight, _ in bring.values()]
        new_out = [
            pltpu.VMEM(weight.shape if cut is None else (weight.shape[0], 2 * cut.width), weight.dtype)
            for weight, cut in bring.values()
        ]
        joined = dict(aliases or {})
        joined.update({1 + n_in + i: n_out + i for i in range(n_kept + 1)})
        results = pl.pallas_call(
            within,
            grid_spec=pltpu.PrefetchScalarGridSpec(
                num_scalar_prefetch=1,
                grid=(grid,),
                in_specs=in_specs + [IN_VMEM] * n_kept + [UNTOUCHED] + [pl.BlockSpec(memory_space=pltpu.HBM)] * n_new,
                out_specs=out_specs + [IN_VMEM] * n_kept + [UNTOUCHED] + [IN_VMEM] * n_new,
                scratch_shapes=list(scratch) + ([pltpu.SemaphoreType.DMA((8 * n_new,))] if bring else []),
            ),
            out_shape=out_shape
            + [pltpu.VMEM(k.shape, k.dtype) for k in kept]
            + [shape(8, 128, dtype=F32)]
            + new_out,
            input_output_aliases=joined,
            compiler_params=pltpu.CompilerParams(vmem_limit_bytes=vmem * MIB),
            cost_estimate=pl.CostEstimate(flops=1, bytes_accessed=1, transcendentals=0),
        )(self.side, *operands, *kept, self.thread, *new)
        self.kept = dict(zip(names, results[n_out:]))
        self.thread = results[n_out + n_kept]
        self.kept.update(zip(bring, results[n_out + n_kept + 1:]))
        return list(results[:n_out])

    def keep(self, **weights):
        self.bring({name: (weight, None) for name, weight in weights.items()})

    def bring(self, new):
        self.call(lambda *refs: None, 1, (), [], [], [], vmem=1, bring=new)

    def drop(self, *names):
        for name in names:
            del self.kept[name]


def project(run, cut, tokens, weight, bring=None):
    count, width = tokens.shape

    def kernel(side_ref, tokens_ref, weight_ref, *refs):
        product = dot(tokens_ref[...], weight_ref[:, cut.columns()], ((1,), (0,))).astype(BF16)
        late = pl.program_id(0) >= cut.steps

        @pl.when(jnp.logical_not(late))
        def _():
            spread(product, refs[:-1])

        @pl.when(late)
        def _():
            refs[-1][...] = product

    each = count // SENT_PARTS
    *for_other, mine = run.call(
        kernel, cut.grid, (tokens,), [IN_VMEM], [cut.first(each)] * SENT_PARTS + [cut.second(count)],
        [shape(each, cut.width)] * SENT_PARTS + [shape(count, cut.width)], use=[weight], bring=bring,
    )
    return for_other, mine


def added(run, mine, received, dtype=BF16):
    def kernel(side_ref, mine_ref, received_ref, out_ref):
        out_ref[...] = (mine_ref[...].astype(F32) + received_ref[...].astype(F32)).astype(dtype)

    return run.call(
        kernel, 1, (mine, received), [IN_VMEM] * 2, [IN_VMEM], [shape(*mine.shape, dtype=dtype)],
    )[0]


def added_parts(run, pairs):
    count, width = pairs[0][0].shape[0], sum(mine.shape[1] for mine, _ in pairs)

    def kernel(side_ref, *refs):
        *refs, out_ref = refs
        first = 0
        for mine, received in pairs:
            (mine_ref, *received_refs), refs = refs[:1 + len(received)], refs[1 + len(received):]
            total = mine_ref[...].astype(F32) + stacked(received_refs).astype(F32)
            out_ref[:, first:first + mine.shape[1]] = total.astype(BF16)
            first += mine.shape[1]

    operands = [ref for mine, received in pairs for ref in (mine, *received)]
    return run.call(kernel, 1, operands, [IN_VMEM] * len(operands), [IN_VMEM], [shape(count, width)])[0]


def token_part(run, activations_t, part, parts):
    width, count = activations_t.shape
    each = count // parts

    def kernel(side_ref, activations_ref, out_ref):
        out_ref[...] = activations_ref[...].T[part * each:(part + 1) * each]

    return run.call(kernel, 1, (activations_t,), [IN_VMEM], [IN_VMEM], [shape(each, width)])[0]


def handed_on(run, arrays):
    return run.call(
        lambda *refs: None, 1, arrays, [UNTOUCHED] * len(arrays), [UNTOUCHED] * len(arrays),
        [shape(*a.shape, dtype=a.dtype) for a in arrays], aliases={1 + i: i for i in range(len(arrays))},
    )


def turned(run, parts):
    count, width = parts[0].shape

    def kernel(side_ref, first_ref, second_ref, out_ref):
        out_ref[...] = jnp.concatenate([first_ref[...], second_ref[...]], axis=0).T

    return run.call(
        kernel, 1, tuple(parts), [IN_VMEM] * 2, [IN_VMEM], [shape(width, 2 * count)]
    )[0]


def residual_grad(run, mine, received, bias, features, dec_scale):
    def kernel(side_ref, mine_ref, received_ref, bias_ref, features_ref, out_ref):
        rebuilt = dec_scale * (mine_ref[...].astype(F32) + received_ref[...].astype(F32)) + bias_ref[...]
        out_ref[...] = (2.0 * (rebuilt - features_ref[...].astype(F32))).astype(BF16)

    return run.call(
        kernel, 1, (mine, received, bias, features), [IN_VMEM] * 4, [IN_VMEM], [shape(*features.shape)],
    )[0]


def update_bias(run, bias, parts):
    def kernel(side_ref, bias_ref, first_ref, second_ref, out_ref):
        both = jnp.concatenate([first_ref[...], second_ref[...]], axis=0).astype(F32)
        out_ref[...] = (bias_ref[...] - dec_bias_rate * jnp.sum(both, axis=0, keepdims=True)).reshape(out_ref.shape)

    return run.call(
        kernel, 1, (bias,) + tuple(parts), [IN_VMEM] * 3, [IN_VMEM], [shape(bias.shape[1], dtype=F32)],
    )[0]


def gate_or_up(run, own, tokens, hidden, received=()):
    count = tokens.shape[0]
    n_out = 1 if own else SENT_PARTS

    def kernel(side_ref, tokens_ref, *refs):
        gate_ref, up_ref, *out_refs = refs[len(received):]
        for value, weight_ref in enumerate((gate_ref, up_ref) if own else (up_ref, gate_ref)):
            @pl.when(side_ref[0] == value)
            def _():
                total = dot(tokens_ref[...], weight_ref[...], ((1,), (0,)))
                if received:
                    total = total + stacked(refs[:len(received)]).astype(F32)
                spread(total.astype(BF16), out_refs)

    return run.call(
        kernel, 1, (tokens, *received), [IN_VMEM] * (1 + len(received)), [IN_VMEM] * n_out,
        [shape(count // n_out, hidden)] * n_out, use=["gate", "up"],
    )


def summed_term(run, mine, received):
    count, hidden = mine.shape

    def kernel(side_ref, mine_ref, received_ref, out_ref, *sent_refs):
        total = mine_ref[...].astype(F32) + received_ref[...].astype(F32)
        out_ref[...] = total
        spread(total, sent_refs)

    total, *sent = run.call(
        kernel, 1, (mine, received), [IN_VMEM] * 2, [IN_VMEM] * (1 + SENT_PARTS),
        [shape(count, hidden, dtype=F32)] + [shape(count // SENT_PARTS, hidden, dtype=F32)] * SENT_PARTS,
    )
    return total, sent


def layer_output(run, own_term, other_parts, width):
    count, hidden = own_term.shape

    def kernel(side_ref, own_ref, *refs):
        *other_refs, down_ref, out_ref = refs
        own_value, other_value = own_ref[...], stacked(other_refs)
        for value, (gate, up) in enumerate(((own_value, other_value), (other_value, own_value))):
            @pl.when(side_ref[0] == value)
            def _():
                hidden = (jax.nn.gelu(gate, approximate=True) * up).astype(BF16)
                out_ref[...] = dot(hidden, down_ref[...], ((1,), (1,))).astype(BF16)

    return run.call(
        kernel, 1, (own_term, *other_parts), [IN_VMEM] * (1 + len(other_parts)), [IN_VMEM], [shape(count, width)],
        use=["down"],
    )[0]


def pre_of(mine, other, bias, enc_scale):
    return enc_scale * (mine.astype(F32) + other.astype(F32)) + bias


def over_own(cut):
    def local(rows, first=0):
        return pl.BlockSpec((rows, cut.step), lambda j, side: (0, first // cut.step + j))

    def whole(rows):
        return pl.BlockSpec((rows, cut.step), lambda j, side: (0, cut.place(j + cut.steps, side)))

    return local, whole


def latents_of(run, cut, mine, other, first, bias, enc_scale):
    count = mine.shape[0]
    local, whole = over_own(cut)

    def kernel(side_ref, mine_ref, other_ref, bias_ref, latents_ref, *sent_refs):
        scaled = sharpness * pre_of(mine_ref[...], other_ref[...], bias_ref[...], enc_scale)
        soft = jnp.maximum(scaled, 0.0) + jnp.log1p(jnp.exp(-jnp.abs(scaled)))
        latents = (soft * (1.0 / sharpness)).astype(BF16)
        latents_ref[...] = latents
        spread(latents, sent_refs)

    each = count // SENT_PARTS
    latents, *sent = run.call(
        kernel, cut.steps, (mine, other, bias), [local(count, first), local(count, first), whole(1)],
        [local(count)] + [local(each)] * SENT_PARTS,
        [shape(count, cut.width)] + [shape(each, cut.width)] * SENT_PARTS,
    )
    return latents, sent


def decode(run, cut, latents_other, latents_own, weight, width, partial, last, bring=None):
    count = latents_own.shape[0]

    n_first = len(latents_other)

    def kernel(side_ref, *refs):
        first_refs, second_ref = refs[:n_first], refs[n_first]
        weight_ref, sum_ref, total = refs[-3:]

        @pl.when(pl.program_id(0) == 0)
        def _():
            total[...] = jnp.zeros_like(total) if partial is None else refs[n_first + 1][...]

        total[...] += dot(
            cut.pick(first_refs, second_ref), weight_ref[:, cut.columns()], ((1,), (1,))
        )

        @pl.when(pl.program_id(0) == cut.grid - 1)
        def _():
            sum_ref[...] = total[...].astype(sum_ref.dtype)

    more = () if partial is None else (partial,)
    return run.call(
        kernel, cut.grid, (*latents_other, latents_own) + more,
        [cut.first(count // n_first)] * n_first + [cut.second(count)] + [IN_VMEM] * len(more),
        [pl.BlockSpec((count, width), lambda j, side: (0, 0))],
        [shape(count, width, dtype=BF16 if last else F32)],
        use=[weight], scratch=[pltpu.VMEM((count, width), F32)], bring=bring,
    )[0]


def latent_grad(run, cut, mine, other, first, bias, back, back_other, back_first, enc_scale, dec_scale, sent_parts):
    count = mine.shape[0]
    local, whole = over_own(cut)

    def kernel(side_ref, mine_ref, other_ref, bias_ref, back_ref, back_other_ref, grad_ref, *sent_refs):
        scaled = sharpness * pre_of(mine_ref[...], other_ref[...], bias_ref[...], enc_scale)
        total = back_ref[...].astype(F32) + back_other_ref[...].astype(F32)
        grad = (jax.nn.sigmoid(scaled) * (dec_scale * total + sparsity_cost)).astype(BF16)
        grad_ref[...] = grad
        spread(grad, sent_refs)

    each = count // sent_parts
    grad, *sent = run.call(
        kernel, cut.steps, (mine, other, bias, back, back_other),
        [local(count, first), local(count, first), whole(1)] + [local(count, back_first)] * 2,
        [local(count)] + [local(each)] * sent_parts,
        [shape(count, cut.width)] + [shape(each, cut.width)] * sent_parts,
    )
    return grad, sent


def update(run, cut, left, rights, weight, scale, target, latents, bias=None, bring=None):
    width = left.shape[0]
    count = rights[0][1].shape[0]
    given = () if bias is None else (bias,)
    more = () if target is None else tuple(target)
    n_out = 1 + len(given)

    def kernel(side_ref, left_ref, *refs):
        weight_ref, outs = refs[-1 - n_out], refs[-n_out:]
        picked, used = [], 0
        for first, _ in rights:
            picked.append(cut.pick(refs[used:used + len(first)], refs[used + len(first)]))
            used += len(first) + 1
        both = jnp.concatenate(picked, axis=0)
        step = (weight_rate * scale) * dot(left_ref[...], both, ((1,), (0,)))
        outs[0][...] = (weight_ref[:, cut.columns()].astype(F32) - step).astype(BF16)
        if bias is not None:
            summed = jnp.sum(both.astype(F32), axis=0, keepdims=True)
            outs[1][...] = refs[used][...] - enc_bias_rate * summed

    operands, specs = [left], [IN_VMEM]
    for first, second in rights:
        operands += [*first, second]
        specs += [cut.first(count // len(first))] * len(first) + [cut.second(count)]
    return run.call(
        kernel, cut.grid, (*operands, *given, *more),
        specs + [cut.whole(1)] * len(given) + [UNTOUCHED] * len(more),
        [cut.whole(width)] + [cut.whole(1)] * len(given),
        [shape(width, latents)] + [shape(1, latents, dtype=F32)] * len(given),
        aliases={1 + len(operands) + len(given) + i: i for i in range(len(more))},
        use=[weight], vmem=14, bring=bring,
    )


def solution(mesh):
    n_rows, n_latent = mesh.shape["rows"], mesh.shape["latent"]
    row_bits = [1 << b for b in range(1, n_rows.bit_length() - 1)]
    latent_bits = [1 << b for b in range(n_latent.bit_length() - 1)]

    def beside(value):
        return flip(value, "rows", n_rows, 1)

    def across(run, value):
        for bit in row_bits[:-1]:
            value = added(run, value, flip(value, "rows", n_rows, bit))
        return value, flip(value, "rows", n_rows, row_bits[-1])

    def body(activations_in, gate_proj, up_proj, down_proj, enc_weight, enc_bias, dec_weight, dec_bias):
        width, local_latents = enc_weight.shape
        count = activations_in.shape[0] * activations_in.shape[1]
        enc_scale = (width * n_rows) ** -0.5
        dec_scale = (local_latents * n_latent) ** -0.5
        row = lax.axis_index("rows")
        core = row % 2
        own = core.astype(jnp.int32).reshape(1)

        parts = 2
        run = Order(own)
        turn = [(a * n_rows + b, b * n_rows + a) for a in range(n_latent) for b in range(n_rows)]
        activations_t = activations_in.reshape(count, activations_in.shape[2]).T

        def own_rows(part):
            piece = token_part(run, activations_t, part, parts)
            if n_rows == n_latent:
                return lax.ppermute(piece, ("latent", "rows"), turn)
            piece = lax.all_gather(piece, "latent", axis=1, tiled=True)
            return lax.dynamic_slice_in_dim(piece, row * width, width, 1)

        pieces = [own_rows(0)]
        bias, out_bias = handed_on(run, (enc_bias.reshape(1, local_latents), dec_bias.reshape(1, width)))
        cuts = cuts_of(local_latents // 2, (1, 1, 2))
        n_cuts = len(cuts)
        hidden = gate_proj.shape[1]
        early, late = [*range(n_cuts - 1)], n_cuts - 1
        last_order = [late, *early]
        dec_t = dec_weight.T

        def piece_of(name, i):
            return {(name, i): (enc_weight if name == "enc" else dec_t, cuts[i])}

        run.keep(gate=gate_proj, up=up_proj, down=down_proj.T)
        for i in range(n_cuts):
            run.bring(piece_of("enc", i))
        pieces.append(own_rows(1))
        chips = []
        for piece in pieces:
            received = [beside(part) for part in gate_or_up(run, False, piece, hidden)]
            chips.append(across(run, *gate_or_up(run, True, piece, hidden, received)))
        run.drop("gate", "up")

        def latent_terms(value, between):
            between = list(between)
            for bit in latent_bits:
                received = flip(value, "latent", n_latent, bit)
                if between:
                    between.pop(0)()
                if bit != latent_bits[-1]:
                    value = added(run, value, received)
            for rest in between:
                rest()
            return value, received

        layer_sums, layer_parts = [None] * parts, [None] * parts

        def open_layer(part):
            term, sent = summed_term(run, *chips[part])
            layer_sums[part] = (term, [beside(piece) for piece in sent])

        def close_layer(part):
            layer_parts[part] = layer_output(run, *layer_sums[part], width)

        open_layer(0)
        close_layer(0)
        def second_layer():
            open_layer(1)
            close_layer(1)

        layer_terms = latent_terms(layer_parts[0], [lambda: None, second_layer])
        run.drop("down")

        sums = [[None] * n_cuts for _ in range(parts)]
        backs = [[None] * n_cuts for _ in range(parts)]

        def project_start(part, i, tokens, weight, bring=None):
            for_other, mine = project(run, cuts[i], tokens, (weight, i), bring)
            return mine, [beside(piece) for piece in for_other]

        def project_end(part, which, totals):
            mine, theirs = across(run, added_parts(run, [held[part][i] for i in which]))
            first = 0
            for i in which:
                totals[part][i] = (mine, theirs, first)
                first += cuts[i].width

        latents_own = [[None] * n_cuts for _ in range(parts)]
        latents_other = [[None] * n_cuts for _ in range(parts)]
        partials = [None] * parts

        def open_latents(part, i):
            latents_own[part][i], sent = latents_of(run, cuts[i], *sums[part][i], bias, enc_scale)
            latents_other[part][i] = [beside(piece) for piece in sent]

        def add_decoded(part, i, bring=None):
            partials[part] = decode(
                run, cuts[i], latents_other[part][i], latents_own[part][i], ("dec", i), width, partials[part],
                i == n_cuts - 1, bring,
            )

        grads_own = [[None] * n_cuts for _ in range(parts)]
        grads_other = [[None] * n_cuts for _ in range(parts)]

        def open_grad(part, i):
            grads_own[part][i], sent = latent_grad(
                run, cuts[i], *sums[part][i], bias, *backs[part][i], enc_scale, dec_scale,
                2 if part else 2,
            )
            grads_other[part][i] = [beside(piece) for piece in sent]

        features, held = [added(run, *layer_terms)], [[None] * n_cuts for _ in range(parts)]

        def encode_first():
            for i in early:
                held[0][i] = project_start(0, i, features[0], "enc")
            if early:
                project_end(0, early, sums)
            held[0][late] = project_start(0, late, features[0], "enc", piece_of("dec", 0) if early else None)

        layer_terms = latent_terms(layer_parts[1], [lambda: None, encode_first])
        features.append(added(run, *layer_terms))
        project_end(0, [late], sums)
        for i in range(n_cuts):
            bring = piece_of("dec", i + 1) if i + 1 < late else piece_of("dec", late) if i == late else None
            held[1][i] = project_start(1, i, features[1], "enc", bring)
            run.drop(("enc", i))

        for i in early:
            open_latents(0, i)
        for i in early:
            if i == min(1, late - 1):
                project_end(1, early, sums)
            add_decoded(0, i)
        open_latents(0, late)
        project_end(1, [late], sums)
        add_decoded(0, late)

        def residual_of(part, between):
            terms = latent_terms(partials[part], between)
            return residual_grad(run, *terms, out_bias, features[part], dec_scale)

        residuals = [residual_of(0, [lambda i=i: open_latents(1, i) for i in early])]
        for i in range(n_cuts):
            held[0][i] = project_start(0, i, residuals[0], "dec")
        project_end(0, range(n_cuts), backs)
        open_latents(1, late)
        for i in range(n_cuts):
            add_decoded(1, i)
        residuals.append(residual_of(1, []))

        dec_new = enc_new = residual_t = features_t = None

        def write_dec(k):
            i = last_order[k]
            rights = [(latents_other[part][i], latents_own[part][i]) for part in range(parts)]
            new = update(
                run, cuts[i], residual_t, rights, ("dec", i), dec_scale, dec_new, local_latents,
                bring=piece_of("enc", last_order[k - 1]) if k else None,
            )
            run.drop(("dec", i))
            return new

        def write_enc(k):
            i = last_order[k]
            rights = [(grads_other[part][i], grads_own[part][i]) for part in range(parts)]
            new = update(
                run, cuts[i], features_t, rights, ("enc", i), enc_scale, enc_new, local_latents, bias,
                bring=piece_of("enc", last_order[-1]) if k == n_cuts - 2 else None,
            )
            run.drop(("enc", i))
            return new

        for i in last_order:
            held[1][i] = project_start(1, i, residuals[1], "dec")
        project_end(1, [late], backs)
        if early:
            project_end(1, early, backs)
        residual_t = turned(run, residuals)
        features_t = turned(run, features)
        for k in range(n_cuts):
            dec_new = write_dec(k)
            if k == 0:
                for i in last_order:
                    open_grad(0, i)
        out_bias_new = update_bias(run, out_bias, residuals)
        if n_cuts == 1:
            run.bring(piece_of("enc", late))
        open_grad(1, late)
        for k in range(n_cuts):
            if k == 1:
                for i in early:
                    open_grad(1, i)
            enc_new = write_enc(k)
        enc_new, bias_new = enc_new
        return enc_new, bias_new.reshape(local_latents), dec_new[0].T, out_bias_new

    return jax.shard_map(
        body,
        mesh=mesh,
        in_specs=(
            P("groups", None, "latent"),
            P("rows", "latent"),
            P("rows", "latent"),
            P("latent", "rows"),
            P(("groups", "rows"), "latent"),
            P(("groups", "latent")),
            P(("groups", "latent"), "rows"),
            P(("groups", "rows")),
        ),
        out_specs=(
            P(("groups", "rows"), "latent"),
            P(("groups", "latent")),
            P(("groups", "latent"), "rows"),
            P(("groups", "rows")),
        ),
        check_vma=False,
    )
```

time: 228 us -> 182 us (0.80)
  starting transfers between devices: 61.8 us -> 38.4 us
  waiting for transfers between devices: 68.3 us -> 47.1 us
    ppermute x122 -> x73, starting transfers between devices: 60.4 us -> 37.1 us  [flip(): return lax.ppermute(value, axis, [(i, i ^ bit) for i in range(size)])]
    ppermute x122 -> x73, waiting for transfers between devices: 68.3 us -> 47.1 us  [flip(): return lax.ppermute(value, axis, [(i, i ^ bit) for i in range(size)])]
    pallas_call x72 -> x69, Pallas kernels: 92.2 us -> 91.4 us  [call(): pl.pallas_call(within, grid_spec=pltpu.PrefetchScalarGridSpec(num_scalar_...]
  transfers between devices with their start and end apart: 124 -> 75, of which waited for: 37 -> 31; matrix products, arithmetic and copies ran while one was open for 0% -> 0% of each run, Pallas kernels for 36% -> 47%
where the time goes in v2:
time: 182 us
  Pallas kernels  91.4 us (50%)
  waiting for transfers between devices  47.1 us (26%)
  starting transfers between devices  38.4 us (21%)
  local copies, waits for them, and re-layouts  3.28 us (2%)
    pallas_call x69, Pallas kernels, call(): pl.pallas_call(within, grid_spec=pltpu.PrefetchScalarGridSpec(num_scalar_...  91.4 us
    ppermute x73, waiting for transfers between devices, flip(): return lax.ppermute(value, axis, [(i, i ^ bit) for i in range(size)])  47.1 us
    ppermute x73, starting transfers between devices, flip(): return lax.ppermute(value, axis, [(i, i ^ bit) for i in range(size)])  37.1 us
  transfers between devices with their start and end apart: 75, of which 31 were waited for; matrix products, arithmetic and copies ran while one was open for 0% of the time, Pallas kernels for 47%

profile of v2, /device:TPU:0, one launch (start us, length us, event | category | flops | bytes accessed | tf_op | source)
XLA Modules:
  0.0 181.8 jit_solution(6866133535329273798)
XLA Ops:
  3.8 2.3 %shard_map.113 = (f32[8,128]{1,0:T(8,128)S(1)}, bf16[576,1152]{1,0:T(8,128)(2,1)S(1)}, bf16[576,1152]{1,0:T(8,128)(2,1)S(1)}, bf16[576,1152]{1,0:T(8,128)(2,1)S(1)}) custom-call(s32[1]{0:T(128)} %bitcast.side_ref, f32[8,128]{1,0:T(8,128)S(1)} %get-tuple-element.406.refs_0_, bf16[576,1152]{1,0:T(8,128)(2,1)} %refs_1_.1, ...), custom_call_target="tpu_custom_call", output_to_operand_aliasing={{0}: (1, {})} | custom-call | flops 1 | bytes 1 | tf_op jit(solution)/shard_map/pallas_call | solution.py:144
  6.2 2.4 %shard_map.114 = (bf16[576,1152]{1,0:T(8,128)(2,1)S(1)}, bf16[576,1152]{1,0:T(8,128)(2,1)S(1)}, bf16[576,1152]{1,0:T(8,128)(2,1)S(1)}, f32[8,128]{1,0:T(8,128)S(1)}, bf16[576,4096]{1,0:T(8,128)(2,1)S(1)}) custom-call(s32[1]{0:T(128)} %bitcast.side_ref, ...), custom_call_target="tpu_custom_call", output_to_operand_aliasing={{0}: (1, {}), {1}: (2, {}), {2}: (3, {}), {3}: (4, {})} | custom-call | flops 1 | bytes 1 | tf_op jit(solution)/shard_map/pallas_call | solution.py:144
  8.6 2.4 %shard_map.115 = (bf16[576,1152]{1,0:T(8,128)(2,1)S(1)}, bf16[576,1152]{1,0:T(8,128)(2,1)S(1)}, bf16[576,1152]{1,0:T(8,128)(2,1)S(1)}, bf16[576,4096]{1,0:T(8,12...) custom-call(s32[1]{0:T(128)} %bitcast.side_ref, ...), custom_call_target="tpu_custom_call", output_to_operand_aliasing={{0}: (1, {}), {1}: (2, {}), {2}: (3, {}), {3}: (4, {}), {4}... | custom-call | flops 1 | bytes 1 | tf_op jit(solution)/shard_map/pallas_call | solution.py:144
  11.0 3.8 %shard_map.116 = (bf16[576,1152]{1,0:T(8,128)(2,1)S(1)}, bf16[576,1152]{1,0:T(8,128)(2,1)S(1)}, bf16[576,1152]{1,0:T(8,128)(2,1)S(1)}, bf16[576,4096]{1,0:T(8,12...) custom-call(s32[1]{0:T(128)} %bitcast.side_ref, ...), custom_call_target="tpu_custom_call", output_to_operand_aliasing={{0}: (1, {}), {1}: (2, {}), {2}: (3, {}), {3}: (4, {}), {4}... | custom-call | flops 1 | bytes 1 | tf_op jit(solution)/shard_map/pallas_call | solution.py:144
  15.4 4.4 %collective-permute-start.1 = (bf16[32,1152]{1,0:T(8,128)(2,1)S(1)}, bf16[32,1152]{1,0:T(8,128)(2,1)S(1)}, u32[]{:S(2)}, u32[]{:S(2)}) collective-permute-start(bf16[32,1152]{1,0:T(8,128)(2,1)S(1)} %get-tuple-element.436), channel_id=1, source_target_pairs={{0,1},{1,0},{2,3},{3,2},{4,5},{5,4},{6,7},{7,6},{8,9},{9,8},{10,11... | collective-permute-start | bytes 221192 | tf_op jit(solution)/shard_map/ppermute | solution.py:27
  21.5 4.9 %collective-permute-start.3 = (bf16[64,1152]{1,0:T(8,128)(2,1)S(1)}, bf16[64,1152]{1,0:T(8,128)(2,1)S(1)}, u32[]{:S(2)}, u32[]{:S(2)}) collective-permute-start(bf16[64,1152]{1,0:T(8,128)(2,1)S(1)} %get-tuple-element.445.refs_0_), channel_id=1, source_target_pairs={{0,2},{1,3},{2,0},{3,1},{4,6},{5,7},{6,4},{7,5},{8,10},{9,11},{10,... | collective-permute-start | bytes 442376 | tf_op jit(solution)/shard_map/ppermute | solution.py:27
  28.6 3.2 %collective-permute-done.3.refs_1_ = bf16[64,1152]{1,0:T(8,128)(2,1)S(1)} collective-permute-done((bf16[64,1152]{1,0:T(8,128)(2,1)S(1)}, bf16[64,1152]{1,0:T(8,128)(2,1)S(1)}, u32[]{:S(2)}, u32[]{:S(2)}) %collective-permute-start.3) | collective-permute-done | bytes 147488 | tf_op jit(solution)/shard_map/ppermute | solution.py:27
  32.5 2.6 %collective-permute-start.11 = (bf16[64,1152]{1,0:T(8,128)(2,1)S(1)}, bf16[64,1152]{1,0:T(8,128)(2,1)S(1)}, u32[]{:S(2)}, u32[]{:S(2)}) collective-permute-start(bf16[64,1152]{1,0:T(8,128)(2,1)S(1)} %get-tuple-element.483.refs_0_), channel_id=1, source_target_pairs={{0,2},{1,3},{2,0},{3,1},{4,6},{5,7},{6,4},{7,5},{8,10},{9,11},{10,... | collective-permute-start | bytes 442376 | tf_op jit(solution)/shard_map/ppermute | solution.py:27
  35.7 4.4 %collective-permute-done.9.refs_1_ = bf16[64,576]{1,0:T(8,128)(2,1)S(1)} collective-permute-done((bf16[64,576]{1,0:T(8,128)(2,1)S(1)}, bf16[64,576]{1,0:T(8,128)(2,1)S(1)}, u32[]{:S(2)}, u32[]{:S(2)}) %collective-permute-start.9) | collective-permute-done | bytes 73760 | tf_op jit(solution)/shard_map/ppermute | solution.py:27
  42.6 1.0 collective-permute-start.14
  43.6 3.8 %collective-permute-done.10.refs_1_ = bf16[64,576]{1,0:T(8,128)(2,1)S(1)} collective-permute-done((bf16[64,576]{1,0:T(8,128)(2,1)S(1)}, bf16[64,576]{1,0:T(8,128)(2,1)S(1)}, u32[]{:S(2)}, u32[]{:S(2)}) %collective-permute-start.10) | collective-permute-done | bytes 73760 | tf_op jit(solution)/shard_map/ppermute | solution.py:27
  47.5 1.5 collective-permute-done.14.refs_1_
  49.0 1.2 shard_map.129
  50.2 1.2 shard_map.130
  53.7 1.3 collective-permute-start.23
  55.1 2.9 %shard_map.132 = (bf16[32,4096]{1,0:T(8,128)(2,1)S(1)}, bf16[32,4096]{1,0:T(8,128)(2,1)S(1)}, bf16[64,4096]{1,0:T(8,128)(2,1)S(1)}, bf16[576,4096]{1,0:T(8,128)(...) custom-call(s32[1]{0:T(128)} %bitcast.side_ref, ...), custom_call_target="tpu_custom_call", output_to_operand_aliasing={{3}: (2, {}), {4}: (3, {}), {5}: (4, {}), {6}: (5, {})} | custom-call | flops 1 | bytes 1 | tf_op jit(solution)/shard_map/pallas_call | solution.py:144
  58.5 6.1 %collective-permute-done.15.refs_1_ = bf16[64,576]{1,0:T(8,128)(2,1)S(1)} collective-permute-done((bf16[64,576]{1,0:T(8,128)(2,1)S(1)}, bf16[64,576]{1,0:T(8,128)(2,1)S(1)}, u32[]{:S(2)}, u32[]{:S(2)}) %collective-permute-start.15) | collective-permute-done | bytes 73760 | tf_op jit(solution)/shard_map/ppermute | solution.py:27
  65.6 2.8 %shard_map.135 = (bf16[32,2048]{1,0:T(8,128)(2,1)S(1)}, bf16[32,2048]{1,0:T(8,128)(2,1)S(1)}, bf16[64,2048]{1,0:T(8,128)(2,1)S(1)}, bf16[576,4096]{1,0:T(8,128)(...) custom-call(s32[1]{0:T(128)} %bitcast.side_ref, ...), custom_call_target="tpu_custom_call", output_to_operand_aliasing={{3}: (2, {}), {4}: (3, {}), {5}: (4, {}), {6}: (5, {}), {7}... | custom-call | flops 1 | bytes 1 | tf_op jit(solution)/shard_map/pallas_call | solution.py:144
  68.5 1.2 shard_map.136
  69.8 4.3 %shard_map.137 = (bf16[32,4096]{1,0:T(8,128)(2,1)S(1)}, bf16[32,4096]{1,0:T(8,128)(2,1)S(1)}, bf16[64,4096]{1,0:T(8,128)(2,1)S(1)}, bf16[576,8192]{1,0:T(8,128)(...) custom-call(s32[1]{0:T(128)} %bitcast.side_ref, ...), custom_call_target="tpu_custom_call", output_to_operand_aliasing={{3}: (2, {}), {4}: (3, {}), {5}: (4, {}), {6}: (5, {})} | custom-call | flops 1 | bytes 1 | tf_op jit(solution)/shard_map/pallas_call | solution.py:144
  77.1 1.7 shard_map.140
  79.0 1.4 collective-permute-start.37
  81.7 1.7 shard_map.142
  83.5 1.0 shard_map.143
  86.4 3.6 %shard_map.145 = (bf16[64,576]{1,0:T(8,128)(2,1)S(1)}, bf16[576,4096]{1,0:T(8,128)(2,1)S(1)}, bf16[576,4096]{1,0:T(8,128)(2,1)S(1)}, bf16[576,8192]{1,0:T(8,128)(2,1)S(1)}, f32[8,128]{1,0:T(8,128)S(1)}) custom-call(s32[1]{0:T(128)} %bitcast.side_ref, ...), custom_call_target="tpu_custom_call", output_to_operand_aliasing={{1}: (5, {}), {2}: (6, {}), {3}: (7, {}), {4}: (8, {})} | custom-call | flops 1 | bytes 1 | tf_op jit(solution)/shard_map/pallas_call | solution.py:144
  90.1 3.7 %collective-permute-done.37.refs_1_ = bf16[64,4096]{1,0:T(8,128)(2,1)S(1)} collective-permute-done((bf16[64,4096]{1,0:T(8,128)(2,1)S(1)}, bf16[64,4096]{1,0:T(8,128)(2,1)S(1)}, u32[]{:S(2)}, u32[]{:S(2)}) %collective-permute-start.37) | collective-permute-done | bytes 524320 | tf_op jit(solution)/shard_map/ppermute | solution.py:27
  95.8 5.2 %collective-permute-done.38.refs_1_ = bf16[64,576]{1,0:T(8,128)(2,1)S(1)} collective-permute-done((bf16[64,576]{1,0:T(8,128)(2,1)S(1)}, bf16[64,576]{1,0:T(8,128)(2,1)S(1)}, u32[]{:S(2)}, u32[]{:S(2)}) %collective-permute-start.38) | collective-permute-done | bytes 73760 | tf_op jit(solution)/shard_map/ppermute | solution.py:27
  101.0 1.2 shard_map.150
  102.3 1.2 shard_map.151
  104.1 2.6 %shard_map.152 = (bf16[32,4096]{1,0:T(8,128)(2,1)S(1)}, bf16[32,4096]{1,0:T(8,128)(2,1)S(1)}, bf16[64,4096]{1,0:T(8,128)(2,1)S(1)}, bf16[576,4096]{1,0:T(8,128)(...) custom-call(s32[1]{0:T(128)} %bitcast.side_ref, ...), custom_call_target="tpu_custom_call", output_to_operand_aliasing={{3}: (2, {}), {4}: (3, {}), {5}: (4, {}), {6}: (5, {})} | custom-call | flops 1 | bytes 1 | tf_op jit(solution)/shard_map/pallas_call | solution.py:144
  107.7 1.1 collective-permute-done.40.refs_1_
  109.3 1.2 shard_map.154
  113.4 1.7 shard_map.155
  115.1 1.7 shard_map.156
  116.9 3.6 %shard_map.157 = (bf16[64,576]{1,0:T(8,128)(2,1)S(1)}, bf16[576,4096]{1,0:T(8,128)(2,1)S(1)}, bf16[576,4096]{1,0:T(8,128)(2,1)S(1)}, bf16[576,8192]{1,0:T(8,128)(2,1)S(1)}, f32[8,128]{1,0:T(8,128)S(1)}) custom-call(s32[1]{0:T(128)} %bitcast.side_ref, ...), custom_call_target="tpu_custom_call", output_to_operand_aliasing={{1}: (5, {}), {2}: (6, {}), {3}: (7, {}), {4}: (8, {})} | custom-call | flops 1 | bytes 1 | tf_op jit(solution)/shard_map/pallas_call | solution.py:144
  120.6 4.4 %collective-permute-done.52.refs_1_ = bf16[64,576]{1,0:T(8,128)(2,1)S(1)} collective-permute-done((bf16[64,576]{1,0:T(8,128)(2,1)S(1)}, bf16[64,576]{1,0:T(8,128)(2,1)S(1)}, u32[]{:S(2)}, u32[]{:S(2)}) %collective-permute-start.52) | collective-permute-done | bytes 73760 | tf_op jit(solution)/shard_map/ppermute | solution.py:27
  125.0 1.1 collective-permute-start.53
  126.1 5.2 %collective-permute-done.53.refs_1_ = bf16[64,576]{1,0:T(8,128)(2,1)S(1)} collective-permute-done((bf16[64,576]{1,0:T(8,128)(2,1)S(1)}, bf16[64,576]{1,0:T(8,128)(2,1)S(1)}, u32[]{:S(2)}, u32[]{:S(2)}) %collective-permute-start.53) | collective-permute-done | bytes 73760 | tf_op jit(solution)/shard_map/ppermute | solution.py:27
  131.3 2.6 %shard_map.160 = (bf16[32,4096]{1,0:T(8,128)(2,1)S(1)}, bf16[32,4096]{1,0:T(8,128)(2,1)S(1)}, bf16[64,4096]{1,0:T(8,128)(2,1)S(1)}, bf16[576,4096]{1,0:T(8,128)(...) custom-call(s32[1]{0:T(128)} %bitcast.side_ref, ...), custom_call_target="tpu_custom_call", output_to_operand_aliasing={{3}: (2, {}), {4}: (3, {}), {5}: (4, {}), {6}: (5, {})} | custom-call | flops 1 | bytes 1 | tf_op jit(solution)/shard_map/pallas_call | solution.py:144
  134.5 1.2 shard_map.161
  135.7 1.2 shard_map.162
  137.1 1.4 collective-permute-start.66
  142.3 5.5 %shard_map.167 = (bf16[576,16384]{1,0:T(8,128)(2,1)}, bf16[576,4096]{1,0:T(8,128)(2,1)S(1)}, bf16[576,4096]{1,0:T(8,128)(2,1)S(1)}, bf16[576,8192]{1,0:T(8,128)(2,1)S(1)}, f32[8,128]{1,0:T(8,128)S(1)}) custom-call(s32[1]{0:T(128)} %bitcast.side_ref, ...), custom_call_target="tpu_custom_call", output_to_operand_aliasing={{1}: (8, {}), {2}: (9, {}), {3}: (10, {}), {4}: (11, {})} | custom-call | flops 1 | bytes 1 | tf_op jit(solution)/shard_map/pallas_call | solution.py:144
  150.5 6.5 %shard_map.171 = (bf16[576,16384]{1,0:T(8,128)(2,1)}, bf16[576,4096]{1,0:T(8,128)(2,1)S(1)}, bf16[576,4096]{1,0:T(8,128)(2,1)S(1)}, f32[8,128]{1,0:T(8,128)S(1)}, bf16[576,8192]{1,0:T(8,128)(2,1)S(1)}) custom-call(s32[1]{0:T(128)} %bitcast.side_ref, ...), custom_call_target="tpu_custom_call", output_to_operand_aliasing={{0}: (8, {}), {1}: (9, {}), {2}: (10, {}), {3}: (11, {})} | custom-call | flops 1 | bytes 1 | tf_op jit(solution)/shard_map/pallas_call | solution.py:144
  157.0 5.1 %shard_map.172 = (bf16[576,16384]{1,0:T(8,128)(2,1)}, bf16[576,4096]{1,0:T(8,128)(2,1)S(1)}, bf16[576,8192]{1,0:T(8,128)(2,1)S(1)}, f32[8,128]{1,0:T(8,128)S(1)}, bf16[576,4096]{1,0:T(8,128)(2,1)S(1)}) custom-call(s32[1]{0:T(128)} %bitcast.side_ref, ...), custom_call_target="tpu_custom_call", output_to_operand_aliasing={{0}: (8, {}), {1}: (9, {}), {2}: (10, {}), {3}: (11, {})} | custom-call | flops 1 | bytes 1 | tf_op jit(solution)/shard_map/pallas_call | solution.py:144
  165.5 5.6 %shard_map.175 = (bf16[576,16384]{1,0:T(8,128)(2,1)}, f32[1,16384]{1,0:T(1,128)}, bf16[576,8192]{1,0:T(8,128)(2,1)S(1)}, bf16[576,4096]{1,0:T(8,128)(2,1)S(1)}, f32[8,128]{1,0:T(8,128)S(1)}) custom-call(s32[1]{0:T(128)} %bitcast.side_ref, ...), custom_call_target="tpu_custom_call", output_to_operand_aliasing={{2}: (9, {}), {3}: (10, {}), {4}: (11, {})} | custom-call | flops 1 | bytes 1 | tf_op jit(solution)/shard_map/pallas_call | solution.py:144
  173.4 5.2 %shard_map.178 = (bf16[576,16384]{1,0:T(8,128)(2,1)}, f32[1,16384]{1,0:T(1,128)}, bf16[576,4096]{1,0:T(8,128)(2,1)S(1)}, f32[8,128]{1,0:T(8,128)S(1)}, bf16[576,4096]{1,0:T(8,128)(2,1)S(1)}) custom-call(s32[1]{0:T(128)} %bitcast.side_ref, ...), custom_call_target="tpu_custom_call", output_to_operand_aliasing={{0}: (9, {}), {1}: (10, {}), {2}: (11, {}), {3}: (12, {})} | custom-call | flops 1 | bytes 1 | tf_op jit(solution)/shard_map/pallas_call | solution.py:144
  178.6 3.2 %shard_map.179 = (bf16[576,16384]{1,0:T(8,128)(2,1)}, f32[1,16384]{1,0:T(1,128)}, bf16[576,4096]{1,0:T(8,128)(2,1)S(1)}, f32[8,128]{1,0:T(8,128)S(1)}) custom-call(s32[1]{0:T(128)} %bitcast.side_ref, bf16[576,128]{1,0:T(8,128)(2,1)S(1)} %get-tuple-element.735.refs_0_, ...), custom_call_target="tpu_custom_call", output_to_operand_aliasing={{0}: (9, {}), {1}: (10, {}), {2}: (11, {}), {3}: (12, {})} | custom-call | flops 1 | bytes 1 | tf_op jit(solution)/shard_map/pallas_call | solution.py:144
  (218 shorter events, 41.4 us)
Async XLA Ops:
  2.5 12.5 %collective-permute-start = (bf16[64,576]{1,0:T(8,128)(2,1)S(1)}, bf16[64,576]{1,0:T(8,128)(2,1)S(1)}, u32[]{:S(2)}, u32[]{:S(2)}) collective-permute-start(bf16[64,576]{1,0:T(8,128)(2,1)S(1)} %get-tuple-element.404), channel_id=1, source_target_pairs={{0,0},{1,4},{2,8},{3,12},{4,1},{5,5},{6,9},{7,13},{8,2},{9,6},{10,... | collective-permute-start | bytes 221192 | tf_op jit(solution)/shard_map/ppermute | solution.py:476
  15.4 5.4 %collective-permute-start.1 = (bf16[32,1152]{1,0:T(8,128)(2,1)S(1)}, bf16[32,1152]{1,0:T(8,128)(2,1)S(1)}, u32[]{:S(2)}, u32[]{:S(2)}) collective-permute-start(bf16[32,1152]{1,0:T(8,128)(2,1)S(1)} %get-tuple-element.436), channel_id=1, source_target_pairs={{0,1},{1,0},{2,3},{3,2},{4,5},{5,4},{6,7},{7,6},{8,9},{9,8},{10,11... | collective-permute-start | bytes 221192 | tf_op jit(solution)/shard_map/ppermute | solution.py:27
  19.9 6.4 %collective-permute-start.4 = (bf16[64,576]{1,0:T(8,128)(2,1)S(1)}, bf16[64,576]{1,0:T(8,128)(2,1)S(1)}, u32[]{:S(2)}, u32[]{:S(2)}) collective-permute-start(bf16[64,576]{1,0:T(8,128)(2,1)S(1)} %get-tuple-element.446), channel_id=1, source_target_pairs={{0,0},{1,4},{2,8},{3,12},{4,1},{5,5},{6,9},{7,13},{8,2},{9,6},{10,... | collective-permute-start | bytes 221192 | tf_op jit(solution)/shard_map/ppermute | solution.py:476
  21.5 10.4 %collective-permute-start.3 = (bf16[64,1152]{1,0:T(8,128)(2,1)S(1)}, bf16[64,1152]{1,0:T(8,128)(2,1)S(1)}, u32[]{:S(2)}, u32[]{:S(2)}) collective-permute-start(bf16[64,1152]{1,0:T(8,128)(2,1)S(1)} %get-tuple-element.445.refs_0_), channel_id=1, source_target_pairs={{0,2},{1,3},{2,0},{3,1},{4,6},{5,7},{6,4},{7,5},{8,10},{9,11},{10,... | collective-permute-start | bytes 442376 | tf_op jit(solution)/shard_map/ppermute | solution.py:27
  31.9 3.2 %collective-permute-start.7 = (f32[32,1152]{1,0:T(8,128)S(1)}, f32[32,1152]{1,0:T(8,128)S(1)}, u32[]{:S(2)}, u32[]{:S(2)}) collective-permute-start(f32[32,1152]{1,0:T(8,128)S(1)} %get-tuple-element.469), channel_id=1, source_target_pairs={{0,1},{1,0},{2,3},{3,2},{4,5},{5,4},{6,7},{7,6},{8,9},{9,8},{10,11... | collective-permute-start | bytes 442376 | tf_op jit(solution)/shard_map/ppermute | solution.py:27
  32.0 3.1 %collective-permute-start.8 = (f32[32,1152]{1,0:T(8,128)S(1)}, f32[32,1152]{1,0:T(8,128)S(1)}, u32[]{:S(2)}, u32[]{:S(2)}) collective-permute-start(f32[32,1152]{1,0:T(8,128)S(1)} %get-tuple-element.470), channel_id=1, source_target_pairs={{0,1},{1,0},{2,3},{3,2},{4,5},{5,4},{6,7},{7,6},{8,9},{9,8},{10,11... | collective-permute-start | bytes 442376 | tf_op jit(solution)/shard_map/ppermute | solution.py:27
  32.5 7.7 %collective-permute-start.11 = (bf16[64,1152]{1,0:T(8,128)(2,1)S(1)}, bf16[64,1152]{1,0:T(8,128)(2,1)S(1)}, u32[]{:S(2)}, u32[]{:S(2)}) collective-permute-start(bf16[64,1152]{1,0:T(8,128)(2,1)S(1)} %get-tuple-element.483.refs_0_), channel_id=1, source_target_pairs={{0,2},{1,3},{2,0},{3,1},{4,6},{5,7},{6,4},{7,5},{8,10},{9,11},{10,... | collective-permute-start | bytes 442376 | tf_op jit(solution)/shard_map/ppermute | solution.py:27
  35.6 4.5 %collective-permute-start.9 = (bf16[64,576]{1,0:T(8,128)(2,1)S(1)}, bf16[64,576]{1,0:T(8,128)(2,1)S(1)}, u32[]{:S(2)}, u32[]{:S(2)}) collective-permute-start(bf16[64,576]{1,0:T(8,128)(2,1)S(1)} %get-tuple-element.476.refs_0_), channel_id=1, source_target_pairs={{0,4},{4,0},{8,12},{12,8},{1,5},{5,1},{9,13},{13,9},{2,6},{6,2},{1... | collective-permute-start | bytes 221192 | tf_op jit(solution)/shard_map/ppermute | solution.py:27
  40.8 6.7 %collective-permute-start.10 = (bf16[64,576]{1,0:T(8,128)(2,1)S(1)}, bf16[64,576]{1,0:T(8,128)(2,1)S(1)}, u32[]{:S(2)}, u32[]{:S(2)}) collective-permute-start(bf16[64,576]{1,0:T(8,128)(2,1)S(1)} %get-tuple-element.482.refs_0_), channel_id=1, source_target_pairs={{0,8},{4,12},{8,0},{12,4},{1,9},{5,13},{9,1},{13,5},{2,10},{6,14},... | collective-permute-start | bytes 221192 | tf_op jit(solution)/shard_map/ppermute | solution.py:27
  42.6 6.4 %collective-permute-start.14 = (bf16[64,576]{1,0:T(8,128)(2,1)S(1)}, bf16[64,576]{1,0:T(8,128)(2,1)S(1)}, u32[]{:S(2)}, u32[]{:S(2)}) collective-permute-start(bf16[64,576]{1,0:T(8,128)(2,1)S(1)} %get-tuple-element.502.refs_0_), channel_id=1, source_target_pairs={{0,4},{4,0},{8,12},{12,8},{1,5},{5,1},{9,13},{13,9},{2,6},{6,2},{1... | collective-permute-start | bytes 221192 | tf_op jit(solution)/shard_map/ppermute | solution.py:27
  53.7 20.4 %collective-permute-start.23 = (bf16[64,4096]{1,0:T(8,128)(2,1)S(1)}, bf16[64,4096]{1,0:T(8,128)(2,1)S(1)}, u32[]{:S(2)}, u32[]{:S(2)}) collective-permute-start(bf16[64,4096]{1,0:T(8,128)(2,1)S(1)} %get-tuple-element.546.refs_0_), channel_id=1, source_target_pairs={{0,2},{1,3},{2,0},{3,1},{4,6},{5,7},{6,4},{7,5},{8,10},{9,11},{10,... | collective-permute-start | bytes 1572872 | tf_op jit(solution)/shard_map/ppermute | solution.py:27
  58.0 6.7 %collective-permute-start.20 = (bf16[32,4096]{1,0:T(8,128)(2,1)S(1)}, bf16[32,4096]{1,0:T(8,128)(2,1)S(1)}, u32[]{:S(2)}, u32[]{:S(2)}) collective-permute-start(bf16[32,4096]{1,0:T(8,128)(2,1)S(1)} %get-tuple-element.537), channel_id=1, source_target_pairs={{0,1},{1,0},{2,3},{3,2},{4,5},{5,4},{6,7},{7,6},{8,9},{9,8},{10,11... | collective-permute-start | bytes 786440 | tf_op jit(solution)/shard_map/ppermute | solution.py:27
  58.1 6.6 %collective-permute-start.21 = (bf16[32,4096]{1,0:T(8,128)(2,1)S(1)}, bf16[32,4096]{1,0:T(8,128)(2,1)S(1)}, u32[]{:S(2)}, u32[]{:S(2)}) collective-permute-start(bf16[32,4096]{1,0:T(8,128)(2,1)S(1)} %get-tuple-element.538), channel_id=1, source_target_pairs={{0,1},{1,0},{2,3},{3,2},{4,5},{5,4},{6,7},{7,6},{8,9},{9,8},{10,11... | collective-permute-start | bytes 786440 | tf_op jit(solution)/shard_map/ppermute | solution.py:27
  58.5 6.1 %collective-permute-start.15 = (bf16[64,576]{1,0:T(8,128)(2,1)S(1)}, bf16[64,576]{1,0:T(8,128)(2,1)S(1)}, u32[]{:S(2)}, u32[]{:S(2)}) collective-permute-start(bf16[64,576]{1,0:T(8,128)(2,1)S(1)} %get-tuple-element.507.refs_0_), channel_id=1, source_target_pairs={{0,8},{4,12},{8,0},{12,4},{1,9},{5,13},{9,1},{13,5},{2,10},{6,14},... | collective-permute-start | bytes 221192 | tf_op jit(solution)/shard_map/ppermute | solution.py:27
  64.8 18.6 %collective-permute-start.22 = (bf16[64,4096]{1,0:T(8,128)(2,1)S(1)}, bf16[64,4096]{1,0:T(8,128)(2,1)S(1)}, u32[]{:S(2)}, u32[]{:S(2)}) collective-permute-start(bf16[64,4096]{1,0:T(8,128)(2,1)S(1)} %get-tuple-element.544.refs_0_), channel_id=1, source_target_pairs={{0,2},{1,3},{2,0},{3,1},{4,6},{5,7},{6,4},{7,5},{8,10},{9,11},{10,... | collective-permute-start | bytes 1572872 | tf_op jit(solution)/shard_map/ppermute | solution.py:27
  69.7 5.9 %collective-permute-start.30 = (bf16[32,2048]{1,0:T(8,128)(2,1)S(1)}, bf16[32,2048]{1,0:T(8,128)(2,1)S(1)}, u32[]{:S(2)}, u32[]{:S(2)}) collective-permute-start(bf16[32,2048]{1,0:T(8,128)(2,1)S(1)} %get-tuple-element.584), channel_id=1, source_target_pairs={{0,1},{1,0},{2,3},{3,2},{4,5},{5,4},{6,7},{7,6},{8,9},{9,8},{10,11... | collective-permute-start | bytes 393224 | tf_op jit(solution)/shard_map/ppermute | solution.py:27
  75.1 3.7 %collective-permute-start.31 = (bf16[32,2048]{1,0:T(8,128)(2,1)S(1)}, bf16[32,2048]{1,0:T(8,128)(2,1)S(1)}, u32[]{:S(2)}, u32[]{:S(2)}) collective-permute-start(bf16[32,2048]{1,0:T(8,128)(2,1)S(1)} %get-tuple-element.585), channel_id=1, source_target_pairs={{0,1},{1,0},{2,3},{3,2},{4,5},{5,4},{6,7},{7,6},{8,9},{9,8},{10,11... | collective-permute-start | bytes 393224 | tf_op jit(solution)/shard_map/ppermute | solution.py:27
  75.6 3.2 %collective-permute-start.28 = (bf16[32,2048]{1,0:T(8,128)(2,1)S(1)}, bf16[32,2048]{1,0:T(8,128)(2,1)S(1)}, u32[]{:S(2)}, u32[]{:S(2)}) collective-permute-start(bf16[32,2048]{1,0:T(8,128)(2,1)S(1)} %get-tuple-element.581), channel_id=1, source_target_pairs={{0,1},{1,0},{2,3},{3,2},{4,5},{5,4},{6,7},{7,6},{8,9},{9,8},{10,11... | collective-permute-start | bytes 393224 | tf_op jit(solution)/shard_map/ppermute | solution.py:27
  76.1 2.8 %collective-permute-start.29 = (bf16[32,2048]{1,0:T(8,128)(2,1)S(1)}, bf16[32,2048]{1,0:T(8,128)(2,1)S(1)}, u32[]{:S(2)}, u32[]{:S(2)}) collective-permute-start(bf16[32,2048]{1,0:T(8,128)(2,1)S(1)} %get-tuple-element.582), channel_id=1, source_target_pairs={{0,1},{1,0},{2,3},{3,2},{4,5},{5,4},{6,7},{7,6},{8,9},{9,8},{10,11... | collective-permute-start | bytes 393224 | tf_op jit(solution)/shard_map/ppermute | solution.py:27
  76.8 4.0 %collective-permute-start.24 = (bf16[32,2048]{1,0:T(8,128)(2,1)S(1)}, bf16[32,2048]{1,0:T(8,128)(2,1)S(1)}, u32[]{:S(2)}, u32[]{:S(2)}) collective-permute-start(bf16[32,2048]{1,0:T(8,128)(2,1)S(1)} %get-tuple-element.569), channel_id=1, source_target_pairs={{0,1},{1,0},{2,3},{3,2},{4,5},{5,4},{6,7},{7,6},{8,9},{9,8},{10,11... | collective-permute-start | bytes 393224 | tf_op jit(solution)/shard_map/ppermute | solution.py:27
  79.0 14.8 %collective-permute-start.37 = (bf16[64,4096]{1,0:T(8,128)(2,1)S(1)}, bf16[64,4096]{1,0:T(8,128)(2,1)S(1)}, u32[]{:S(2)}, u32[]{:S(2)}) collective-permute-start(bf16[64,4096]{1,0:T(8,128)(2,1)S(1)} %get-tuple-element.614.refs_0_), channel_id=1, source_target_pairs={{0,2},{1,3},{2,0},{3,1},{4,6},{5,7},{6,4},{7,5},{8,10},{9,11},{10,... | collective-permute-start | bytes 1572872 | tf_op jit(solution)/shard_map/ppermute | solution.py:27
  80.4 4.6 %collective-permute-start.34 = (bf16[32,4096]{1,0:T(8,128)(2,1)S(1)}, bf16[32,4096]{1,0:T(8,128)(2,1)S(1)}, u32[]{:S(2)}, u32[]{:S(2)}) collective-permute-start(bf16[32,4096]{1,0:T(8,128)(2,1)S(1)} %get-tuple-element.603), channel_id=1, source_target_pairs={{0,1},{1,0},{2,3},{3,2},{4,5},{5,4},{6,7},{7,6},{8,9},{9,8},{10,11... | collective-permute-start | bytes 786440 | tf_op jit(solution)/shard_map/ppermute | solution.py:27
  80.9 4.2 %collective-permute-start.35 = (bf16[32,4096]{1,0:T(8,128)(2,1)S(1)}, bf16[32,4096]{1,0:T(8,128)(2,1)S(1)}, u32[]{:S(2)}, u32[]{:S(2)}) collective-permute-start(bf16[32,4096]{1,0:T(8,128)(2,1)S(1)} %get-tuple-element.604), channel_id=1, source_target_pairs={{0,1},{1,0},{2,3},{3,2},{4,5},{5,4},{6,7},{7,6},{8,9},{9,8},{10,11... | collective-permute-start | bytes 786440 | tf_op jit(solution)/shard_map/ppermute | solution.py:27
  85.2 24.1 %collective-permute-start.39 = (bf16[64,4096]{1,0:T(8,128)(2,1)S(1)}, bf16[64,4096]{1,0:T(8,128)(2,1)S(1)}, u32[]{:S(2)}, u32[]{:S(2)}) collective-permute-start(bf16[64,4096]{1,0:T(8,128)(2,1)S(1)} %get-tuple-element.634.refs_0_), channel_id=1, source_target_pairs={{0,2},{1,3},{2,0},{3,1},{4,6},{5,7},{6,4},{7,5},{8,10},{9,11},{10,... | collective-permute-start | bytes 1572872 | tf_op jit(solution)/shard_map/ppermute | solution.py:27
  90.0 4.6 %collective-permute-start.36 = (bf16[64,576]{1,0:T(8,128)(2,1)S(1)}, bf16[64,576]{1,0:T(8,128)(2,1)S(1)}, u32[]{:S(2)}, u32[]{:S(2)}) collective-permute-start(bf16[64,576]{1,0:T(8,128)(2,1)S(1)} %get-tuple-element.613.refs_0_), channel_id=1, source_target_pairs={{0,4},{4,0},{8,12},{12,8},{1,5},{5,1},{9,13},{13,9},{2,6},{6,2},{1... | collective-permute-start | bytes 221192 | tf_op jit(solution)/shard_map/ppermute | solution.py:27
  94.6 6.4 %collective-permute-start.38 = (bf16[64,576]{1,0:T(8,128)(2,1)S(1)}, bf16[64,576]{1,0:T(8,128)(2,1)S(1)}, u32[]{:S(2)}, u32[]{:S(2)}) collective-permute-start(bf16[64,576]{1,0:T(8,128)(2,1)S(1)} %get-tuple-element.623.refs_0_), channel_id=1, source_target_pairs={{0,8},{4,12},{8,0},{12,4},{1,9},{5,13},{9,1},{13,5},{2,10},{6,14},... | collective-permute-start | bytes 221192 | tf_op jit(solution)/shard_map/ppermute | solution.py:27
  103.5 3.7 %collective-permute-start.42 = (bf16[32,2048]{1,0:T(8,128)(2,1)S(1)}, bf16[32,2048]{1,0:T(8,128)(2,1)S(1)}, u32[]{:S(2)}, u32[]{:S(2)}) collective-permute-start(bf16[32,2048]{1,0:T(8,128)(2,1)S(1)} %get-tuple-element.647), channel_id=1, source_target_pairs={{0,1},{1,0},{2,3},{3,2},{4,5},{5,4},{6,7},{7,6},{8,9},{9,8},{10,11... | collective-permute-start | bytes 393224 | tf_op jit(solution)/shard_map/ppermute | solution.py:27
  103.6 3.7 %collective-permute-start.43 = (bf16[32,2048]{1,0:T(8,128)(2,1)S(1)}, bf16[32,2048]{1,0:T(8,128)(2,1)S(1)}, u32[]{:S(2)}, u32[]{:S(2)}) collective-permute-start(bf16[32,2048]{1,0:T(8,128)(2,1)S(1)} %get-tuple-element.648), channel_id=1, source_target_pairs={{0,1},{1,0},{2,3},{3,2},{4,5},{5,4},{6,7},{7,6},{8,9},{9,8},{10,11... | collective-permute-start | bytes 393224 | tf_op jit(solution)/shard_map/ppermute | solution.py:27
  108.8 2.8 %collective-permute-start.50 = (bf16[32,2048]{1,0:T(8,128)(2,1)S(1)}, bf16[32,2048]{1,0:T(8,128)(2,1)S(1)}, u32[]{:S(2)}, u32[]{:S(2)}) collective-permute-start(bf16[32,2048]{1,0:T(8,128)(2,1)S(1)} %get-tuple-element.670), channel_id=1, source_target_pairs={{0,1},{1,0},{2,3},{3,2},{4,5},{5,4},{6,7},{7,6},{8,9},{9,8},{10,11... | collective-permute-start | bytes 393224 | tf_op jit(solution)/shard_map/ppermute | solution.py:27
  110.5 6.3 %collective-permute-start.46 = (bf16[32,4096]{1,0:T(8,128)(2,1)S(1)}, bf16[32,4096]{1,0:T(8,128)(2,1)S(1)}, u32[]{:S(2)}, u32[]{:S(2)}) collective-permute-start(bf16[32,4096]{1,0:T(8,128)(2,1)S(1)} %get-tuple-element.664), channel_id=1, source_target_pairs={{0,1},{1,0},{2,3},{3,2},{4,5},{5,4},{6,7},{7,6},{8,9},{9,8},{10,11... | collective-permute-start | bytes 786440 | tf_op jit(solution)/shard_map/ppermute | solution.py:27
  110.9 5.9 %collective-permute-start.47 = (bf16[32,4096]{1,0:T(8,128)(2,1)S(1)}, bf16[32,4096]{1,0:T(8,128)(2,1)S(1)}, u32[]{:S(2)}, u32[]{:S(2)}) collective-permute-start(bf16[32,4096]{1,0:T(8,128)(2,1)S(1)} %get-tuple-element.665), channel_id=1, source_target_pairs={{0,1},{1,0},{2,3},{3,2},{4,5},{5,4},{6,7},{7,6},{8,9},{9,8},{10,11... | collective-permute-start | bytes 786440 | tf_op jit(solution)/shard_map/ppermute | solution.py:27
  111.4 3.7 %collective-permute-start.48 = (bf16[32,2048]{1,0:T(8,128)(2,1)S(1)}, bf16[32,2048]{1,0:T(8,128)(2,1)S(1)}, u32[]{:S(2)}, u32[]{:S(2)}) collective-permute-start(bf16[32,2048]{1,0:T(8,128)(2,1)S(1)} %get-tuple-element.667), channel_id=1, source_target_pairs={{0,1},{1,0},{2,3},{3,2},{4,5},{5,4},{6,7},{7,6},{8,9},{9,8},{10,11... | collective-permute-start | bytes 393224 | tf_op jit(solution)/shard_map/ppermute | solution.py:27
  111.6 3.5 %collective-permute-start.49 = (bf16[32,2048]{1,0:T(8,128)(2,1)S(1)}, bf16[32,2048]{1,0:T(8,128)(2,1)S(1)}, u32[]{:S(2)}, u32[]{:S(2)}) collective-permute-start(bf16[32,2048]{1,0:T(8,128)(2,1)S(1)} %get-tuple-element.668), channel_id=1, source_target_pairs={{0,1},{1,0},{2,3},{3,2},{4,5},{5,4},{6,7},{7,6},{8,9},{9,8},{10,11... | collective-permute-start | bytes 393224 | tf_op jit(solution)/shard_map/ppermute | solution.py:27
  112.7 35.1 %collective-permute-start.60 = (bf16[64,8192]{1,0:T(8,128)(2,1)S(1)}, bf16[64,8192]{1,0:T(8,128)(2,1)S(1)}, u32[]{:S(2)}, u32[]{:S(2)}) collective-permute-start(bf16[64,8192]{1,0:T(8,128)(2,1)S(1)} %get-tuple-element.736.refs_3_), channel_id=1, source_target_pairs={{0,2},{1,3},{2,0},{3,1},{4,6},{5,7},{6,4},{7,5},{8,10},{9,11},{10,... | collective-permute-start | bytes 3145736 | tf_op jit(solution)/shard_map/ppermute | solution.py:27
  120.5 4.5 %collective-permute-start.52 = (bf16[64,576]{1,0:T(8,128)(2,1)S(1)}, bf16[64,576]{1,0:T(8,128)(2,1)S(1)}, u32[]{:S(2)}, u32[]{:S(2)}) collective-permute-start(bf16[64,576]{1,0:T(8,128)(2,1)S(1)} %get-tuple-element.687.refs_0_), channel_id=1, source_target_pairs={{0,4},{4,0},{8,12},{12,8},{1,5},{5,1},{9,13},{13,9},{2,6},{6,2},{1... | collective-permute-start | bytes 221192 | tf_op jit(solution)/shard_map/ppermute | solution.py:27
  125.0 6.3 %collective-permute-start.53 = (bf16[64,576]{1,0:T(8,128)(2,1)S(1)}, bf16[64,576]{1,0:T(8,128)(2,1)S(1)}, u32[]{:S(2)}, u32[]{:S(2)}) collective-permute-start(bf16[64,576]{1,0:T(8,128)(2,1)S(1)} %get-tuple-element.692.refs_0_), channel_id=1, source_target_pairs={{0,8},{4,12},{8,0},{12,4},{1,9},{5,13},{9,1},{13,5},{2,10},{6,14},... | collective-permute-start | bytes 221192 | tf_op jit(solution)/shard_map/ppermute | solution.py:27
  133.9 3.0 %collective-permute-start.58 = (bf16[32,4096]{1,0:T(8,128)(2,1)S(1)}, bf16[32,4096]{1,0:T(8,128)(2,1)S(1)}, u32[]{:S(2)}, u32[]{:S(2)}) collective-permute-start(bf16[32,4096]{1,0:T(8,128)(2,1)S(1)} %get-tuple-element.717), channel_id=1, source_target_pairs={{0,1},{1,0},{2,3},{3,2},{4,5},{5,4},{6,7},{7,6},{8,9},{9,8},{10,11... | collective-permute-start | bytes 786440 | tf_op jit(solution)/shard_map/ppermute | solution.py:27
  134.0 2.9 %collective-permute-start.59 = (bf16[32,4096]{1,0:T(8,128)(2,1)S(1)}, bf16[32,4096]{1,0:T(8,128)(2,1)S(1)}, u32[]{:S(2)}, u32[]{:S(2)}) collective-permute-start(bf16[32,4096]{1,0:T(8,128)(2,1)S(1)} %get-tuple-element.718), channel_id=1, source_target_pairs={{0,1},{1,0},{2,3},{3,2},{4,5},{5,4},{6,7},{7,6},{8,9},{9,8},{10,11... | collective-permute-start | bytes 786440 | tf_op jit(solution)/shard_map/ppermute | solution.py:27
  137.1 25.7 %collective-permute-start.66 = (bf16[64,4096]{1,0:T(8,128)(2,1)S(1)}, bf16[64,4096]{1,0:T(8,128)(2,1)S(1)}, u32[]{:S(2)}, u32[]{:S(2)}) collective-permute-start(bf16[64,4096]{1,0:T(8,128)(2,1)S(1)} %get-tuple-element.758.refs_3_), channel_id=1, source_target_pairs={{0,2},{1,3},{2,0},{3,1},{4,6},{5,7},{6,4},{7,5},{8,10},{9,11},{10,... | collective-permute-start | bytes 1572872 | tf_op jit(solution)/shard_map/ppermute | solution.py:27
  141.4 29.8 %collective-permute-start.63 = (bf16[64,4096]{1,0:T(8,128)(2,1)S(1)}, bf16[64,4096]{1,0:T(8,128)(2,1)S(1)}, u32[]{:S(2)}, u32[]{:S(2)}) collective-permute-start(bf16[64,4096]{1,0:T(8,128)(2,1)S(1)} %get-tuple-element.754.refs_3_), channel_id=1, source_target_pairs={{0,2},{1,3},{2,0},{3,1},{4,6},{5,7},{6,4},{7,5},{8,10},{9,11},{10,... | collective-permute-start | bytes 1572872 | tf_op jit(solution)/shard_map/ppermute | solution.py:27
  148.6 15.6 %collective-permute-start.64 = (bf16[32,4096]{1,0:T(8,128)(2,1)S(1)}, bf16[32,4096]{1,0:T(8,128)(2,1)S(1)}, u32[]{:S(2)}, u32[]{:S(2)}) collective-permute-start(bf16[32,4096]{1,0:T(8,128)(2,1)S(1)} %get-tuple-element.755), channel_id=1, source_target_pairs={{0,1},{1,0},{2,3},{3,2},{4,5},{5,4},{6,7},{7,6},{8,9},{9,8},{10,11... | collective-permute-start | bytes 786440 | tf_op jit(solution)/shard_map/ppermute | solution.py:27
  148.7 15.6 %collective-permute-start.65 = (bf16[32,4096]{1,0:T(8,128)(2,1)S(1)}, bf16[32,4096]{1,0:T(8,128)(2,1)S(1)}, u32[]{:S(2)}, u32[]{:S(2)}) collective-permute-start(bf16[32,4096]{1,0:T(8,128)(2,1)S(1)} %get-tuple-element.756), channel_id=1, source_target_pairs={{0,1},{1,0},{2,3},{3,2},{4,5},{5,4},{6,7},{7,6},{8,9},{9,8},{10,11... | collective-permute-start | bytes 786440 | tf_op jit(solution)/shard_map/ppermute | solution.py:27
  164.1 8.2 %collective-permute-start.71 = (bf16[32,2048]{1,0:T(8,128)(2,1)S(1)}, bf16[32,2048]{1,0:T(8,128)(2,1)S(1)}, u32[]{:S(2)}, u32[]{:S(2)}) collective-permute-start(bf16[32,2048]{1,0:T(8,128)(2,1)S(1)} %get-tuple-element.786), channel_id=1, source_target_pairs={{0,1},{1,0},{2,3},{3,2},{4,5},{5,4},{6,7},{7,6},{8,9},{9,8},{10,11... | collective-permute-start | bytes 393224 | tf_op jit(solution)/shard_map/ppermute | solution.py:27
  164.2 8.6 %collective-permute-start.72 = (bf16[32,2048]{1,0:T(8,128)(2,1)S(1)}, bf16[32,2048]{1,0:T(8,128)(2,1)S(1)}, u32[]{:S(2)}, u32[]{:S(2)}) collective-permute-start(bf16[32,2048]{1,0:T(8,128)(2,1)S(1)} %get-tuple-element.787), channel_id=1, source_target_pairs={{0,1},{1,0},{2,3},{3,2},{4,5},{5,4},{6,7},{7,6},{8,9},{9,8},{10,11... | collective-permute-start | bytes 393224 | tf_op jit(solution)/shard_map/ppermute | solution.py:27
  171.6 7.0 %collective-permute-start.61 = (bf16[32,2048]{1,0:T(8,128)(2,1)S(1)}, bf16[32,2048]{1,0:T(8,128)(2,1)S(1)}, u32[]{:S(2)}, u32[]{:S(2)}) collective-permute-start(bf16[32,2048]{1,0:T(8,128)(2,1)S(1)} %get-tuple-element.751), channel_id=1, source_target_pairs={{0,1},{1,0},{2,3},{3,2},{4,5},{5,4},{6,7},{7,6},{8,9},{9,8},{10,11... | collective-permute-start | bytes 393224 | tf_op jit(solution)/shard_map/ppermute | solution.py:27
  172.4 6.2 %collective-permute-start.62 = (bf16[32,2048]{1,0:T(8,128)(2,1)S(1)}, bf16[32,2048]{1,0:T(8,128)(2,1)S(1)}, u32[]{:S(2)}, u32[]{:S(2)}) collective-permute-start(bf16[32,2048]{1,0:T(8,128)(2,1)S(1)} %get-tuple-element.752), channel_id=1, source_target_pairs={{0,1},{1,0},{2,3},{3,2},{4,5},{5,4},{6,7},{7,6},{8,9},{9,8},{10,11... | collective-permute-start | bytes 393224 | tf_op jit(solution)/shard_map/ppermute | solution.py:27
  172.8 5.8 %collective-permute-start.69 = (bf16[32,2048]{1,0:T(8,128)(2,1)S(1)}, bf16[32,2048]{1,0:T(8,128)(2,1)S(1)}, u32[]{:S(2)}, u32[]{:S(2)}) collective-permute-start(bf16[32,2048]{1,0:T(8,128)(2,1)S(1)} %get-tuple-element.783), channel_id=1, source_target_pairs={{0,1},{1,0},{2,3},{3,2},{4,5},{5,4},{6,7},{7,6},{8,9},{9,8},{10,11... | collective-permute-start | bytes 393224 | tf_op jit(solution)/shard_map/ppermute | solution.py:27
  173.0 5.7 %collective-permute-start.70 = (bf16[32,2048]{1,0:T(8,128)(2,1)S(1)}, bf16[32,2048]{1,0:T(8,128)(2,1)S(1)}, u32[]{:S(2)}, u32[]{:S(2)}) collective-permute-start(bf16[32,2048]{1,0:T(8,128)(2,1)S(1)} %get-tuple-element.784), channel_id=1, source_target_pairs={{0,1},{1,0},{2,3},{3,2},{4,5},{5,4},{6,7},{7,6},{8,9},{9,8},{10,11... | collective-permute-start | bytes 393224 | tf_op jit(solution)/shard_map/ppermute | solution.py:27
  (49 other events, 114.2 us)

commit v3 on v2

--- a/solution.py
+++ b/solution.py
@@ -174,7 +174,7 @@
             del self.kept[name]
 
 
-def project(run, cut, tokens, weight, bring=None):
+def project(run, cut, tokens, weight, sent_parts=SENT_PARTS, bring=None):
     count, width = tokens.shape
 
     def kernel(side_ref, tokens_ref, weight_ref, *refs):
@@ -189,10 +189,10 @@
         def _():
             refs[-1][...] = product
 
-    each = count // SENT_PARTS
+    each = count // sent_parts
     *for_other, mine = run.call(
-        kernel, cut.grid, (tokens,), [IN_VMEM], [cut.first(each)] * SENT_PARTS + [cut.second(count)],
-        [shape(each, cut.width)] * SENT_PARTS + [shape(count, cut.width)], use=[weight], bring=bring,
+        kernel, cut.grid, (tokens,), [IN_VMEM], [cut.first(each)] * sent_parts + [cut.second(count)],
+        [shape(each, cut.width)] * sent_parts + [shape(count, cut.width)], use=[weight], bring=bring,
     )
     return for_other, mine
 
@@ -337,7 +337,7 @@
     return local, whole
 
 
-def latents_of(run, cut, mine, other, first, bias, enc_scale):
+def latents_of(run, cut, mine, other, first, bias, enc_scale, sent_parts=SENT_PARTS):
     count = mine.shape[0]
     local, whole = over_own(cut)
 
@@ -348,11 +348,11 @@
         latents_ref[...] = latents
         spread(latents, sent_refs)
 
-    each = count // SENT_PARTS
+    each = count // sent_parts
     latents, *sent = run.call(
         kernel, cut.steps, (mine, other, bias), [local(count, first), local(count, first), whole(1)],
-        [local(count)] + [local(each)] * SENT_PARTS,
-        [shape(count, cut.width)] + [shape(each, cut.width)] * SENT_PARTS,
+        [local(count)] + [local(each)] * sent_parts,
+        [shape(count, cut.width)] + [shape(each, cut.width)] * sent_parts,
     )
     return latents, sent
 
@@ -478,7 +478,6 @@
             return lax.dynamic_slice_in_dim(piece, row * width, width, 1)
 
         pieces = [own_rows(0)]
-        bias, out_bias = handed_on(run, (enc_bias.reshape(1, local_latents), dec_bias.reshape(1, width)))
         cuts = cuts_of(local_latents // 2, (1, 1, 2))
         n_cuts = len(cuts)
         hidden = gate_proj.shape[1]
@@ -490,14 +489,18 @@
             return {(name, i): (enc_weight if name == "enc" else dec_t, cuts[i])}
 
         run.keep(gate=gate_proj, up=up_proj, down=down_proj.T)
-        for i in range(n_cuts):
-            run.bring(piece_of("enc", i))
         pieces.append(own_rows(1))
         chips = []
-        for piece in pieces:
-            received = [beside(part) for part in gate_or_up(run, False, piece, hidden)]
-            chips.append(across(run, *gate_or_up(run, True, piece, hidden, received)))
+
+        def start_layer(part):
+            received = [beside(sent) for sent in gate_or_up(run, False, pieces[part], hidden)]
+            chips.append(across(run, *gate_or_up(run, True, pieces[part], hidden, received)))
+
+        start_layer(0)
+        bias, out_bias = handed_on(run, (enc_bias.reshape(1, local_latents), dec_bias.reshape(1, width)))
+        start_layer(1)
         run.drop("gate", "up")
+        run.bring(piece_of("enc", 0))
 
         def latent_terms(value, between):
             between = list(between)
@@ -525,15 +528,21 @@
         def second_layer():
             open_layer(1)
             close_layer(1)
-
-        layer_terms = latent_terms(layer_parts[0], [lambda: None, second_layer])
+            if n_cuts > 1:
+                run.bring(piece_of("enc", late))
+
+        def more_pieces():
+            for i in early[1:]:
+                run.bring(piece_of("enc", i))
+
+        layer_terms = latent_terms(layer_parts[0], [more_pieces, second_layer])
         run.drop("down")
 
         sums = [[None] * n_cuts for _ in range(parts)]
         backs = [[None] * n_cuts for _ in range(parts)]
 
-        def project_start(part, i, tokens, weight, bring=None):
-            for_other, mine = project(run, cuts[i], tokens, (weight, i), bring)
+        def project_start(part, i, tokens, weight, bring=None, sent_parts=SENT_PARTS):
+            for_other, mine = project(run, cuts[i], tokens, (weight, i), sent_parts, bring)
             return mine, [beside(piece) for piece in for_other]
 
         def project_end(part, which, totals):
@@ -548,7 +557,9 @@
         partials = [None] * parts
 
         def open_latents(part, i):
-            latents_own[part][i], sent = latents_of(run, cuts[i], *sums[part][i], bias, enc_scale)
+            latents_own[part][i], sent = latents_of(
+                run, cuts[i], *sums[part][i], bias, enc_scale, 2 * SENT_PARTS if part and i != late else SENT_PARTS
+            )
             latents_other[part][i] = [beside(piece) for piece in sent]
 
         def add_decoded(part, i, bring=None):
@@ -571,16 +582,16 @@
 
         def encode_first():
             for i in early:
-                held[0][i] = project_start(0, i, features[0], "enc")
-            if early:
-                project_end(0, early, sums)
-            held[0][late] = project_start(0, late, features[0], "enc", piece_of("dec", 0) if early else None)
+                held[0][i] = project_start(0, i, features[0], "enc", sent_parts=2 * SENT_PARTS)
 
         layer_terms = latent_terms(layer_parts[1], [lambda: None, encode_first])
         features.append(added(run, *layer_terms))
+        if early:
+            project_end(0, early, sums)
+        held[0][late] = project_start(0, late, features[0], "enc", piece_of("dec", 0) if early else None)
         project_end(0, [late], sums)
         for i in range(n_cuts):
-            bring = piece_of("dec", i + 1) if i + 1 < late else piece_of("dec", late) if i == late else None
+            bring = piece_of("dec", i + 1) if i + 1 < late else None
             held[1][i] = project_start(1, i, features[1], "enc", bring)
             run.drop(("enc", i))
 
@@ -589,7 +600,9 @@
         for i in early:
             if i == min(1, late - 1):
                 project_end(1, early, sums)
-            add_decoded(0, i)
+            add_decoded(0, i, piece_of("dec", late) if i == 0 else None)
+        if not early:
+            run.bring(piece_of("dec", late))
         open_latents(0, late)
         project_end(1, [late], sums)
         add_decoded(0, late)
@@ -598,14 +611,21 @@
             terms = latent_terms(partials[part], between)
             return residual_grad(run, *terms, out_bias, features[part], dec_scale)
 
-        residuals = [residual_of(0, [lambda i=i: open_latents(1, i) for i in early])]
+        def open_second():
+            for i in early:
+                open_latents(1, i)
+
+        def decode_second():
+            for i in early:
+                add_decoded(1, i)
+
+        residuals = [residual_of(0, [open_second, decode_second])]
         for i in range(n_cuts):
             held[0][i] = project_start(0, i, residuals[0], "dec")
         project_end(0, range(n_cuts), backs)
         open_latents(1, late)
-        for i in range(n_cuts):
-            add_decoded(1, i)
-        residuals.append(residual_of(1, []))
+        add_decoded(1, late)
+        residuals.append(residual_of(1, [lambda: run.bring(piece_of("enc", early[0])) if early else None]))
 
         dec_new = enc_new = residual_t = features_t = None
 
@@ -614,7 +634,7 @@
             rights = [(latents_other[part][i], latents_own[part][i]) for part in range(parts)]
             new = update(
                 run, cuts[i], residual_t, rights, ("dec", i), dec_scale, dec_new, local_latents,
-                bring=piece_of("enc", last_order[k - 1]) if k else None,
+                bring=piece_of("enc", late) if k == min(n_cuts - 2, 1) else None,
             )
             run.drop(("dec", i))
             return new
@@ -624,23 +644,26 @@
             rights = [(grads_other[part][i], grads_own[part][i]) for part in range(parts)]
             new = update(
                 run, cuts[i], features_t, rights, ("enc", i), enc_scale, enc_new, local_latents, bias,
-                bring=piece_of("enc", last_order[-1]) if k == n_cuts - 2 else None,
+                bring=piece_of("enc", early[k + 1]) if k + 1 < len(early) else None,
             )
             run.drop(("enc", i))
             return new
 
+        residual_t = turned(run, residuals)
+        features_t = turned(run, features)
         for i in last_order:
             held[1][i] = project_start(1, i, residuals[1], "dec")
+        dec_new = write_dec(n_cuts - 1)
         project_end(1, [late], backs)
         if early:
             project_end(1, early, backs)
-        residual_t = turned(run, residuals)
-        features_t = turned(run, features)
-        for k in range(n_cuts):
+        for k in range(n_cuts - 1):
             dec_new = write_dec(k)
             if k == 0:
                 for i in last_order:
                     open_grad(0, i)
+        if n_cuts == 1:
+            open_grad(0, late)
         out_bias_new = update_bias(run, out_bias, residuals)
         if n_cuts == 1:
             run.bring(piece_of("enc", late))

time: 182 us -> 173 us (0.951)
  waiting for transfers between devices: 47.1 us -> 29.9 us
  starting transfers between devices: 38.4 us -> 47.4 us
    ppermute x73 -> x81, waiting for transfers between devices: 47.1 us -> 29.9 us  [flip(): return lax.ppermute(value, axis, [(i, i ^ bit) for i in range(size)])]
    ppermute x73 -> x81, starting transfers between devices: 37.1 us -> 46.1 us  [flip(): return lax.ppermute(value, axis, [(i, i ^ bit) for i in range(size)])]
    pallas_call x69 -> x70, Pallas kernels: 91.4 us -> 91.5 us  [call(): pl.pallas_call(within, grid_spec=pltpu.PrefetchScalarGridSpec(num_scalar_...]
  transfers between devices with their start and end apart: 75 -> 83, of which waited for: 31 -> 29; matrix products, arithmetic and copies ran while one was open for 0% -> 0% of each run, Pallas kernels for 47% -> 50%
where the time goes in v3:
time: 173 us
  Pallas kernels  91.5 us (53%)
  starting transfers between devices  47.4 us (27%)
  waiting for transfers between devices  29.9 us (17%)
  local copies, waits for them, and re-layouts  2.73 us (2%)
    pallas_call x70, Pallas kernels, call(): pl.pallas_call(within, grid_spec=pltpu.PrefetchScalarGridSpec(num_scalar_...  91.5 us
    ppermute x81, starting transfers between devices, flip(): return lax.ppermute(value, axis, [(i, i ^ bit) for i in range(size)])  46.1 us
    ppermute x81, waiting for transfers between devices, flip(): return lax.ppermute(value, axis, [(i, i ^ bit) for i in range(size)])  29.9 us
  transfers between devices with their start and end apart: 83, of which 29 were waited for; matrix products, arithmetic and copies ran while one was open for 0% of the time, Pallas kernels for 50%

profile of v3, /device:TPU:0, one launch (start us, length us, event | category | flops | bytes accessed | tf_op | source)
XLA Modules:
  0.0 173.1 jit_solution(8137394410003474579)
XLA Ops:
  3.2 2.3 %shard_map.112 = (f32[8,128]{1,0:T(8,128)S(1)}, bf16[576,1152]{1,0:T(8,128)(2,1)S(1)}, bf16[576,1152]{1,0:T(8,128)(2,1)S(1)}, bf16[576,1152]{1,0:T(8,128)(2,1)S(1)}) custom-call(s32[1]{0:T(128)} %bitcast.side_ref, f32[8,128]{1,0:T(8,128)S(1)} %get-tuple-element.400.refs_0_, bf16[576,1152]{1,0:T(8,128)(2,1)} %refs_1_.1, ...), custom_call_target="tpu_custom_call", output_to_operand_aliasing={{0}: (1, {})} | custom-call | flops 1 | bytes 1 | tf_op jit(solution)/shard_map/pallas_call | solution.py:144
  6.0 4.5 %collective-permute-start.1 = (bf16[32,1152]{1,0:T(8,128)(2,1)S(1)}, bf16[32,1152]{1,0:T(8,128)(2,1)S(1)}, u32[]{:S(2)}, u32[]{:S(2)}) collective-permute-start(bf16[32,1152]{1,0:T(8,128)(2,1)S(1)} %get-tuple-element.409), channel_id=1, source_target_pairs={{0,1},{1,0},{2,3},{3,2},{4,5},{5,4},{6,7},{7,6},{8,9},{9,8},{10,11... | collective-permute-start | bytes 221192 | tf_op jit(solution)/shard_map/ppermute | solution.py:27
  12.1 8.0 %collective-permute-start.3 = (bf16[64,1152]{1,0:T(8,128)(2,1)S(1)}, bf16[64,1152]{1,0:T(8,128)(2,1)S(1)}, u32[]{:S(2)}, u32[]{:S(2)}) collective-permute-start(bf16[64,1152]{1,0:T(8,128)(2,1)S(1)} %get-tuple-element.415.refs_0_), channel_id=1, source_target_pairs={{0,2},{1,3},{2,0},{3,1},{4,6},{5,7},{6,4},{7,5},{8,10},{9,11},{10,... | collective-permute-start | bytes 442376 | tf_op jit(solution)/shard_map/ppermute | solution.py:27
  20.7 1.1 collective-permute-start.5
  23.4 2.4 %shard_map.119 = (bf16[576,1152]{1,0:T(8,128)(2,1)S(1)}, f32[8,128]{1,0:T(8,128)S(1)}, bf16[576,4096]{1,0:T(8,128)(2,1)S(1)}) custom-call(s32[1]{0:T(128)} %bitcast.side_ref, bf16[576,1152]{1,0:T(8,128)(2,1)S(1)} %get-tuple-element.431.refs_0_, f32[8,128]{1,0:T(8,128)S(1)} %get-tuple-element.432.refs_1_, ...), custom_call_target="tpu_custom_call", output_to_operand_aliasing={{0}: (1, {}), {1}: (2, {})} | custom-call | flops 1 | bytes 1 | tf_op jit(solution)/shard_map/pallas_call | solution.py:144
  26.5 4.7 %collective-permute-start.11 = (bf16[64,1152]{1,0:T(8,128)(2,1)S(1)}, bf16[64,1152]{1,0:T(8,128)(2,1)S(1)}, u32[]{:S(2)}, u32[]{:S(2)}) collective-permute-start(bf16[64,1152]{1,0:T(8,128)(2,1)S(1)} %get-tuple-element.451.refs_0_), channel_id=1, source_target_pairs={{0,2},{1,3},{2,0},{3,1},{4,6},{5,7},{6,4},{7,5},{8,10},{9,11},{10,... | collective-permute-start | bytes 442376 | tf_op jit(solution)/shard_map/ppermute | solution.py:27
  31.7 2.4 %shard_map.122 = (bf16[576,1152]{1,0:T(8,128)(2,1)S(1)}, bf16[576,4096]{1,0:T(8,128)(2,1)S(1)}, f32[8,128]{1,0:T(8,128)S(1)}, bf16[576,4096]{1,0:T(8,128)(2,1)S(1)}) custom-call(s32[1]{0:T(128)} %bitcast.side_ref, bf16[576,1152]{1,0:T(8,128)(2,1)S(1)} %get-tuple-element.443.refs_0_, ...), custom_call_target="tpu_custom_call", output_to_operand_aliasing={{0}: (1, {}), {1}: (2, {}), {2}: (3, {})} | custom-call | flops 1 | bytes 1 | tf_op jit(solution)/shard_map/pallas_call | solution.py:144
  34.2 2.0 %collective-permute-done.9.refs_1_ = bf16[64,576]{1,0:T(8,128)(2,1)S(1)} collective-permute-done((bf16[64,576]{1,0:T(8,128)(2,1)S(1)}, bf16[64,576]{1,0:T(8,128)(2,1)S(1)}, u32[]{:S(2)}, u32[]{:S(2)}) %collective-permute-start.9) | collective-permute-done | bytes 73760 | tf_op jit(solution)/shard_map/ppermute | solution.py:27
  38.5 1.4 collective-permute-start.14
  39.9 3.8 %shard_map.126 = (bf16[576,1152]{1,0:T(8,128)(2,1)S(1)}, bf16[576,4096]{1,0:T(8,128)(2,1)S(1)}, bf16[576,4096]{1,0:T(8,128)(2,1)S(1)}, f32[8,128]{1,0:T(8,128)S(1)}, bf16[576,8192]{1,0:T(8,128)(2,1)S(1)}) custom-call(s32[1]{0:T(128)} %bitcast.side_ref, ...), custom_call_target="tpu_custom_call", output_to_operand_aliasing={{0}: (1, {}), {1}: (2, {}), {2}: (3, {}), {3}: (4, {})} | custom-call | flops 1 | bytes 1 | tf_op jit(solution)/shard_map/pallas_call | solution.py:144
  43.8 1.1 collective-permute-done.14.refs_1_
  45.0 1.4 shard_map.129
  46.4 1.2 shard_map.130
  49.6 1.4 collective-permute-done.15.refs_1_
  51.0 1.2 collective-permute-done.19.refs_4_
  52.4 1.4 collective-permute-start.27
  53.8 2.9 %shard_map.133 = (bf16[32,4096]{1,0:T(8,128)(2,1)S(1)}, bf16[32,4096]{1,0:T(8,128)(2,1)S(1)}, bf16[64,4096]{1,0:T(8,128)(2,1)S(1)}, bf16[576,4096]{1,0:T(8,128)(...) custom-call(s32[1]{0:T(128)} %bitcast.side_ref, ...), custom_call_target="tpu_custom_call", output_to_operand_aliasing={{3}: (2, {}), {4}: (3, {}), {5}: (4, {}), {6}: (5, {})} | custom-call | flops 1 | bytes 1 | tf_op jit(solution)/shard_map/pallas_call | solution.py:144
  59.6 2.8 %shard_map.135 = (bf16[32,2048]{1,0:T(8,128)(2,1)S(1)}, bf16[32,2048]{1,0:T(8,128)(2,1)S(1)}, bf16[64,2048]{1,0:T(8,128)(2,1)S(1)}, bf16[576,4096]{1,0:T(8,128)(...) custom-call(s32[1]{0:T(128)} %bitcast.side_ref, ...), custom_call_target="tpu_custom_call", output_to_operand_aliasing={{3}: (2, {}), {4}: (3, {}), {5}: (4, {}), {6}: (5, {}), {7}... | custom-call | flops 1 | bytes 1 | tf_op jit(solution)/shard_map/pallas_call | solution.py:144
  62.4 1.2 shard_map.136
  63.6 2.6 %shard_map.137 = (bf16[32,4096]{1,0:T(8,128)(2,1)S(1)}, bf16[32,4096]{1,0:T(8,128)(2,1)S(1)}, bf16[64,4096]{1,0:T(8,128)(2,1)S(1)}, bf16[576,8192]{1,0:T(8,128)(...) custom-call(s32[1]{0:T(128)} %bitcast.side_ref, ...), custom_call_target="tpu_custom_call", output_to_operand_aliasing={{3}: (2, {}), {4}: (3, {}), {5}: (4, {}), {6}: (5, {})} | custom-call | flops 1 | bytes 1 | tf_op jit(solution)/shard_map/pallas_call | solution.py:144
  70.0 3.8 %shard_map.140 = (f32[64,576]{1,0:T(8,128)S(1)}, bf16[576,4096]{1,0:T(8,128)(2,1)S(1)}, bf16[576,4096]{1,0:T(8,128)(2,1)S(1)}, f32[8,128]{1,0:T(8,128)S(1)}, bf16[576,8192]{1,0:T(8,128)(2,1)S(1)}) custom-call(s32[1]{0:T(128)} %bitcast.side_ref, ...), custom_call_target="tpu_custom_call", output_to_operand_aliasing={{1}: (4, {}), {2}: (5, {}), {3}: (6, {})} | custom-call | flops 1 | bytes 1 | tf_op jit(solution)/shard_map/pallas_call | solution.py:144
  74.0 1.4 collective-permute-start.41
  76.9 1.7 shard_map.142
  80.4 1.1 collective-permute-start.51
  81.7 3.6 %shard_map.145 = (bf16[64,576]{1,0:T(8,128)(2,1)S(1)}, bf16[576,4096]{1,0:T(8,128)(2,1)S(1)}, bf16[576,4096]{1,0:T(8,128)(2,1)S(1)}, bf16[576,8192]{1,0:T(8,128)(2,1)S(1)}, f32[8,128]{1,0:T(8,128)S(1)}) custom-call(s32[1]{0:T(128)} %bitcast.side_ref, ...), custom_call_target="tpu_custom_call", output_to_operand_aliasing={{1}: (5, {}), {2}: (6, {}), {3}: (7, {}), {4}: (8, {})} | custom-call | flops 1 | bytes 1 | tf_op jit(solution)/shard_map/pallas_call | solution.py:144
  85.9 3.8 %collective-permute-done.41.refs_1_ = bf16[64,4096]{1,0:T(8,128)(2,1)S(1)} collective-permute-done((bf16[64,4096]{1,0:T(8,128)(2,1)S(1)}, bf16[64,4096]{1,0:T(8,128)(2,1)S(1)}, u32[]{:S(2)}, u32[]{:S(2)}) %collective-permute-start.41) | collective-permute-done | bytes 524320 | tf_op jit(solution)/shard_map/ppermute | solution.py:27
  91.8 1.4 collective-permute-start.42
  93.8 1.7 shard_map.149
  95.6 1.7 %shard_map.150 = (f32[64,576]{1,0:T(8,128)S(1)}, bf16[576,4096]{1,0:T(8,128)(2,1)S(1)}, bf16[576,4096]{1,0:T(8,128)(2,1)S(1)}, bf16[576,8192]{1,0:T(8,128)(2,1)S(1)}, f32[8,128]{1,0:T(8,128)S(1)}) custom-call(s32[1]{0:T(128)} %bitcast.side_ref, ...), custom_call_target="tpu_custom_call", output_to_operand_aliasing={{1}: (7, {}), {2}: (8, {}), {3}: (9, {}), {4}: (10, {})} | custom-call | flops 1 | bytes 1 | tf_op jit(solution)/shard_map/pallas_call | solution.py:144
  97.3 1.9 %collective-permute-done.42.refs_1_ = bf16[64,576]{1,0:T(8,128)(2,1)S(1)} collective-permute-done((bf16[64,576]{1,0:T(8,128)(2,1)S(1)}, bf16[64,576]{1,0:T(8,128)(2,1)S(1)}, u32[]{:S(2)}, u32[]{:S(2)}) %collective-permute-start.42) | collective-permute-done | bytes 73760 | tf_op jit(solution)/shard_map/ppermute | solution.py:27
  99.3 1.2 shard_map.152
  100.6 1.4 shard_map.153
  102.6 2.5 %shard_map.154 = (bf16[32,4096]{1,0:T(8,128)(2,1)S(1)}, bf16[32,4096]{1,0:T(8,128)(2,1)S(1)}, bf16[64,4096]{1,0:T(8,128)(2,1)S(1)}, bf16[576,4096]{1,0:T(8,128)(...) custom-call(s32[1]{0:T(128)} %bitcast.side_ref, ...), custom_call_target="tpu_custom_call", output_to_operand_aliasing={{3}: (2, {}), {4}: (3, {}), {5}: (4, {}), {6}: (5, {})} | custom-call | flops 1 | bytes 1 | tf_op jit(solution)/shard_map/pallas_call | solution.py:144
  110.7 3.6 %shard_map.157 = (bf16[64,576]{1,0:T(8,128)(2,1)S(1)}, bf16[576,4096]{1,0:T(8,128)(2,1)S(1)}, bf16[576,4096]{1,0:T(8,128)(2,1)S(1)}, bf16[576,8192]{1,0:T(8,128)(2,1)S(1)}, f32[8,128]{1,0:T(8,128)S(1)}) custom-call(s32[1]{0:T(128)} %bitcast.side_ref, ...), custom_call_target="tpu_custom_call", output_to_operand_aliasing={{1}: (5, {}), {2}: (6, {}), {3}: (7, {}), {4}: (8, {})} | custom-call | flops 1 | bytes 1 | tf_op jit(solution)/shard_map/pallas_call | solution.py:144
  114.4 2.4 %shard_map.158 = (bf16[576,4096]{1,0:T(8,128)(2,1)S(1)}, bf16[576,4096]{1,0:T(8,128)(2,1)S(1)}, bf16[576,8192]{1,0:T(8,128)(2,1)S(1)}, f32[8,128]{1,0:T(8,128)S(1)}, bf16[576,4096]{1,0:T(8,128)(2,1)S(1)}) custom-call(s32[1]{0:T(128)} %bitcast.side_ref, ...), custom_call_target="tpu_custom_call", output_to_operand_aliasing={{0}: (1, {}), {1}: (2, {}), {2}: (3, {}), {3}: (4, {})} | custom-call | flops 1 | bytes 1 | tf_op jit(solution)/shard_map/pallas_call | solution.py:144
  116.8 2.1 %collective-permute-done.60.refs_1_ = bf16[64,576]{1,0:T(8,128)(2,1)S(1)} collective-permute-done((bf16[64,576]{1,0:T(8,128)(2,1)S(1)}, bf16[64,576]{1,0:T(8,128)(2,1)S(1)}, u32[]{:S(2)}, u32[]{:S(2)}) %collective-permute-start.60) | collective-permute-done | bytes 73760 | tf_op jit(solution)/shard_map/ppermute | solution.py:27
  119.7 5.6 %collective-permute-done.61.refs_1_ = bf16[64,576]{1,0:T(8,128)(2,1)S(1)} collective-permute-done((bf16[64,576]{1,0:T(8,128)(2,1)S(1)}, bf16[64,576]{1,0:T(8,128)(2,1)S(1)}, u32[]{:S(2)}, u32[]{:S(2)}) %collective-permute-start.61) | collective-permute-done | bytes 73760 | tf_op jit(solution)/shard_map/ppermute | solution.py:27
  125.5 2.6 %shard_map.163 = (bf16[32,4096]{1,0:T(8,128)(2,1)S(1)}, bf16[32,4096]{1,0:T(8,128)(2,1)S(1)}, bf16[64,4096]{1,0:T(8,128)(2,1)S(1)}, bf16[576,4096]{1,0:T(8,128)(...) custom-call(s32[1]{0:T(128)} %bitcast.side_ref, ...), custom_call_target="tpu_custom_call", output_to_operand_aliasing={{3}: (2, {}), {4}: (3, {}), {5}: (4, {}), {6}: (5, {}), {7}... | custom-call | flops 1 | bytes 1 | tf_op jit(solution)/shard_map/pallas_call | solution.py:144
  128.7 1.2 shard_map.164
  129.9 1.2 shard_map.165
  131.2 3.1 %shard_map.166 = (bf16[576,16384]{1,0:T(8,128)(2,1)}, bf16[576,4096]{1,0:T(8,128)(2,1)S(1)}, bf16[576,4096]{1,0:T(8,128)(2,1)S(1)}, bf16[576,8192]{1,0:T(8,128)(...) custom-call(s32[1]{0:T(128)} %bitcast.side_ref, ...), custom_call_target="tpu_custom_call", output_to_operand_aliasing={{1}: (10, {}), {2}: (11, {}), {3}: (12, {}), {4}: (13, {}),... | custom-call | flops 1 | bytes 1 | tf_op jit(solution)/shard_map/pallas_call | solution.py:144
  134.4 1.1 collective-permute-start.74
  138.3 1.1 collective-permute-start.71
  139.4 5.4 %shard_map.169 = (bf16[576,16384]{1,0:T(8,128)(2,1)}, bf16[576,4096]{1,0:T(8,128)(2,1)S(1)}, bf16[576,8192]{1,0:T(8,128)(2,1)S(1)}, bf16[576,4096]{1,0:T(8,128)(2,1)S(1)}, f32[8,128]{1,0:T(8,128)S(1)}) custom-call(s32[1]{0:T(128)} %bitcast.side_ref, ...), custom_call_target="tpu_custom_call", output_to_operand_aliasing={{0}: (8, {}), {1}: (9, {}), {2}: (10, {}), {3}: (11, {}), {... | custom-call | flops 1 | bytes 1 | tf_op jit(solution)/shard_map/pallas_call | solution.py:144
  147.5 6.5 %shard_map.173 = (bf16[576,16384]{1,0:T(8,128)(2,1)}, bf16[576,4096]{1,0:T(8,128)(2,1)S(1)}, bf16[576,4096]{1,0:T(8,128)(2,1)S(1)}, f32[8,128]{1,0:T(8,128)S(1)}, bf16[576,8192]{1,0:T(8,128)(2,1)S(1)}) custom-call(s32[1]{0:T(128)} %bitcast.side_ref, ...), custom_call_target="tpu_custom_call", output_to_operand_aliasing={{0}: (10, {}), {1}: (11, {}), {2}: (12, {}), {3}: (13, {})} | custom-call | flops 1 | bytes 1 | tf_op jit(solution)/shard_map/pallas_call | solution.py:144
  157.3 7.3 %shard_map.176 = (bf16[576,16384]{1,0:T(8,128)(2,1)}, f32[1,16384]{1,0:T(1,128)}, bf16[576,4096]{1,0:T(8,128)(2,1)S(1)}, bf16[576,8192]{1,0:T(8,128)(2,1)S(1)}, ...) custom-call(s32[1]{0:T(128)} %bitcast.side_ref, ...), custom_call_target="tpu_custom_call", output_to_operand_aliasing={{2}: (9, {}), {3}: (10, {}), {4}: (11, {})} | custom-call | flops 1 | bytes 1 | tf_op jit(solution)/shard_map/pallas_call | solution.py:144
  166.8 3.1 %shard_map.179 = (bf16[576,16384]{1,0:T(8,128)(2,1)}, f32[1,16384]{1,0:T(1,128)}, bf16[576,4096]{1,0:T(8,128)(2,1)S(1)}, bf16[576,4096]{1,0:T(8,128)(2,1)S(1)}, f32[8,128]{1,0:T(8,128)S(1)}) custom-call(s32[1]{0:T(128)} %bitcast.side_ref, ...), custom_call_target="tpu_custom_call", output_to_operand_aliasing={{0}: (9, {}), {1}: (10, {}), {2}: (11, {}), {3}: (12, {}), ... | custom-call | flops 1 | bytes 1 | tf_op jit(solution)/shard_map/pallas_call | solution.py:144
  169.9 3.2 %shard_map.180 = (bf16[576,16384]{1,0:T(8,128)(2,1)}, f32[1,16384]{1,0:T(1,128)}, bf16[576,4096]{1,0:T(8,128)(2,1)S(1)}, f32[8,128]{1,0:T(8,128)S(1)}) custom-call(s32[1]{0:T(128)} %bitcast.side_ref, bf16[576,128]{1,0:T(8,128)(2,1)S(1)} %get-tuple-element.688.refs_0_, ...), custom_call_target="tpu_custom_call", output_to_operand_aliasing={{0}: (9, {}), {1}: (10, {}), {2}: (11, {}), {3}: (12, {})} | custom-call | flops 1 | bytes 1 | tf_op jit(solution)/shard_map/pallas_call | solution.py:144
  (219 shorter events, 45.2 us)
Async XLA Ops:
  2.5 3.1 %collective-permute-start = (bf16[64,576]{1,0:T(8,128)(2,1)S(1)}, bf16[64,576]{1,0:T(8,128)(2,1)S(1)}, u32[]{:S(2)}, u32[]{:S(2)}) collective-permute-start(bf16[64,576]{1,0:T(8,128)(2,1)S(1)} %get-tuple-element.399), channel_id=1, source_target_pairs={{0,0},{1,4},{2,8},{3,12},{4,1},{5,5},{6,9},{7,13},{8,2},{9,6},{10,... | collective-permute-start | bytes 221192 | tf_op jit(solution)/shard_map/ppermute | solution.py:476
  6.0 5.4 %collective-permute-start.1 = (bf16[32,1152]{1,0:T(8,128)(2,1)S(1)}, bf16[32,1152]{1,0:T(8,128)(2,1)S(1)}, u32[]{:S(2)}, u32[]{:S(2)}) collective-permute-start(bf16[32,1152]{1,0:T(8,128)(2,1)S(1)} %get-tuple-element.409), channel_id=1, source_target_pairs={{0,1},{1,0},{2,3},{3,2},{4,5},{5,4},{6,7},{7,6},{8,9},{9,8},{10,11... | collective-permute-start | bytes 221192 | tf_op jit(solution)/shard_map/ppermute | solution.py:27
  10.5 9.6 %collective-permute-start.4 = (bf16[64,576]{1,0:T(8,128)(2,1)S(1)}, bf16[64,576]{1,0:T(8,128)(2,1)S(1)}, u32[]{:S(2)}, u32[]{:S(2)}) collective-permute-start(bf16[64,576]{1,0:T(8,128)(2,1)S(1)} %get-tuple-element.416), channel_id=1, source_target_pairs={{0,0},{1,4},{2,8},{3,12},{4,1},{5,5},{6,9},{7,13},{8,2},{9,6},{10,... | collective-permute-start | bytes 221192 | tf_op jit(solution)/shard_map/ppermute | solution.py:476
  12.1 13.7 %collective-permute-start.3 = (bf16[64,1152]{1,0:T(8,128)(2,1)S(1)}, bf16[64,1152]{1,0:T(8,128)(2,1)S(1)}, u32[]{:S(2)}, u32[]{:S(2)}) collective-permute-start(bf16[64,1152]{1,0:T(8,128)(2,1)S(1)} %get-tuple-element.415.refs_0_), channel_id=1, source_target_pairs={{0,2},{1,3},{2,0},{3,1},{4,6},{5,7},{6,4},{7,5},{8,10},{9,11},{10,... | collective-permute-start | bytes 442376 | tf_op jit(solution)/shard_map/ppermute | solution.py:27
  25.9 5.2 %collective-permute-start.7 = (f32[32,1152]{1,0:T(8,128)S(1)}, f32[32,1152]{1,0:T(8,128)S(1)}, u32[]{:S(2)}, u32[]{:S(2)}) collective-permute-start(f32[32,1152]{1,0:T(8,128)S(1)} %get-tuple-element.437), channel_id=1, source_target_pairs={{0,1},{1,0},{2,3},{3,2},{4,5},{5,4},{6,7},{7,6},{8,9},{9,8},{10,11... | collective-permute-start | bytes 442376 | tf_op jit(solution)/shard_map/ppermute | solution.py:27
  26.3 4.8 %collective-permute-start.8 = (f32[32,1152]{1,0:T(8,128)S(1)}, f32[32,1152]{1,0:T(8,128)S(1)}, u32[]{:S(2)}, u32[]{:S(2)}) collective-permute-start(f32[32,1152]{1,0:T(8,128)S(1)} %get-tuple-element.438), channel_id=1, source_target_pairs={{0,1},{1,0},{2,3},{3,2},{4,5},{5,4},{6,7},{7,6},{8,9},{9,8},{10,11... | collective-permute-start | bytes 442376 | tf_op jit(solution)/shard_map/ppermute | solution.py:27
  26.5 9.8 %collective-permute-start.11 = (bf16[64,1152]{1,0:T(8,128)(2,1)S(1)}, bf16[64,1152]{1,0:T(8,128)(2,1)S(1)}, u32[]{:S(2)}, u32[]{:S(2)}) collective-permute-start(bf16[64,1152]{1,0:T(8,128)(2,1)S(1)} %get-tuple-element.451.refs_0_), channel_id=1, source_target_pairs={{0,2},{1,3},{2,0},{3,1},{4,6},{5,7},{6,4},{7,5},{8,10},{9,11},{10,... | collective-permute-start | bytes 442376 | tf_op jit(solution)/shard_map/ppermute | solution.py:27
  31.7 4.5 %collective-permute-start.9 = (bf16[64,576]{1,0:T(8,128)(2,1)S(1)}, bf16[64,576]{1,0:T(8,128)(2,1)S(1)}, u32[]{:S(2)}, u32[]{:S(2)}) collective-permute-start(bf16[64,576]{1,0:T(8,128)(2,1)S(1)} %get-tuple-element.442.refs_0_), channel_id=1, source_target_pairs={{0,4},{4,0},{8,12},{12,8},{1,5},{5,1},{9,13},{13,9},{2,6},{6,2},{1... | collective-permute-start | bytes 221192 | tf_op jit(solution)/shard_map/ppermute | solution.py:27
  36.8 6.9 %collective-permute-start.10 = (bf16[64,576]{1,0:T(8,128)(2,1)S(1)}, bf16[64,576]{1,0:T(8,128)(2,1)S(1)}, u32[]{:S(2)}, u32[]{:S(2)}) collective-permute-start(bf16[64,576]{1,0:T(8,128)(2,1)S(1)} %get-tuple-element.450.refs_0_), channel_id=1, source_target_pairs={{0,8},{4,12},{8,0},{12,4},{1,9},{5,13},{9,1},{13,5},{2,10},{6,14},... | collective-permute-start | bytes 221192 | tf_op jit(solution)/shard_map/ppermute | solution.py:27
  38.5 6.4 %collective-permute-start.14 = (bf16[64,576]{1,0:T(8,128)(2,1)S(1)}, bf16[64,576]{1,0:T(8,128)(2,1)S(1)}, u32[]{:S(2)}, u32[]{:S(2)}) collective-permute-start(bf16[64,576]{1,0:T(8,128)(2,1)S(1)} %get-tuple-element.472.refs_0_), channel_id=1, source_target_pairs={{0,4},{4,0},{8,12},{12,8},{1,5},{5,1},{9,13},{13,9},{2,6},{6,2},{1... | collective-permute-start | bytes 221192 | tf_op jit(solution)/shard_map/ppermute | solution.py:27
  44.9 6.1 %collective-permute-start.15 = (bf16[64,576]{1,0:T(8,128)(2,1)S(1)}, bf16[64,576]{1,0:T(8,128)(2,1)S(1)}, u32[]{:S(2)}, u32[]{:S(2)}) collective-permute-start(bf16[64,576]{1,0:T(8,128)(2,1)S(1)} %get-tuple-element.477.refs_0_), channel_id=1, source_target_pairs={{0,8},{4,12},{8,0},{12,4},{1,9},{5,13},{9,1},{13,5},{2,10},{6,14},... | collective-permute-start | bytes 221192 | tf_op jit(solution)/shard_map/ppermute | solution.py:27
  48.3 2.7 %collective-permute-start.23 = (bf16[16,2048]{1,0:T(8,128)(2,1)S(1)}, bf16[16,2048]{1,0:T(8,128)(2,1)S(1)}, u32[]{:S(2)}, u32[]{:S(2)}) collective-permute-start(bf16[16,2048]{1,0:T(8,128)(2,1)S(1)} %get-tuple-element.500), channel_id=1, source_target_pairs={{0,1},{1,0},{2,3},{3,2},{4,5},{5,4},{6,7},{7,6},{8,9},{9,8},{10,11... | collective-permute-start | bytes 196616 | tf_op jit(solution)/shard_map/ppermute | solution.py:27
  48.9 2.1 %collective-permute-start.16 = (bf16[16,2048]{1,0:T(8,128)(2,1)S(1)}, bf16[16,2048]{1,0:T(8,128)(2,1)S(1)}, u32[]{:S(2)}, u32[]{:S(2)}) collective-permute-start(bf16[16,2048]{1,0:T(8,128)(2,1)S(1)} %get-tuple-element.492), channel_id=1, source_target_pairs={{0,1},{1,0},{2,3},{3,2},{4,5},{5,4},{6,7},{7,6},{8,9},{9,8},{10,11... | collective-permute-start | bytes 196616 | tf_op jit(solution)/shard_map/ppermute | solution.py:27
  52.4 14.8 %collective-permute-start.27 = (bf16[64,4096]{1,0:T(8,128)(2,1)S(1)}, bf16[64,4096]{1,0:T(8,128)(2,1)S(1)}, u32[]{:S(2)}, u32[]{:S(2)}) collective-permute-start(bf16[64,4096]{1,0:T(8,128)(2,1)S(1)} %get-tuple-element.519.refs_0_), channel_id=1, source_target_pairs={{0,2},{1,3},{2,0},{3,1},{4,6},{5,7},{6,4},{7,5},{8,10},{9,11},{10,... | collective-permute-start | bytes 1572872 | tf_op jit(solution)/shard_map/ppermute | solution.py:27
  58.8 19.9 %collective-permute-start.26 = (bf16[64,4096]{1,0:T(8,128)(2,1)S(1)}, bf16[64,4096]{1,0:T(8,128)(2,1)S(1)}, u32[]{:S(2)}, u32[]{:S(2)}) collective-permute-start(bf16[64,4096]{1,0:T(8,128)(2,1)S(1)} %get-tuple-element.517.refs_0_), channel_id=1, source_target_pairs={{0,2},{1,3},{2,0},{3,1},{4,6},{5,7},{6,4},{7,5},{8,10},{9,11},{10,... | collective-permute-start | bytes 1572872 | tf_op jit(solution)/shard_map/ppermute | solution.py:27
  68.2 5.6 %collective-permute-start.34 = (bf16[32,2048]{1,0:T(8,128)(2,1)S(1)}, bf16[32,2048]{1,0:T(8,128)(2,1)S(1)}, u32[]{:S(2)}, u32[]{:S(2)}) collective-permute-start(bf16[32,2048]{1,0:T(8,128)(2,1)S(1)} %get-tuple-element.554), channel_id=1, source_target_pairs={{0,1},{1,0},{2,3},{3,2},{4,5},{5,4},{6,7},{7,6},{8,9},{9,8},{10,11... | collective-permute-start | bytes 393224 | tf_op jit(solution)/shard_map/ppermute | solution.py:27
  68.3 5.5 %collective-permute-start.35 = (bf16[32,2048]{1,0:T(8,128)(2,1)S(1)}, bf16[32,2048]{1,0:T(8,128)(2,1)S(1)}, u32[]{:S(2)}, u32[]{:S(2)}) collective-permute-start(bf16[32,2048]{1,0:T(8,128)(2,1)S(1)} %get-tuple-element.555), channel_id=1, source_target_pairs={{0,1},{1,0},{2,3},{3,2},{4,5},{5,4},{6,7},{7,6},{8,9},{9,8},{10,11... | collective-permute-start | bytes 393224 | tf_op jit(solution)/shard_map/ppermute | solution.py:27
  69.0 4.8 %collective-permute-start.32 = (bf16[32,2048]{1,0:T(8,128)(2,1)S(1)}, bf16[32,2048]{1,0:T(8,128)(2,1)S(1)}, u32[]{:S(2)}, u32[]{:S(2)}) collective-permute-start(bf16[32,2048]{1,0:T(8,128)(2,1)S(1)} %get-tuple-element.551), channel_id=1, source_target_pairs={{0,1},{1,0},{2,3},{3,2},{4,5},{5,4},{6,7},{7,6},{8,9},{9,8},{10,11... | collective-permute-start | bytes 393224 | tf_op jit(solution)/shard_map/ppermute | solution.py:27
  69.2 4.6 %collective-permute-start.33 = (bf16[32,2048]{1,0:T(8,128)(2,1)S(1)}, bf16[32,2048]{1,0:T(8,128)(2,1)S(1)}, u32[]{:S(2)}, u32[]{:S(2)}) collective-permute-start(bf16[32,2048]{1,0:T(8,128)(2,1)S(1)} %get-tuple-element.552), channel_id=1, source_target_pairs={{0,1},{1,0},{2,3},{3,2},{4,5},{5,4},{6,7},{7,6},{8,9},{9,8},{10,11... | collective-permute-start | bytes 393224 | tf_op jit(solution)/shard_map/ppermute | solution.py:27
  74.0 15.7 %collective-permute-start.41 = (bf16[64,4096]{1,0:T(8,128)(2,1)S(1)}, bf16[64,4096]{1,0:T(8,128)(2,1)S(1)}, u32[]{:S(2)}, u32[]{:S(2)}) collective-permute-start(bf16[64,4096]{1,0:T(8,128)(2,1)S(1)} %get-tuple-element.584.refs_0_), channel_id=1, source_target_pairs={{0,2},{1,3},{2,0},{3,1},{4,6},{5,7},{6,4},{7,5},{8,10},{9,11},{10,... | collective-permute-start | bytes 1572872 | tf_op jit(solution)/shard_map/ppermute | solution.py:27
  75.9 4.4 %collective-permute-start.38 = (bf16[32,4096]{1,0:T(8,128)(2,1)S(1)}, bf16[32,4096]{1,0:T(8,128)(2,1)S(1)}, u32[]{:S(2)}, u32[]{:S(2)}) collective-permute-start(bf16[32,4096]{1,0:T(8,128)(2,1)S(1)} %get-tuple-element.573), channel_id=1, source_target_pairs={{0,1},{1,0},{2,3},{3,2},{4,5},{5,4},{6,7},{7,6},{8,9},{9,8},{10,11... | collective-permute-start | bytes 786440 | tf_op jit(solution)/shard_map/ppermute | solution.py:27
  76.7 3.5 %collective-permute-start.39 = (bf16[32,4096]{1,0:T(8,128)(2,1)S(1)}, bf16[32,4096]{1,0:T(8,128)(2,1)S(1)}, u32[]{:S(2)}, u32[]{:S(2)}) collective-permute-start(bf16[32,4096]{1,0:T(8,128)(2,1)S(1)} %get-tuple-element.574), channel_id=1, source_target_pairs={{0,1},{1,0},{2,3},{3,2},{4,5},{5,4},{6,7},{7,6},{8,9},{9,8},{10,11... | collective-permute-start | bytes 786440 | tf_op jit(solution)/shard_map/ppermute | solution.py:27
  80.4 27.4 %collective-permute-start.51 = (bf16[64,4096]{1,0:T(8,128)(2,1)S(1)}, bf16[64,4096]{1,0:T(8,128)(2,1)S(1)}, u32[]{:S(2)}, u32[]{:S(2)}) collective-permute-start(bf16[64,4096]{1,0:T(8,128)(2,1)S(1)} %get-tuple-element.623.refs_0_), channel_id=1, source_target_pairs={{0,2},{1,3},{2,0},{3,1},{4,6},{5,7},{6,4},{7,5},{8,10},{9,11},{10,... | collective-permute-start | bytes 1572872 | tf_op jit(solution)/shard_map/ppermute | solution.py:27
  85.2 5.9 %collective-permute-start.40 = (bf16[64,576]{1,0:T(8,128)(2,1)S(1)}, bf16[64,576]{1,0:T(8,128)(2,1)S(1)}, u32[]{:S(2)}, u32[]{:S(2)}) collective-permute-start(bf16[64,576]{1,0:T(8,128)(2,1)S(1)} %get-tuple-element.583.refs_0_), channel_id=1, source_target_pairs={{0,4},{4,0},{8,12},{12,8},{1,5},{5,1},{9,13},{13,9},{2,6},{6,2},{1... | collective-permute-start | bytes 221192 | tf_op jit(solution)/shard_map/ppermute | solution.py:27
  90.7 2.5 %collective-permute-start.49 = (bf16[16,2048]{1,0:T(8,128)(2,1)S(1)}, bf16[16,2048]{1,0:T(8,128)(2,1)S(1)}, u32[]{:S(2)}, u32[]{:S(2)}) collective-permute-start(bf16[16,2048]{1,0:T(8,128)(2,1)S(1)} %get-tuple-element.606), channel_id=1, source_target_pairs={{0,1},{1,0},{2,3},{3,2},{4,5},{5,4},{6,7},{7,6},{8,9},{9,8},{10,11... | collective-permute-start | bytes 196616 | tf_op jit(solution)/shard_map/ppermute | solution.py:27
  91.1 2.2 %collective-permute-start.50 = (bf16[16,2048]{1,0:T(8,128)(2,1)S(1)}, bf16[16,2048]{1,0:T(8,128)(2,1)S(1)}, u32[]{:S(2)}, u32[]{:S(2)}) collective-permute-start(bf16[16,2048]{1,0:T(8,128)(2,1)S(1)} %get-tuple-element.607), channel_id=1, source_target_pairs={{0,1},{1,0},{2,3},{3,2},{4,5},{5,4},{6,7},{7,6},{8,9},{9,8},{10,11... | collective-permute-start | bytes 196616 | tf_op jit(solution)/shard_map/ppermute | solution.py:27
  91.8 7.5 %collective-permute-start.42 = (bf16[64,576]{1,0:T(8,128)(2,1)S(1)}, bf16[64,576]{1,0:T(8,128)(2,1)S(1)}, u32[]{:S(2)}, u32[]{:S(2)}) collective-permute-start(bf16[64,576]{1,0:T(8,128)(2,1)S(1)} %get-tuple-element.597.refs_0_), channel_id=1, source_target_pairs={{0,8},{4,12},{8,0},{12,4},{1,9},{5,13},{9,1},{13,5},{2,10},{6,14},... | collective-permute-start | bytes 221192 | tf_op jit(solution)/shard_map/ppermute | solution.py:27
  93.1 2.4 %collective-permute-start.44 = (bf16[16,2048]{1,0:T(8,128)(2,1)S(1)}, bf16[16,2048]{1,0:T(8,128)(2,1)S(1)}, u32[]{:S(2)}, u32[]{:S(2)}) collective-permute-start(bf16[16,2048]{1,0:T(8,128)(2,1)S(1)} %get-tuple-element.600), channel_id=1, source_target_pairs={{0,1},{1,0},{2,3},{3,2},{4,5},{5,4},{6,7},{7,6},{8,9},{9,8},{10,11... | collective-permute-start | bytes 196616 | tf_op jit(solution)/shard_map/ppermute | solution.py:27
  93.3 2.3 %collective-permute-start.45 = (bf16[16,2048]{1,0:T(8,128)(2,1)S(1)}, bf16[16,2048]{1,0:T(8,128)(2,1)S(1)}, u32[]{:S(2)}, u32[]{:S(2)}) collective-permute-start(bf16[16,2048]{1,0:T(8,128)(2,1)S(1)} %get-tuple-element.601), channel_id=1, source_target_pairs={{0,1},{1,0},{2,3},{3,2},{4,5},{5,4},{6,7},{7,6},{8,9},{9,8},{10,11... | collective-permute-start | bytes 196616 | tf_op jit(solution)/shard_map/ppermute | solution.py:27
  102.0 3.7 %collective-permute-start.54 = (bf16[32,2048]{1,0:T(8,128)(2,1)S(1)}, bf16[32,2048]{1,0:T(8,128)(2,1)S(1)}, u32[]{:S(2)}, u32[]{:S(2)}) collective-permute-start(bf16[32,2048]{1,0:T(8,128)(2,1)S(1)} %get-tuple-element.636), channel_id=1, source_target_pairs={{0,1},{1,0},{2,3},{3,2},{4,5},{5,4},{6,7},{7,6},{8,9},{9,8},{10,11... | collective-permute-start | bytes 393224 | tf_op jit(solution)/shard_map/ppermute | solution.py:27
  102.1 3.7 %collective-permute-start.55 = (bf16[32,2048]{1,0:T(8,128)(2,1)S(1)}, bf16[32,2048]{1,0:T(8,128)(2,1)S(1)}, u32[]{:S(2)}, u32[]{:S(2)}) collective-permute-start(bf16[32,2048]{1,0:T(8,128)(2,1)S(1)} %get-tuple-element.637), channel_id=1, source_target_pairs={{0,1},{1,0},{2,3},{3,2},{4,5},{5,4},{6,7},{7,6},{8,9},{9,8},{10,11... | collective-permute-start | bytes 393224 | tf_op jit(solution)/shard_map/ppermute | solution.py:27
  105.1 2.4 %collective-permute-start.56 = (bf16[32,4096]{1,0:T(8,128)(2,1)S(1)}, bf16[32,4096]{1,0:T(8,128)(2,1)S(1)}, u32[]{:S(2)}, u32[]{:S(2)}) collective-permute-start(bf16[32,4096]{1,0:T(8,128)(2,1)S(1)} %get-tuple-element.643), channel_id=1, source_target_pairs={{0,1},{1,0},{2,3},{3,2},{4,5},{5,4},{6,7},{7,6},{8,9},{9,8},{10,11... | collective-permute-start | bytes 786440 | tf_op jit(solution)/shard_map/ppermute | solution.py:27
  105.3 2.2 %collective-permute-start.57 = (bf16[32,4096]{1,0:T(8,128)(2,1)S(1)}, bf16[32,4096]{1,0:T(8,128)(2,1)S(1)}, u32[]{:S(2)}, u32[]{:S(2)}) collective-permute-start(bf16[32,4096]{1,0:T(8,128)(2,1)S(1)} %get-tuple-element.644), channel_id=1, source_target_pairs={{0,1},{1,0},{2,3},{3,2},{4,5},{5,4},{6,7},{7,6},{8,9},{9,8},{10,11... | collective-permute-start | bytes 786440 | tf_op jit(solution)/shard_map/ppermute | solution.py:27
  109.3 35.5 %collective-permute-start.62 = (bf16[64,8192]{1,0:T(8,128)(2,1)S(1)}, bf16[64,8192]{1,0:T(8,128)(2,1)S(1)}, u32[]{:S(2)}, u32[]{:S(2)}) collective-permute-start(bf16[64,8192]{1,0:T(8,128)(2,1)S(1)} %get-tuple-element.689.refs_3_), channel_id=1, source_target_pairs={{0,2},{1,3},{2,0},{3,1},{4,6},{5,7},{6,4},{7,5},{8,10},{9,11},{10,... | collective-permute-start | bytes 3145736 | tf_op jit(solution)/shard_map/ppermute | solution.py:27
  114.3 4.6 %collective-permute-start.60 = (bf16[64,576]{1,0:T(8,128)(2,1)S(1)}, bf16[64,576]{1,0:T(8,128)(2,1)S(1)}, u32[]{:S(2)}, u32[]{:S(2)}) collective-permute-start(bf16[64,576]{1,0:T(8,128)(2,1)S(1)} %get-tuple-element.661.refs_0_), channel_id=1, source_target_pairs={{0,4},{4,0},{8,12},{12,8},{1,5},{5,1},{9,13},{13,9},{2,6},{6,2},{1... | collective-permute-start | bytes 221192 | tf_op jit(solution)/shard_map/ppermute | solution.py:27
  118.9 6.4 %collective-permute-start.61 = (bf16[64,576]{1,0:T(8,128)(2,1)S(1)}, bf16[64,576]{1,0:T(8,128)(2,1)S(1)}, u32[]{:S(2)}, u32[]{:S(2)}) collective-permute-start(bf16[64,576]{1,0:T(8,128)(2,1)S(1)} %get-tuple-element.671.refs_0_), channel_id=1, source_target_pairs={{0,8},{4,12},{8,0},{12,4},{1,9},{5,13},{9,1},{13,5},{2,10},{6,14},... | collective-permute-start | bytes 221192 | tf_op jit(solution)/shard_map/ppermute | solution.py:27
  128.1 6.1 %collective-permute-start.67 = (bf16[32,4096]{1,0:T(8,128)(2,1)S(1)}, bf16[32,4096]{1,0:T(8,128)(2,1)S(1)}, u32[]{:S(2)}, u32[]{:S(2)}) collective-permute-start(bf16[32,4096]{1,0:T(8,128)(2,1)S(1)} %get-tuple-element.719), channel_id=1, source_target_pairs={{0,1},{1,0},{2,3},{3,2},{4,5},{5,4},{6,7},{7,6},{8,9},{9,8},{10,11... | collective-permute-start | bytes 786440 | tf_op jit(solution)/shard_map/ppermute | solution.py:27
  128.2 6.0 %collective-permute-start.68 = (bf16[32,4096]{1,0:T(8,128)(2,1)S(1)}, bf16[32,4096]{1,0:T(8,128)(2,1)S(1)}, u32[]{:S(2)}, u32[]{:S(2)}) collective-permute-start(bf16[32,4096]{1,0:T(8,128)(2,1)S(1)} %get-tuple-element.720), channel_id=1, source_target_pairs={{0,1},{1,0},{2,3},{3,2},{4,5},{5,4},{6,7},{7,6},{8,9},{9,8},{10,11... | collective-permute-start | bytes 786440 | tf_op jit(solution)/shard_map/ppermute | solution.py:27
  134.4 20.2 %collective-permute-start.74 = (bf16[64,4096]{1,0:T(8,128)(2,1)S(1)}, bf16[64,4096]{1,0:T(8,128)(2,1)S(1)}, u32[]{:S(2)}, u32[]{:S(2)}) collective-permute-start(bf16[64,4096]{1,0:T(8,128)(2,1)S(1)} %get-tuple-element.749.refs_3_), channel_id=1, source_target_pairs={{0,2},{1,3},{2,0},{3,1},{4,6},{5,7},{6,4},{7,5},{8,10},{9,11},{10,... | collective-permute-start | bytes 1572872 | tf_op jit(solution)/shard_map/ppermute | solution.py:27
  138.3 26.3 %collective-permute-start.71 = (bf16[64,4096]{1,0:T(8,128)(2,1)S(1)}, bf16[64,4096]{1,0:T(8,128)(2,1)S(1)}, u32[]{:S(2)}, u32[]{:S(2)}) collective-permute-start(bf16[64,4096]{1,0:T(8,128)(2,1)S(1)} %get-tuple-element.745.refs_3_), channel_id=1, source_target_pairs={{0,2},{1,3},{2,0},{3,1},{4,6},{5,7},{6,4},{7,5},{8,10},{9,11},{10,... | collective-permute-start | bytes 1572872 | tf_op jit(solution)/shard_map/ppermute | solution.py:27
  145.6 10.3 %collective-permute-start.72 = (bf16[32,4096]{1,0:T(8,128)(2,1)S(1)}, bf16[32,4096]{1,0:T(8,128)(2,1)S(1)}, u32[]{:S(2)}, u32[]{:S(2)}) collective-permute-start(bf16[32,4096]{1,0:T(8,128)(2,1)S(1)} %get-tuple-element.746), channel_id=1, source_target_pairs={{0,1},{1,0},{2,3},{3,2},{4,5},{5,4},{6,7},{7,6},{8,9},{9,8},{10,11... | collective-permute-start | bytes 786440 | tf_op jit(solution)/shard_map/ppermute | solution.py:27
  145.7 10.3 %collective-permute-start.73 = (bf16[32,4096]{1,0:T(8,128)(2,1)S(1)}, bf16[32,4096]{1,0:T(8,128)(2,1)S(1)}, u32[]{:S(2)}, u32[]{:S(2)}) collective-permute-start(bf16[32,4096]{1,0:T(8,128)(2,1)S(1)} %get-tuple-element.747), channel_id=1, source_target_pairs={{0,1},{1,0},{2,3},{3,2},{4,5},{5,4},{6,7},{7,6},{8,9},{9,8},{10,11... | collective-permute-start | bytes 786440 | tf_op jit(solution)/shard_map/ppermute | solution.py:27
  155.9 9.9 %collective-permute-start.79 = (bf16[32,2048]{1,0:T(8,128)(2,1)S(1)}, bf16[32,2048]{1,0:T(8,128)(2,1)S(1)}, u32[]{:S(2)}, u32[]{:S(2)}) collective-permute-start(bf16[32,2048]{1,0:T(8,128)(2,1)S(1)} %get-tuple-element.775), channel_id=1, source_target_pairs={{0,1},{1,0},{2,3},{3,2},{4,5},{5,4},{6,7},{7,6},{8,9},{9,8},{10,11... | collective-permute-start | bytes 393224 | tf_op jit(solution)/shard_map/ppermute | solution.py:27
  156.0 10.3 %collective-permute-start.80 = (bf16[32,2048]{1,0:T(8,128)(2,1)S(1)}, bf16[32,2048]{1,0:T(8,128)(2,1)S(1)}, u32[]{:S(2)}, u32[]{:S(2)}) collective-permute-start(bf16[32,2048]{1,0:T(8,128)(2,1)S(1)} %get-tuple-element.776), channel_id=1, source_target_pairs={{0,1},{1,0},{2,3},{3,2},{4,5},{5,4},{6,7},{7,6},{8,9},{9,8},{10,11... | collective-permute-start | bytes 393224 | tf_op jit(solution)/shard_map/ppermute | solution.py:27
  165.1 4.8 %collective-permute-start.69 = (bf16[32,2048]{1,0:T(8,128)(2,1)S(1)}, bf16[32,2048]{1,0:T(8,128)(2,1)S(1)}, u32[]{:S(2)}, u32[]{:S(2)}) collective-permute-start(bf16[32,2048]{1,0:T(8,128)(2,1)S(1)} %get-tuple-element.742), channel_id=1, source_target_pairs={{0,1},{1,0},{2,3},{3,2},{4,5},{5,4},{6,7},{7,6},{8,9},{9,8},{10,11... | collective-permute-start | bytes 393224 | tf_op jit(solution)/shard_map/ppermute | solution.py:27
  165.9 4.1 %collective-permute-start.70 = (bf16[32,2048]{1,0:T(8,128)(2,1)S(1)}, bf16[32,2048]{1,0:T(8,128)(2,1)S(1)}, u32[]{:S(2)}, u32[]{:S(2)}) collective-permute-start(bf16[32,2048]{1,0:T(8,128)(2,1)S(1)} %get-tuple-element.743), channel_id=1, source_target_pairs={{0,1},{1,0},{2,3},{3,2},{4,5},{5,4},{6,7},{7,6},{8,9},{9,8},{10,11... | collective-permute-start | bytes 393224 | tf_op jit(solution)/shard_map/ppermute | solution.py:27
  166.3 3.6 %collective-permute-start.77 = (bf16[32,2048]{1,0:T(8,128)(2,1)S(1)}, bf16[32,2048]{1,0:T(8,128)(2,1)S(1)}, u32[]{:S(2)}, u32[]{:S(2)}) collective-permute-start(bf16[32,2048]{1,0:T(8,128)(2,1)S(1)} %get-tuple-element.772), channel_id=1, source_target_pairs={{0,1},{1,0},{2,3},{3,2},{4,5},{5,4},{6,7},{7,6},{8,9},{9,8},{10,11... | collective-permute-start | bytes 393224 | tf_op jit(solution)/shard_map/ppermute | solution.py:27
  166.4 3.5 %collective-permute-start.78 = (bf16[32,2048]{1,0:T(8,128)(2,1)S(1)}, bf16[32,2048]{1,0:T(8,128)(2,1)S(1)}, u32[]{:S(2)}, u32[]{:S(2)}) collective-permute-start(bf16[32,2048]{1,0:T(8,128)(2,1)S(1)} %get-tuple-element.773), channel_id=1, source_target_pairs={{0,1},{1,0},{2,3},{3,2},{4,5},{5,4},{6,7},{7,6},{8,9},{9,8},{10,11... | collective-permute-start | bytes 393224 | tf_op jit(solution)/shard_map/ppermute | solution.py:27
  (49 other events, 113.1 us)
